TPU v7x, 32 devices: a whole 2x2x4 slice. The times are simulated.
32 devices in a mesh: fsdp: 4 (over y, x), ctx: 4 (over z), tp: 2 (over core).
Axes of the slice: x: 2, y: 2, z: 4, core: 2. Of those that a mesh axis runs over, the one named last changes fastest.
Arguments:
- block_input: bfloat16 [8, 1024, 2560], P('fsdp', 'ctx'), may hold values from -6 to 6
- segments: int32 [8, 1024], P('fsdp', 'ctx'), may hold values from 0 to 4, as said below
- token_mask: int32 [8, 1024], P('fsdp', 'ctx'), may hold values from 0 to 1, as said below
- cotangent: bfloat16 [8, 1024, 2560], P('fsdp', 'ctx'), may hold values from -6 to 6
- norm_gains: float32 [2, 2560], replicated, may hold values from 0.1 to 1.9
- conv_taps: float32 [4, 2560], P(None, 'tp'), may hold values from -3 to 3
- conv_offset: float32 [2560], P('tp'), may hold values from -3 to 3
- gate_offset: float32 [2, 2560], P(None, 'tp'), may hold values from -4 to 4
- decay_logit: float32 [2560], P('tp'), may hold values from 4.5 to 10
- intake: bfloat16 [2560, 2, 2560], P(('fsdp', 'ctx'), None, 'tp'), may hold values from -0.125 to 0.125
- gate_blocks: bfloat16 [256, 2, 2560], P(('fsdp', 'ctx'), None, 'tp'), may hold values from -0.375 to 0.375
- outlet: bfloat16 [2560, 2560], P(('fsdp', 'ctx'), 'tp'), may hold values from -0.5 to 0.5
- expand: bfloat16 [2560, 2, 7680], P(('fsdp', 'ctx'), None, 'tp'), may hold values from -0.125 to 0.125
- contract: bfloat16 [2560, 7680], P(('fsdp', 'ctx'), 'tp'), may hold values from -0.125 to 0.125
Outputs:
- block_output: bfloat16 [8, 1024, 2560], P('fsdp', 'ctx')
- input_grad: float32 [8, 1024, 2560], P('fsdp', 'ctx')
- gains_grad: float32 [2, 2560], replicated
- taps_grad: float32 [4, 2560], P(None, 'tp')
- offset_grad: float32 [2560], P('tp')
- gating_grad: float32 [2, 2560], P(None, 'tp')
- decay_grad: float32 [2560], P('tp')
- intake_grad: float32 [2560, 2, 2560], P(('fsdp', 'ctx'), None, 'tp')
- blocks_grad: float32 [256, 2, 2560], P(('fsdp', 'ctx'), None, 'tp')
- outlet_grad: float32 [2560, 2560], P(('fsdp', 'ctx'), 'tp')
- expand_grad: float32 [2560, 2, 7680], P(('fsdp', 'ctx'), None, 'tp')
- contract_grad: float32 [2560, 7680], P(('fsdp', 'ctx'), 'tp')
Inputs may be any that keep to these rules, and one draw needn't show every extreme that they name: `segments`: segment numbers never fall along a row. Every row holds exactly five documents, numbered 0 to 4; document 0 ends before position 64, document 1 begins before position 128, document 3 begins at or after position 896 and before position 960, and document 4 begins at or after position 960. `token_mask`: in every row the ones come first; the padding is a final run of 1 to 64 positions.
All inputs are finite; a program needn't handle non-finite values.
Results may differ from a plain program's by a relative error of at most 0.015.
Values may be sent and summed in bfloat16 or wider, within the bound.
A program may use at most 280 MiB of HBM per device.

v0:
```python
from functools import partial

import jax
import jax.numpy as jnp
from jax import lax
from jax.sharding import PartitionSpec as P

HEAD_W = 256
ROWS_MB = 1
MICRO = 2


EPSILON = 1e-06
DECAY_SCALE = 8.0


def from_behind(x, axis, by):
    length = lax.axis_size(axis)
    pairs = [(i, i + by) for i in range(length) if 0 <= i + by < length]
    return lax.ppermute(x, axis, pairs)


def prefix(x, axis, combine, identity, reverse):
    length, place = (lax.axis_size(axis), lax.axis_index(axis))
    everything = jax.tree.map(lambda part: lax.all_gather(part, axis), x)
    start = jax.tree.map(
        lambda part, zero: jnp.broadcast_to(jnp.asarray(zero, part.dtype), part.shape), x, identity
    )

    def lap(k, before):
        at = length - 1 - k if reverse else k
        reached = at > place if reverse else at < place
        new = combine(before, jax.tree.map(lambda part: part[at], everything))
        return jax.tree.map(lambda a, b: jnp.where(reached, a, b), new, before)

    return lax.fori_loop(0, length, lap, start)


def rms_scale(values, weighting):
    inverse = lax.rsqrt(jnp.mean(values * values, axis=-1, keepdims=True) + EPSILON)
    return values * inverse * weighting


def gelu_tanh(values):
    return jax.nn.gelu(values, approximate=True)


def gated_hidden(first_half, second_half):
    return gelu_tanh(first_half) * second_half


def conv_mix(before, current, conv_taps, conv_offset, seg_ext):
    joined = jnp.concatenate([before, current], axis=1)
    sequence_extent = current.shape[1]
    own_seg = seg_ext[:, 3:]
    summed = jnp.zeros(current.shape, jnp.float32) + conv_offset
    for tap_index in range(4):
        window = joined[:, 3 - tap_index : 3 - tap_index + sequence_extent]
        matching = (seg_ext[:, 3 - tap_index : 3 - tap_index + sequence_extent] == own_seg).astype(
            jnp.float32
        )
        summed = summed + conv_taps[tap_index] * window * matching[:, :, None]
    return summed


def lru_terms(pre_rate, pre_inlet, conv_out, decay_logit, gate_offset, starts):
    recur_gate = jax.nn.sigmoid(pre_rate + gate_offset[0])
    input_gate = jax.nn.sigmoid(pre_inlet + gate_offset[1])
    log_keep = -DECAY_SCALE * recur_gate * jax.nn.softplus(-decay_logit)
    carry_coef = jnp.exp(log_keep) * (1.0 - starts)
    norm_scale = jnp.where(starts > 0.5, 1.0, jnp.sqrt(-jnp.expm1(2.0 * log_keep)))
    return (carry_coef, input_gate * conv_out * norm_scale)


def merge_affine_maps(earlier, later):
    return (earlier[0] * later[0], later[0] * earlier[1] + later[1])


def affine_state_sweep(forget_multipliers, sweep_increment_terms):
    return lax.associative_scan(
        merge_affine_maps, (forget_multipliers, sweep_increment_terms), axis=1
    )


def across_units(partial_sum):
    return lax.psum(partial_sum, "tp")


def fetch_weights(intake, gate_blocks, outlet, expand, contract):
    return (
        lax.all_gather(intake, ("fsdp", "ctx"), axis=0, tiled=True),
        lax.all_gather(gate_blocks, ("fsdp", "ctx"), axis=0, tiled=True),
        lax.all_gather(outlet, ("fsdp", "ctx"), axis=0, tiled=True),
        lax.all_gather(expand, ("fsdp", "ctx"), axis=0, tiled=True),
        lax.all_gather(contract, ("fsdp", "ctx"), axis=0, tiled=True),
    )


def weight_grads(pieces):
    joined = [jnp.concatenate([piece[member] for piece in pieces], axis=0) for member in range(10)]
    (
        normed_low,
        intake_low,
        heads_in,
        gate_heads,
        branch_grad,
        recurrent_block,
        second_normed_rows,
        expand_low,
        feed_grad,
        hidden_low,
    ) = joined
    expand_term = jnp.einsum(
        "td,tkf->dkf", second_normed_rows, expand_low, preferred_element_type=jnp.float32
    )
    contract_term = jnp.einsum(
        "td,tf->df", feed_grad, hidden_low, preferred_element_type=jnp.float32
    )
    expand_part, contract_part = (
        lax.psum_scatter(expand_term, ("fsdp", "ctx"), scatter_dimension=0, tiled=True),
        lax.psum_scatter(contract_term, ("fsdp", "ctx"), scatter_dimension=0, tiled=True),
    )
    intake_term = jnp.einsum(
        "td,tkr->dkr", normed_low, intake_low, preferred_element_type=jnp.float32
    )
    blocks_term = jnp.einsum(
        "thi,tkhj->ikhj", heads_in, gate_heads, preferred_element_type=jnp.float32
    )
    blocks_term = blocks_term.reshape(blocks_term.shape[0], 2, -1)
    outlet_term = jnp.einsum(
        "td,tr->dr", branch_grad, recurrent_block, preferred_element_type=jnp.float32
    )
    intake_part, blocks_part, outlet_part = (
        lax.psum_scatter(intake_term, ("fsdp", "ctx"), scatter_dimension=0, tiled=True),
        lax.psum_scatter(blocks_term, ("fsdp", "ctx"), scatter_dimension=0, tiled=True),
        lax.psum_scatter(outlet_term, ("fsdp", "ctx"), scatter_dimension=0, tiled=True),
    )
    return (intake_part, blocks_part, outlet_part, expand_part, contract_part)


def shards(
    block_input,
    segments,
    token_mask,
    cotangent,
    norm_gains,
    conv_taps,
    conv_offset,
    gate_offset,
    decay_logit,
    intake,
    gate_blocks,
    outlet,
    expand,
    contract,
):
    local_len = block_input.shape[1]
    embedding_dimension = block_input.shape[2]
    unit_count = intake.shape[2]
    heads_here = unit_count // HEAD_W
    token_count = ROWS_MB * local_len
    seg_next = segments + 1
    seg_before = from_behind(seg_next[:, -3:], "ctx", 1)
    seg_ext = jnp.concatenate([seg_before, seg_next], axis=1)
    document_beginnings = (seg_ext[:, 3:] != seg_ext[:, 2:-1]).astype(jnp.float32)[:, :, None]
    outputs = []
    input_grads = []
    pieces = []
    small_total = None
    weight_total = None
    for micro_index in range(MICRO):
        weights = fetch_weights(intake, gate_blocks, outlet, expand, contract)
        w_intake, w_gates, w_outlet, w_expand, w_contract = weights
        row_start = micro_index * ROWS_MB
        flat_in = (
            block_input[row_start : row_start + ROWS_MB]
            .astype(jnp.float32)
            .reshape(token_count, embedding_dimension)
        )
        seg_rows = seg_ext[row_start : row_start + ROWS_MB]
        starts = document_beginnings[row_start : row_start + ROWS_MB]
        normed_rows, norm_pull = jax.vjp(rms_scale, flat_in, norm_gains[0])
        normed_low = normed_rows.astype(jnp.bfloat16)
        projected_rows = jnp.einsum(
            "td,dkr->tkr", normed_low, w_intake, preferred_element_type=jnp.float32
        )
        gelu_in = projected_rows[:, 0]
        x_branch = projected_rows[:, 1].astype(jnp.bfloat16).reshape(ROWS_MB, local_len, unit_count)
        x_before = from_behind(x_branch[:, -3:], "ctx", 1)
        conv_out, conv_pull = jax.vjp(
            partial(conv_mix, seg_ext=seg_rows),
            x_before.astype(jnp.float32),
            x_branch.astype(jnp.float32),
            conv_taps,
            conv_offset,
        )
        conv_low = conv_out.astype(jnp.bfloat16)
        heads_in = conv_low.reshape(token_count, heads_here, HEAD_W)
        blocks = w_gates.reshape(HEAD_W, 2, heads_here, HEAD_W)
        gate_pre = jnp.einsum(
            "thi,ikhj->tkhj", heads_in, blocks, preferred_element_type=jnp.float32
        )
        gate_pre = gate_pre.reshape(ROWS_MB, local_len, 2, unit_count)
        (carry_coef, normed_x), lru_pull = jax.vjp(
            partial(lru_terms, starts=starts),
            gate_pre[:, :, 0],
            gate_pre[:, :, 1],
            conv_low.astype(jnp.float32),
            decay_logit,
            gate_offset,
        )
        partial_ends, local_states = affine_state_sweep(carry_coef, normed_x)
        state_ones = jnp.ones((ROWS_MB, unit_count), jnp.float32)
        state_zeros = jnp.zeros((ROWS_MB, unit_count), jnp.float32)
        entering = prefix(
            (partial_ends[:, -1], local_states[:, -1]),
            "ctx",
            merge_affine_maps,
            (state_ones, state_zeros),
            False,
        )
        state_in = entering[1]
        states = local_states + partial_ends * state_in[:, None]
        gelu_out, gelu_pull = jax.vjp(gelu_tanh, gelu_in)
        gelu_rows = gelu_out.reshape(ROWS_MB, local_len, unit_count)
        recurrent_block = (states * gelu_rows).astype(jnp.bfloat16).reshape(token_count, unit_count)
        branch_path = across_units(
            jnp.einsum("tr,dr->td", recurrent_block, w_outlet, preferred_element_type=jnp.float32)
        )
        residual = flat_in + branch_path
        second_normed_rows, norm_two_pull = jax.vjp(rms_scale, residual, norm_gains[1])
        normed_two_low = second_normed_rows.astype(jnp.bfloat16)
        expanded_rows = jnp.einsum(
            "td,dkf->tkf", normed_two_low, w_expand, preferred_element_type=jnp.float32
        )
        hidden_rows, hidden_pull = jax.vjp(gated_hidden, expanded_rows[:, 0], expanded_rows[:, 1])
        hidden_low = hidden_rows.astype(jnp.bfloat16)
        feed_output = across_units(
            jnp.einsum("tf,df->td", hidden_low, w_contract, preferred_element_type=jnp.float32)
        )
        outputs.append(
            (residual + feed_output)
            .astype(jnp.bfloat16)
            .reshape(ROWS_MB, local_len, embedding_dimension)
        )
        mask_rows = token_mask[row_start : row_start + ROWS_MB].astype(jnp.float32)[:, :, None]
        out_grad = (
            cotangent[row_start : row_start + ROWS_MB].astype(jnp.float32) * mask_rows
        ).reshape(token_count, embedding_dimension)
        feed_grad = out_grad.astype(jnp.bfloat16)
        hidden_grad = jnp.einsum(
            "td,df->tf", feed_grad, w_contract, preferred_element_type=jnp.float32
        )
        first_grad, second_grad = hidden_pull(hidden_grad)
        expand_low = jnp.stack([first_grad, second_grad], axis=1).astype(jnp.bfloat16)
        normed_two_grad = across_units(
            jnp.einsum("tkf,dkf->td", expand_low, w_expand, preferred_element_type=jnp.float32)
        )
        residual_part, gain_two = norm_two_pull(normed_two_grad)
        residual_grad = out_grad + residual_part
        branch_grad = residual_grad.astype(jnp.bfloat16)
        recurrent_grad = jnp.einsum(
            "td,dr->tr", branch_grad, w_outlet, preferred_element_type=jnp.float32
        )
        recurrent_grad = recurrent_grad.reshape(ROWS_MB, local_len, unit_count)
        state_grad = recurrent_grad * gelu_rows
        (gelu_grad,) = gelu_pull((recurrent_grad * states).reshape(token_count, unit_count))
        shifted = jnp.concatenate([carry_coef[:, 1:], jnp.ones_like(carry_coef[:, :1])], axis=1)
        tail_prod, tail_sums = affine_state_sweep(jnp.flip(shifted, 1), jnp.flip(state_grad, 1))
        tail_prod = jnp.flip(tail_prod, 1)
        tail_sums = jnp.flip(tail_sums, 1)
        first_coef = carry_coef[:, 0]
        leaving = prefix(
            (first_coef * tail_prod[:, 0], first_coef * tail_sums[:, 0]),
            "ctx",
            merge_affine_maps,
            (state_ones, state_zeros),
            True,
        )
        adjoint = tail_sums + tail_prod * leaving[1][:, None]
        prev_states = jnp.concatenate([state_in[:, None], states[:, :-1]], axis=1)
        rate_grad, inlet_grad, conv_part, decay_part, gating_part = lru_pull(
            (adjoint * prev_states, adjoint)
        )
        gating_reduced_format = jnp.stack([rate_grad, inlet_grad], axis=2).astype(jnp.bfloat16)
        gate_heads = gating_reduced_format.reshape(token_count, 2, heads_here, HEAD_W)
        conv_grad = conv_part + jnp.einsum(
            "tkhj,ikhj->thi", gate_heads, blocks, preferred_element_type=jnp.float32
        ).reshape(ROWS_MB, local_len, unit_count)
        before_grad, branch_x_grad, taps_part, offset_part = conv_pull(conv_grad)
        from_next = from_behind(before_grad, "ctx", -1)
        branch_x_grad = branch_x_grad + jnp.pad(from_next, ((0, 0), (local_len - 3, 0), (0, 0)))
        intake_low = jnp.stack(
            [gelu_grad, branch_x_grad.reshape(token_count, unit_count)], axis=1
        ).astype(jnp.bfloat16)
        normed_grad = across_units(
            jnp.einsum("tkr,dkr->td", intake_low, w_intake, preferred_element_type=jnp.float32)
        )
        input_part, gain_one = norm_pull(normed_grad)
        input_grads.append(
            (residual_grad + input_part).reshape(ROWS_MB, local_len, embedding_dimension)
        )
        small_terms = (
            jnp.stack([gain_one, gain_two]),
            taps_part,
            offset_part,
            gating_part,
            decay_part,
        )
        small_total = (
            small_terms if small_total is None else jax.tree.map(jnp.add, small_total, small_terms)
        )
        piece = (
            normed_low,
            intake_low,
            heads_in,
            gate_heads,
            branch_grad,
            recurrent_block,
            normed_two_low,
            expand_low,
            feed_grad,
            hidden_low,
        )
        pieces.append(piece)
    weight_total = weight_grads(pieces)
    small_sum = lax.psum(small_total, ("fsdp", "ctx"))
    return (
        jnp.concatenate(outputs, axis=0),
        jnp.concatenate(input_grads, axis=0),
        small_sum[0],
        small_sum[1],
        small_sum[2],
        small_sum[3],
        small_sum[4],
        weight_total[0],
        weight_total[1],
        weight_total[2],
        weight_total[3],
        weight_total[4],
    )


def solution(mesh):
    placed = (
        P("fsdp", "ctx", None),
        P("fsdp", "ctx"),
        P("fsdp", "ctx"),
        P("fsdp", "ctx", None),
        P(),
        P(None, "tp"),
        P("tp"),
        P(None, "tp"),
        P("tp"),
        P(("fsdp", "ctx"), None, "tp"),
        P(("fsdp", "ctx"), None, "tp"),
        P(("fsdp", "ctx"), "tp"),
        P(("fsdp", "ctx"), None, "tp"),
        P(("fsdp", "ctx"), "tp"),
    )
    return jax.shard_map(
        shards,
        mesh=mesh,
        in_specs=placed,
        out_specs=(
            P("fsdp", "ctx", None),
            P("fsdp", "ctx", None),
            P(),
            P(None, "tp"),
            P("tp"),
            P(None, "tp"),
            P("tp"),
            P(("fsdp", "ctx"), None, "tp"),
            P(("fsdp", "ctx"), None, "tp"),
            P(("fsdp", "ctx"), "tp"),
            P(("fsdp", "ctx"), None, "tp"),
            P(("fsdp", "ctx"), "tp"),
        ),
        check_vma=False,
    )
```

profile of v0, /device:TPU:0, one launch (start us, length us, event | category | flops | bytes accessed | tf_op | source)
XLA Modules:
  0.0 4543.9 jit_solution(2774497364414201711)
XLA Ops:
  20.1 50.3 %all-gather.8.cloned.1.call-done = bf16[256,2,1280]{2,1,0:T(2,128)(2,1)} async-done(((bf16[16,2,1280]{2,1,0:T(2,128)(2,1)}), bf16[256,2,1280]{2,1,0:T(2,128)(2,1)}) %all-gather.8.cloned.1.call-update) | async-done | bytes 1310736 | tf_op jit(solution)/shard_map/all_gather | solution.py:92
  74.6 154.9 %all-gather.6.cloned.1.call-done = bf16[2560,2,1280]{2,0,1:T(8,128)(2,1)} async-done(((bf16[160,2,1280]{2,0,1:T(8,128)(2,1)}), bf16[2560,2,1280]{2,0,1:T(8,128)(2,1)}) %all-gather.6.cloned.1.call-update) | async-done | bytes 13107216 | tf_op jit(solution)/shard_map/all_gather | solution.py:91
  613.9 13.1 all_gather.55
  627.8 13.1 all_gather.56
  642.0 13.1 all_gather.50
  694.8 19.8 all-reduce.170.cloned.1.call-done
  720.8 404.1 %all-gather.12.cloned.1.call-done = bf16[2560,2,3840]{2,0,1:T(8,128)(2,1)} async-done(((bf16[160,2,3840]{2,0,1:T(8,128)(2,1)}), bf16[2560,2,3840]{2,0,1:T(8,128)(2,1)}) %all-gather.12.cloned.1.call-update) | async-done | bytes 39321616 | tf_op jit(solution)/shard_map/all_gather | solution.py:94
  1124.9 21.9 fusion.177
  1146.9 19.7 fusion.189
  1166.5 178.5 %all-gather.14.cloned.1.call-done = bf16[2560,3840]{1,0:T(8,128)(2,1)} async-done(((bf16[160,3840]{1,0:T(8,128)(2,1)}), bf16[2560,3840]{1,0:T(8,128)(2,1)}) %all-gather.14.cloned.1.call-update) | async-done | bytes 19660816 | tf_op jit(solution)/shard_map/all_gather | solution.py:95
  1345.0 14.3 fusion.79
  1359.4 14.3 fusion.80
  1373.6 18.9 convolution_bitcast_fusion.2
  1392.5 19.4 convolution_bitcast_fusion.3
  1885.4 13.9 fusion.50
  1901.0 33.0 fusion
  1945.4 18.1 fusion.28
  1965.8 35.7 all-reduce.164.cloned.1.call-done
  2003.1 44.3 all-reduce.166.cloned.1.call-done
  2052.0 85.0 %all-reduce.155 = (f32[2,2560]{1,0:T(2,128)}, f32[4,1280]{1,0:T(4,128)}, f32[1280]{0:T(1024)}, f32[2,1280]{1,0:T(2,128)}, f32[1280]{0:T(1024)}) all-reduce(f32[2,2560]{1,0:T(2,128)S(1)} %maximum_add_fusion, f32[4,1280]{1,0:T(4,128)S(1)} %add_add_fusion.4, ...), channel_id=1, replica_groups=mesh['fsdp'=4,'ctx'=4,'tp'=2] {'fsdp','ctx'}, use_global_device_ids=true, to_apply=%region_28.30 | all-reduce | flops 15360 | bytes 122880 | tf_op jit(solution)/shard_map/psum | solution.py:327
  2149.5 444.8 %reduce-scatter.5.cloned.1.call-done = f32[160,2,1280]{2,0,1:T(8,128)} async-done(((f32[2560,2,1280]{2,0,1:T(8,128)}), f32[160,2,1280]{2,0,1:T(8,128)}) %reduce-scatter.5.cloned.1.call-update) | async-done | bytes 1638416 | tf_op jit(solution)/shard_map/reduce_scatter | solution.py:134
  2598.2 1087.7 %reduce-scatter.9.cloned.1.call-done = f32[160,2,3840]{2,0,1:T(8,128)} async-done(((f32[2560,2,3840]{2,0,1:T(8,128)}), f32[160,2,3840]{2,0,1:T(8,128)}) %reduce-scatter.9.cloned.1.call-update) | async-done | bytes 4915216 | tf_op jit(solution)/shard_map/reduce_scatter | solution.py:120
  3694.3 270.3 %reduce-scatter.7.cloned.1.call-done = f32[160,1280]{1,0:T(8,128)} async-done(((f32[2560,1280]{1,0:T(8,128)}), f32[160,1280]{1,0:T(8,128)}) %reduce-scatter.7.cloned.1.call-update) | async-done | bytes 819216 | tf_op jit(solution)/shard_map/reduce_scatter | solution.py:136
  3964.6 572.6 %reduce-scatter.11.cloned.1.call-done = f32[160,3840]{1,0:T(8,128)} async-done(((f32[2560,3840]{1,0:T(8,128)}), f32[160,3840]{1,0:T(8,128)}) %reduce-scatter.11.cloned.1.call-update) | async-done | bytes 2457616 | tf_op jit(solution)/shard_map/reduce_scatter | solution.py:121
  (1278 shorter events, 964.2 us)
Async XLA Ops:
  7.2 63.2 %all-gather.8.cloned.1.call-start = ((), (), s32[]{:S(2)}) async-start(), calls=%async_computation.5 | async-start | bytes 1392640 | tf_op jit(solution)/shard_map/all_gather | solution.py:92
  7.9 221.6 %all-gather.6.cloned.1.call-start = ((), (), s32[]{:S(2)}) async-start(), calls=%async_computation.4 | async-start | bytes 13926400 | tf_op jit(solution)/shard_map/all_gather | solution.py:91
  10.3 666.7 %all-gather.10.cloned.1.call-start = ((), (), s32[]{:S(2)}) async-start(), calls=%async_computation.6 | async-start | bytes 6963200 | tf_op jit(solution)/shard_map/all_gather | solution.py:93
  10.4 9.4 collective-permute-start.1
  15.4 699.3 %all-reduce.170.cloned.1.call-start = ((), (), s32[]{:S(2)}) async-start(), calls=%async_computation.16 | async-start | bytes 10485760 | tf_op jit(solution)/shard_map/psum | solution.py:86
  15.5 703.0 %copy-start.130 = (f32[2560]{0:T(1024)}, f32[2560]{0:T(1024)S(1)}, u32[]{:S(2)}) copy-start(f32[2560]{0:T(1024)S(1)} %get-tuple-element.606) | copy-start | bytes 30724
  17.5 258.8 %copy-start.153 = (f32[1280]{0:T(1024)}, f32[1280]{0:T(1024)S(1)}, u32[]{:S(2)}) copy-start(f32[1280]{0:T(1024)S(1)} %get-tuple-element.880) | copy-start | bytes 15364
  17.6 258.8 %copy-start.114 = (f32[1280]{0:T(1024)}, f32[1280]{0:T(1024)S(1)}, u32[]{:S(2)}) copy-start(f32[1280]{0:T(1024)S(1)} %get-tuple-element.614) | copy-start | bytes 15364
  17.6 258.8 %copy-start.128 = (f32[1280]{0:T(1024)}, f32[1280]{0:T(1024)S(1)}, u32[]{:S(2)}) copy-start(f32[1280]{0:T(1024)S(1)} %get-tuple-element.615) | copy-start | bytes 15364
  238.2 12.0 collective-permute-start
  246.2 15.7 collective-permute-start.2
  686.8 438.1 %all-gather.12.cloned.1.call-start = ((), (), s32[]{:S(2)}) async-start(), calls=%async_computation.7 | async-start | bytes 41779200 | tf_op jit(solution)/shard_map/all_gather | solution.py:94
  690.3 654.8 %all-gather.14.cloned.1.call-start = ((), (), s32[]{:S(2)}) async-start(), calls=%async_computation.8 | async-start | bytes 20889600 | tf_op jit(solution)/shard_map/all_gather | solution.py:95
  690.8 777.1 %all-reduce.168.cloned.1.call-start = ((), (), s32[]{:S(2)}) async-start(), calls=%async_computation.15 | async-start | bytes 10485760 | tf_op jit(solution)/shard_map/psum | solution.py:86
  720.8 426.0 %copy-start.58 = (bf16[256,2560]{1,0:T(8,128)(2,1)}, bf16[256,2560]{1,0:T(8,128)(2,1)S(1)}, u32[]{:S(2)}) copy-start(bf16[256,2560]{1,0:T(8,128)(2,1)S(1)} %get-tuple-element.853) | copy-start | bytes 3932164
  720.8 426.0 %copy-start.56 = (bf16[256,2560]{1,0:T(8,128)(2,1)}, bf16[256,2560]{1,0:T(8,128)(2,1)S(1)}, u32[]{:S(2)}) copy-start(bf16[256,2560]{1,0:T(8,128)(2,1)S(1)} %get-tuple-element.852) | copy-start | bytes 3932164
  1411.9 589.6 %all-reduce.164.cloned.1.call-start = ((), (), s32[]{:S(2)}) async-start(), calls=%async_computation.13 | async-start | bytes 5242880
  1856.9 7.4 collective-permute-start.4
  1858.3 7.4 collective-permute-start.3
  1864.2 183.2 %all-reduce.166.cloned.1.call-start = ((), (), s32[]{:S(2)}) async-start(), calls=%async_computation.14 | async-start | bytes 20971520 | tf_op jit(solution)/shard_map/psum | solution.py:86
  1883.6 710.7 %reduce-scatter.5.cloned.1.call-start = ((), (), s32[]{:S(2)}) async-start(), calls=%async_computation.9 | async-start | bytes 27852800 | tf_op jit(solution)/shard_map/reduce_scatter | solution.py:134
  1899.3 1786.6 %reduce-scatter.9.cloned.1.call-start = ((), (), s32[]{:S(2)}) async-start(), calls=%async_computation.11 | async-start | bytes 83558400 | tf_op jit(solution)/shard_map/reduce_scatter | solution.py:120
  1934.0 2030.6 %reduce-scatter.7.cloned.1.call-start = ((), (), s32[]{:S(2)}) async-start(), calls=%async_computation.10 | async-start | bytes 13926400 | tf_op jit(solution)/shard_map/reduce_scatter | solution.py:136
  1943.7 2593.5 %reduce-scatter.11.cloned.1.call-start = ((), (), s32[]{:S(2)}) async-start(), calls=%async_computation.12 | async-start | bytes 41779200 | tf_op jit(solution)/shard_map/reduce_scatter | solution.py:121
  (275 other events, 5778.2 us)
Sparse Core Ops, SparseCore 0:
  10.7 59.5 all-gather.7
  73.7 155.7 all-gather.5
  232.3 94.7 all-gather.9
  686.9 27.6 all-reduce.169
  718.3 406.5 all-gather.11
  1127.9 217.0 all-gather.13
  1412.1 28.3 all-reduce.167
  1864.4 137.1 all-reduce.163
  2004.9 42.4 all-reduce.165
  2049.7 544.5 reduce-scatter.4
  2601.5 1084.3 reduce-scatter.8
  3688.6 275.9 reduce-scatter.6
  3971.3 565.8 reduce-scatter.10
where the time goes:
time: 4560 us; the launch traced here: 4540 us
  waiting for transfers between devices  3260 us (71%)
  local copies, waits for them, and re-layouts  574 us (13%)
  matrix products  262 us (6%)
  other arithmetic  220 us (5%)
  blocking collectives  190 us (4%)
    reduce_scatter x1, waiting for transfers between devices, weight_grads(): lax.psum_scatter(expand_term, ('fsdp', 'ctx'), scatter_dimension=0, tiled...  1090 us
    reduce_scatter x1, waiting for transfers between devices, weight_grads(): lax.psum_scatter(contract_term, ('fsdp', 'ctx'), scatter_dimension=0, til...  573 us
    reduce_scatter x1, waiting for transfers between devices, weight_grads(): lax.psum_scatter(intake_term, ('fsdp', 'ctx'), scatter_dimension=0, tiled...  445 us
    all_gather x1, waiting for transfers between devices, fetch_weights(): lax.all_gather(expand, ('fsdp', 'ctx'), axis=0, tiled=True)  404 us
    slice x218, local copies, waits for them, and re-layouts, affine_state_sweep(): lax.associative_scan(merge_affine_maps, (forget_multipliers, sweep_increm...  338 us
    reduce_scatter x1, waiting for transfers between devices, weight_grads(): lax.psum_scatter(outlet_term, ('fsdp', 'ctx'), scatter_dimension=0, tiled...  270 us
    all_gather x1, waiting for transfers between devices, fetch_weights(): lax.all_gather(contract, ('fsdp', 'ctx'), axis=0, tiled=True)  179 us
    all_gather x1, waiting for transfers between devices, fetch_weights(): lax.all_gather(intake, ('fsdp', 'ctx'), axis=0, tiled=True)  155 us
  transfers between devices with their start and end apart: 18, of which 11 were waited for; matrix products, arithmetic and copies ran while one was open for 14% of the time, Pallas kernels for 0%

commit v1 on v0

v1 whole, which is shorter than its diff:
```python
import jax
import jax.numpy as jnp
from jax import lax
from jax.experimental import pallas as pl
from jax.experimental.pallas import tpu as pltpu
from jax.sharding import PartitionSpec as P

HEAD_W = 256
LANES = 128
CHUNKS = 8

EPSILON = 1e-06
DECAY_SCALE = 8.0
GELU_C = 0.7978845608028654
GELU_A = 0.044715

F32 = jnp.float32
BF16 = jnp.bfloat16

TAP0, OFFSET, RATE_OFF, INLET_OFF, SOFTPLUS, NEG_SIG, PARAM_ROWS = 0, 4, 5, 6, 7, 8, 16


def shifted(x, axis, by):
    length = lax.axis_size(axis)
    pairs = [(i, i + by) for i in range(length) if 0 <= i + by < length]
    return lax.ppermute(x, axis, pairs)


def swap(x, axis):
    length = lax.axis_size(axis)
    return lax.ppermute(x, axis, [(i, (i + 1) % length) for i in range(length)])


def gelu_pair(v):
    t = jnp.tanh(GELU_C * (v + GELU_A * v * v * v))
    value = 0.5 * v * (1.0 + t)
    slope = 0.5 * (1.0 + t) + 0.5 * v * (1.0 - t * t) * GELU_C * (1.0 + 3.0 * GELU_A * v * v)
    return value, slope


def one_minus_exp(x):
    s = 1.0 + x / 7.0
    for n in (6.0, 5.0, 4.0, 3.0, 2.0):
        s = 1.0 + x / n * s
    return jnp.where(x > -0.5, -x * s, 1.0 - jnp.exp(x))


def sigmoid(v):
    return 1.0 / (1.0 + jnp.exp(-v))


def dot(a, b, dims):
    return lax.dot_general(a, b, (dims, ((), ())), preferred_element_type=F32)


def lane_scan(load_a, load_b, store, length, reverse):
    steps = length // CHUNKS
    prod = jnp.ones((CHUNKS, LANES), F32)
    total = jnp.zeros((CHUNKS, LANES), F32)
    for n in range(steps):
        s = steps - 1 - n if reverse else n
        coef = load_a(s)
        total = coef * total + load_b(s)
        prod = coef * prod
        store(s, prod, total)
    return prod, total


def chunk_carries(prod, total, reverse):
    order = range(CHUNKS - 1, -1, -1) if reverse else range(CHUNKS)
    run_p = jnp.ones((1, LANES), F32)
    run_s = jnp.zeros((1, LANES), F32)
    carries = [None] * CHUNKS
    for c in order:
        carries[c] = (run_p, run_s)
        run_s = prod[c : c + 1] * run_s + total[c : c + 1]
        run_p = prod[c : c + 1] * run_p
    return carries


def sweep(a_scr, b_scr, p_scr, s_scr, prod_ref, sum_ref, rows, length, reverse, shift):
    steps = length // CHUNKS
    for b in range(rows):
        for j in range(HEAD_W // LANES):
            av, bv, pv, sv = (a_scr.at[b, j], b_scr.at[b, j], p_scr.at[b, j], s_scr.at[b, j])

            def store(s, prod, total):
                pv[pl.ds(s, CHUNKS, stride=steps), :] = prod
                sv[pl.ds(s, CHUNKS, stride=steps), :] = total

            prod, total = lane_scan(
                lambda s: av[pl.ds(s + shift, CHUNKS, stride=steps), :],
                lambda s: bv[pl.ds(s, CHUNKS, stride=steps), :],
                store,
                length,
                reverse,
            )
            carries = chunk_carries(prod, total, reverse)
            lanes = slice(j * LANES, (j + 1) * LANES)
            for c in range(CHUNKS):
                here = slice(c * steps, (c + 1) * steps)
                p = pv[here, :]
                prod_ref[b, here, lanes] = p * carries[c][0]
                sum_ref[b, here, lanes] = sv[here, :] + p * carries[c][1]


def to_lanes(ref, b, at, value):
    for j in range(HEAD_W // LANES):
        ref[b, j, pl.ds(at, value.shape[0]), :] = value[:, j * LANES : (j + 1) * LANES]


def forward_kernel(
    x_ref, halo_ref, mask_ref, par_ref, w_ref,
    conv_ref, r_ref, i_ref, a_ref, prod_ref, sum_ref,
    ext, a_scr, b_scr, p_scr, s_scr,
):
    rows, length, _ = x_ref.shape
    par = par_ref[...]
    w0, w1 = w_ref[0], w_ref[1]
    for b in range(rows):
        ext[b, pl.ds(0, 8), :] = halo_ref[b]
        ext[b, pl.ds(8, length), :] = x_ref[b].astype(F32)
        conv = ext[b, pl.ds(8, length), :] * par[TAP0 : TAP0 + 1] + par[OFFSET : OFFSET + 1]
        for k in range(1, 4):
            match = mask_ref[b, :, k : k + 1]
            conv = conv + par[TAP0 + k : TAP0 + k + 1] * ext[b, pl.ds(8 - k, length), :] * match
        conv_low = conv.astype(BF16)
        conv_ref[b] = conv_low
        conv = conv_low.astype(F32)
        r = sigmoid(dot(conv_low, w0, ((1,), (0,))) + par[RATE_OFF : RATE_OFF + 1])
        i = sigmoid(dot(conv_low, w1, ((1,), (0,))) + par[INLET_OFF : INLET_OFF + 1])
        r_ref[b] = r
        i_ref[b] = i
        log_keep = -DECAY_SCALE * r * par[SOFTPLUS : SOFTPLUS + 1]
        going = mask_ref[b, :, 0:1]
        a = jnp.exp(log_keep) * going
        a_ref[b] = a
        scale = jnp.where(going > 0.5, jnp.sqrt(one_minus_exp(2.0 * log_keep)), 1.0)
        to_lanes(a_scr, b, 0, a)
        to_lanes(b_scr, b, 0, i * conv * scale)
    sweep(a_scr, b_scr, p_scr, s_scr, prod_ref, sum_ref, rows, length, False, 0)


def head_spec(rows, length):
    return pl.BlockSpec((rows, length, HEAD_W), lambda h: (0, 0, h))


def recurrent_forward(x_branch, halo, masks, params, blocks):
    rows, length, units = x_branch.shape
    full = head_spec(rows, length)
    scan = pltpu.VMEM((rows, HEAD_W // LANES, length, LANES), F32)
    big = jax.ShapeDtypeStruct((rows, length, units), F32)
    return pl.pallas_call(
        forward_kernel,
        grid=(units // HEAD_W,),
        in_specs=[
            full,
            head_spec(rows, 8),
            pl.BlockSpec((rows, length, 8), lambda h: (0, 0, 0)),
            pl.BlockSpec((PARAM_ROWS, HEAD_W), lambda h: (0, h)),
            pl.BlockSpec((2, HEAD_W, HEAD_W), lambda h: (0, 0, h)),
        ],
        out_specs=[full] * 6,
        out_shape=[jax.ShapeDtypeStruct((rows, length, units), BF16)] + [big] * 5,
        scratch_shapes=[pltpu.VMEM((rows, length + 8, HEAD_W), F32), scan, scan, scan, scan],
        compiler_params=pltpu.CompilerParams(vmem_limit_bytes=48 * 1024 * 1024),
        cost_estimate=pl.CostEstimate(
            flops=4 * rows * length * units * HEAD_W,
            bytes_accessed=24 * rows * length * units,
            transcendentals=8 * rows * length * units,
        ),
        name="recurrent_forward",
    )(x_branch, halo, masks, params, blocks)


def adjoint_kernel(
    rg_ref, gelu_ref, a_ref, prod_ref, sum_ref, in_ref,
    gg_ref, tprod_ref, tsum_ref,
    a_scr, b_scr, p_scr, s_scr,
):
    rows, length, _ = rg_ref.shape
    for b in range(rows):
        states = sum_ref[b] + prod_ref[b] * in_ref[b, 0:1]
        value, slope = gelu_pair(gelu_ref[b])
        rg = rg_ref[b]
        gg_ref[b] = (rg * states * slope).astype(BF16)
        to_lanes(a_scr, b, 0, a_ref[b])
        to_lanes(a_scr, b, length, jnp.ones((8, HEAD_W), F32))
        to_lanes(b_scr, b, 0, rg * value)
    sweep(a_scr, b_scr, p_scr, s_scr, tprod_ref, tsum_ref, rows, length, True, 1)


def recurrent_adjoint(rec_grad, gelu_in, coef, prod, total, state_in):
    rows, length, units = rec_grad.shape
    full = head_spec(rows, length)
    scan = pltpu.VMEM((rows, HEAD_W // LANES, length, LANES), F32)
    longer = pltpu.VMEM((rows, HEAD_W // LANES, length + 8, LANES), F32)
    big = jax.ShapeDtypeStruct((rows, length, units), F32)
    return pl.pallas_call(
        adjoint_kernel,
        grid=(units // HEAD_W,),
        in_specs=[full] * 5 + [head_spec(rows, 8)],
        out_specs=[full] * 3,
        out_shape=[jax.ShapeDtypeStruct((rows, length, units), BF16), big, big],
        scratch_shapes=[longer, scan, scan, scan],
        compiler_params=pltpu.CompilerParams(vmem_limit_bytes=48 * 1024 * 1024),
        cost_estimate=pl.CostEstimate(
            flops=30 * rows * length * units,
            bytes_accessed=32 * rows * length * units,
            transcendentals=rows * length * units,
        ),
        name="recurrent_adjoint",
    )(rec_grad, gelu_in, coef, prod, total, state_in)


def backward_kernel(
    tprod_ref, tsum_ref, leave_ref, prod_ref, sum_ref, in_ref, a_ref, r_ref, i_ref, conv_ref,
    x_ref, halo_ref, mask_ref, par_ref, w_ref,
    bx_ref, before_ref, small_ref, blocks_ref,
    ext, st_ext, g_ext,
):
    rows, length, _ = tprod_ref.shape
    par = par_ref[...]
    w0, w1 = w_ref[0], w_ref[1]
    sums = [jnp.zeros((1, HEAD_W), F32) for _ in range(8)]
    blocks = [jnp.zeros((HEAD_W, HEAD_W), F32) for _ in range(2)]

    def add(n, value):
        sums[n] = sums[n] + jnp.sum(value, axis=0, keepdims=True)

    for b in range(rows):
        adjoint = tsum_ref[b] + tprod_ref[b] * leave_ref[b, 0:1]
        st_ext[b, pl.ds(0, 8), :] = in_ref[b]
        st_ext[b, pl.ds(8, length), :] = sum_ref[b] + prod_ref[b] * in_ref[b, 0:1]
        prev = st_ext[b, pl.ds(7, length), :]
        r, i, a = r_ref[b], i_ref[b], a_ref[b]
        conv_low = conv_ref[b]
        conv = conv_low.astype(F32)
        going = mask_ref[b, :, 0:1]
        log_keep = -DECAY_SCALE * r * par[SOFTPLUS : SOFTPLUS + 1]
        scale = jnp.where(going > 0.5, jnp.sqrt(one_minus_exp(2.0 * log_keep)), 1.0)
        log_grad = adjoint * prev * a - adjoint * i * conv * (a * a) / scale
        rate = log_grad * (-DECAY_SCALE * par[SOFTPLUS : SOFTPLUS + 1]) * r * (1.0 - r)
        spread = adjoint * scale
        inlet = spread * conv * i * (1.0 - i)
        add(5, rate)
        add(6, inlet)
        add(7, log_grad * r)
        rate_low = rate.astype(BF16)
        inlet_low = inlet.astype(BF16)
        grad = spread * i + dot(rate_low, w0, ((1,), (1,))) + dot(inlet_low, w1, ((1,), (1,)))
        blocks[0] = blocks[0] + dot(conv_low, rate_low, ((0,), (0,)))
        blocks[1] = blocks[1] + dot(conv_low, inlet_low, ((0,), (0,)))
        ext[b, pl.ds(0, 8), :] = halo_ref[b]
        ext[b, pl.ds(8, length), :] = x_ref[b].astype(F32)
        add(4, grad)
        add(0, grad * ext[b, pl.ds(8, length), :])
        bx = grad * par[TAP0 : TAP0 + 1]
        g_ext[b, pl.ds(0, 8), :] = jnp.zeros((8, HEAD_W), F32)
        g_ext[b, pl.ds(8 + length, 8), :] = jnp.zeros((8, HEAD_W), F32)
        before = jnp.zeros((8, HEAD_W), F32)
        for k in range(1, 4):
            masked = grad * mask_ref[b, :, k : k + 1]
            add(k, masked * ext[b, pl.ds(8 - k, length), :])
            g_ext[b, pl.ds(8, length), :] = masked
            tap = par[TAP0 + k : TAP0 + k + 1]
            bx = bx + tap * g_ext[b, pl.ds(8 + k, length), :]
            before = before + tap * g_ext[b, pl.ds(k, 8), :]
        bx_ref[b] = bx
        before_ref[b] = before
    sums[7] = sums[7] * (DECAY_SCALE * par[NEG_SIG : NEG_SIG + 1])
    for n in range(8):
        small_ref[pl.ds(n, 1), :] = sums[n]
    blocks_ref[0] = blocks[0].astype(blocks_ref.dtype)
    blocks_ref[1] = blocks[1].astype(blocks_ref.dtype)


def recurrent_backward(tprod, tsum, leaving, prod, total, state_in, coef, r, i, conv_low, x_branch, halo, masks, params, blocks):
    rows, length, units = tprod.shape
    full = head_spec(rows, length)
    edge = head_spec(rows, 8)
    return pl.pallas_call(
        backward_kernel,
        grid=(units // HEAD_W,),
        in_specs=[
            full, full, edge, full, full, edge, full, full, full, full, full, edge,
            pl.BlockSpec((rows, length, 8), lambda h: (0, 0, 0)),
            pl.BlockSpec((PARAM_ROWS, HEAD_W), lambda h: (0, h)),
            pl.BlockSpec((2, HEAD_W, HEAD_W), lambda h: (0, 0, h)),
        ],
        out_specs=[
            full,
            edge,
            pl.BlockSpec((8, HEAD_W), lambda h: (0, h)),
            pl.BlockSpec((2, HEAD_W, HEAD_W), lambda h: (0, 0, h)),
        ],
        out_shape=[
            jax.ShapeDtypeStruct((rows, length, units), F32),
            jax.ShapeDtypeStruct((rows, 8, units), F32),
            jax.ShapeDtypeStruct((8, units), F32),
            jax.ShapeDtypeStruct((2, HEAD_W, units), BF16),
        ],
        scratch_shapes=[
            pltpu.VMEM((rows, length + 8, HEAD_W), F32),
            pltpu.VMEM((rows, length + 8, HEAD_W), F32),
            pltpu.VMEM((rows, length + 16, HEAD_W), F32),
        ],
        compiler_params=pltpu.CompilerParams(vmem_limit_bytes=48 * 1024 * 1024),
        cost_estimate=pl.CostEstimate(
            flops=8 * rows * length * units * HEAD_W,
            bytes_accessed=40 * rows * length * units,
            transcendentals=4 * rows * length * units,
        ),
        name="recurrent_backward",
    )(tprod, tsum, leaving, prod, total, state_in, coef, r, i, conv_low, x_branch, halo, masks, params, blocks)


def rms(values):
    return lax.rsqrt(jnp.mean(values * values, axis=-1, keepdims=True) + EPSILON)


def rms_back(values, inverse, gain, grad):
    u = grad * gain
    inner = jnp.mean(values * u, axis=-1, keepdims=True)
    gain_grad = jnp.sum(grad * values * inverse, axis=0)
    return inverse * u - values * (inverse * inverse * inverse) * inner, gain_grad


def exchange_units(x, axis):
    length, me = lax.axis_size(axis), lax.axis_index(axis)
    got = [lax.dynamic_index_in_dim(x, me, 0, keepdims=False)]
    for by in range(1, length):
        piece = lax.dynamic_index_in_dim(x, (me + by) % length, 0, keepdims=False)
        got.append(lax.ppermute(piece, axis, [(s, (s + by) % length) for s in range(length)]))
    stacked = jnp.stack(got)
    order = (me - jnp.arange(length)) % length
    return jnp.take(stacked, order, axis=0)


def shards(
    block_input, segments, token_mask, cotangent, norm_gains, conv_taps, conv_offset, gate_offset,
    decay_logit, intake, gate_blocks, outlet, expand, contract,
):
    rows, length, width = block_input.shape
    depth = intake.shape[0]
    units = intake.shape[2]
    hidden_units = contract.shape[1]
    tokens = rows * length
    ctx, tp = lax.axis_size("ctx"), lax.axis_size("tp")
    mine = lax.axis_index("tp")
    half = tokens // tp
    share = -(-hidden_units // (ctx * 256)) * 256
    padding = ctx * share - hidden_units

    def own(x):
        return lax.dynamic_slice_in_dim(x, mine * half, half, 0)

    def other(x):
        return lax.dynamic_slice_in_dim(x, (1 - mine) * half, half, 0)

    def join(x):
        theirs = swap(x, "tp")
        return jnp.concatenate(
            [jnp.where(mine == 0, x, theirs), jnp.where(mine == 0, theirs, x)], axis=0
        )

    w_intake = lax.all_gather(intake.reshape(depth, 2 * units), ("fsdp", "ctx"), axis=0, tiled=True)
    w_gates = lax.all_gather(gate_blocks, ("fsdp", "ctx"), axis=0, tiled=True)
    w_outlet = lax.all_gather(outlet, ("fsdp", "ctx"), axis=0, tiled=True)

    feed_in = jnp.concatenate([expand, contract[:, None, :]], axis=1)
    feed_in = jnp.pad(feed_in, ((0, 0), (0, 0), (0, padding)))
    feed_in = feed_in.reshape(depth, 3, ctx, share).transpose(2, 0, 1, 3).reshape(ctx, depth, 3 * share)
    feed_in = exchange_units(feed_in, "ctx").reshape(ctx * depth, 3 * share)
    w_feed = lax.all_gather(feed_in, "fsdp", axis=0, tiled=True)
    w_expand, w_contract = w_feed[:, : 2 * share], w_feed[:, 2 * share :]

    mask_rows = token_mask.astype(F32).reshape(tokens, 1)
    out_grad = own(cotangent.reshape(tokens, width)).astype(F32) * own(mask_rows)
    feed_grad = lax.all_gather(out_grad.astype(BF16), ("ctx", "tp"), axis=0, tiled=True)

    seg_next = segments + 1
    seg_before = shifted(seg_next[:, -3:], "ctx", 1)
    seg_ext = jnp.concatenate([seg_before, seg_next], axis=1)
    masks = jnp.stack(
        [(seg_ext[:, 3 - k : 3 - k + length] == seg_next).astype(F32) for k in (1, 1, 2, 3)]
        + [jnp.zeros(segments.shape, F32)] * 4,
        axis=2,
    )
    params = jnp.concatenate(
        [
            conv_taps,
            conv_offset[None],
            gate_offset,
            jax.nn.softplus(-decay_logit)[None],
            jax.nn.sigmoid(-decay_logit)[None],
            jnp.zeros((PARAM_ROWS - 9, units), F32),
        ],
        axis=0,
    )

    x = block_input.reshape(tokens, width).astype(F32)
    inverse_one = rms(x)
    normed = (x * inverse_one * norm_gains[0]).astype(BF16)
    x_branch = dot(normed, w_intake[:, units:], ((1,), (0,))).astype(BF16).reshape(rows, length, units)
    gelu_in = dot(normed, w_intake[:, :units], ((1,), (0,))).reshape(rows, length, units)
    x_before = shifted(x_branch[:, -3:], "ctx", 1)
    halo = jnp.pad(x_before, ((0, 0), (5, 0), (0, 0))).astype(F32)
    blocks = w_gates.transpose(1, 0, 2)
    conv_low, r, i, coef, prod, total = recurrent_forward(x_branch, halo, masks, params, blocks)
    ends = jnp.stack([prod[:, -1], total[:, -1]])
    entering = jnp.zeros((rows, units), F32)
    for by in range(ctx - 1, 0, -1):
        end = shifted(ends, "ctx", by)
        entering = end[1] + end[0] * entering
    state_in = jnp.broadcast_to(entering[:, None], (rows, 8, units))
    states = total + prod * entering[:, None]
    recurrent = (states * jax.nn.gelu(gelu_in, approximate=True)).astype(BF16).reshape(tokens, units)

    sent = swap(dot(other(recurrent), w_outlet, ((1,), (1,))), "tp")
    branch = dot(own(recurrent), w_outlet, ((1,), (1,))) + sent
    residual = own(x) + branch
    inverse_two = rms(residual)
    normed_two = lax.all_gather(
        (residual * inverse_two * norm_gains[1]).astype(BF16), ("ctx", "tp"), axis=0, tiled=True
    )

    expanded = dot(normed_two, w_expand, ((1,), (0,)))
    gate, up = expanded[:, :share], expanded[:, share:]
    value, slope = gelu_pair(gate)
    hidden = (value * up).astype(BF16)
    hidden_grad = dot(feed_grad, w_contract, ((1,), (0,)))
    expand_low = jnp.concatenate(
        [(hidden_grad * up * slope).astype(BF16), (hidden_grad * value).astype(BF16)], axis=1
    )
    normed_two_grad = lax.psum_scatter(
        dot(expand_low, w_expand, ((1,), (1,))).astype(BF16), ("ctx", "tp"), scatter_dimension=0, tiled=True
    ).astype(F32)
    feed_out = lax.psum_scatter(
        dot(hidden, w_contract, ((1,), (1,))).astype(BF16), ("ctx", "tp"), scatter_dimension=0, tiled=True
    ).astype(F32)
    block_output = join((residual + feed_out).astype(BF16)).reshape(rows, length, width)

    feed_weight_grad = jnp.concatenate(
        [
            dot(normed_two, expand_low, ((0,), (0,))).astype(BF16),
            dot(feed_grad, hidden, ((0,), (0,))).astype(BF16),
        ],
        axis=1,
    )
    feed_part = lax.psum_scatter(feed_weight_grad, "fsdp", scatter_dimension=0, tiled=True)
    feed_part = exchange_units(feed_part.reshape(ctx, depth, 3 * share), "ctx")
    feed_part = feed_part.reshape(ctx, depth, 3, share).transpose(1, 2, 0, 3).reshape(depth, 3, ctx * share)
    feed_part = feed_part[:, :, :hidden_units].astype(F32)

    norm_part, gain_two = rms_back(residual, inverse_two, norm_gains[1], normed_two_grad)
    residual_grad = out_grad + norm_part
    branch_grad = join(residual_grad.astype(BF16))
    outlet_grad = dot(branch_grad, recurrent, ((0,), (0,))).astype(BF16)
    rec_grad = dot(branch_grad, w_outlet, ((1,), (0,))).reshape(rows, length, units)
    gelu_grad, tprod, tsum = recurrent_adjoint(rec_grad, gelu_in, coef, prod, total, state_in)
    heads = jnp.stack([coef[:, 0] * tprod[:, 0], coef[:, 0] * tsum[:, 0]])
    leaving = jnp.zeros((rows, units), F32)
    for by in range(ctx - 1, 0, -1):
        head = shifted(heads, "ctx", -by)
        leaving = head[1] + head[0] * leaving
    leaving = jnp.broadcast_to(leaving[:, None], (rows, 8, units))
    branch_x, before, small, blocks_grad = recurrent_backward(
        tprod, tsum, leaving, prod, total, state_in, coef, r, i, conv_low, x_branch, halo, masks, params, blocks
    )
    from_next = shifted(before[:, 5:], "ctx", -1)
    branch_x = branch_x + jnp.pad(from_next, ((0, 0), (length - 3, 0), (0, 0)))
    intake_low = jnp.concatenate([gelu_grad, branch_x.astype(BF16)], axis=2).reshape(tokens, 2 * units)

    sent = swap(dot(other(intake_low), w_intake, ((1,), (1,))), "tp")
    normed_grad = dot(own(intake_low), w_intake, ((1,), (1,))) + sent
    norm_part, gain_one = rms_back(own(x), own(inverse_one), norm_gains[0], normed_grad)
    input_grad = join(residual_grad + norm_part).reshape(rows, length, width)

    intake_grad = dot(normed, intake_low, ((0,), (0,))).astype(BF16)

    def scatter(grad):
        part = lax.psum_scatter(grad, "fsdp", scatter_dimension=0, tiled=True)
        return lax.psum_scatter(part, "ctx", scatter_dimension=0, tiled=True).astype(F32)

    outlet_part = scatter(outlet_grad)
    blocks_part = scatter(blocks_grad.transpose(1, 0, 2).reshape(HEAD_W, 2 * units)).reshape(-1, 2, units)
    intake_part = scatter(intake_grad).reshape(depth, 2, units)

    gains = jnp.stack([gain_one, gain_two])
    gains, small = lax.psum((gains, small), ("fsdp", "ctx"))
    gains = lax.psum(gains, "tp")
    return (
        block_output,
        input_grad,
        gains,
        small[0:4],
        small[4],
        small[5:7],
        small[7],
        intake_part,
        blocks_part,
        outlet_part,
        feed_part[:, :2],
        feed_part[:, 2],
    )


def solution(mesh):
    placed = (
        P("fsdp", "ctx", None),
        P("fsdp", "ctx"),
        P("fsdp", "ctx"),
        P("fsdp", "ctx", None),
        P(),
        P(None, "tp"),
        P("tp"),
        P(None, "tp"),
        P("tp"),
        P(("fsdp", "ctx"), None, "tp"),
        P(("fsdp", "ctx"), None, "tp"),
        P(("fsdp", "ctx"), "tp"),
        P(("fsdp", "ctx"), None, "tp"),
        P(("fsdp", "ctx"), "tp"),
    )
    return jax.shard_map(
        shards,
        mesh=mesh,
        in_specs=placed,
        out_specs=(
            P("fsdp", "ctx", None),
            P("fsdp", "ctx", None),
            P(),
            P(None, "tp"),
            P("tp"),
            P(None, "tp"),
            P("tp"),
            P(("fsdp", "ctx"), None, "tp"),
            P(("fsdp", "ctx"), None, "tp"),
            P(("fsdp", "ctx"), "tp"),
            P(("fsdp", "ctx"), None, "tp"),
            P(("fsdp", "ctx"), "tp"),
        ),
        check_vma=False,
    )
```

time: 4560 us -> 1690 us (0.37)
  waiting for transfers between devices: 3260 us -> 985 us
  local copies, waits for them, and re-layouts: 574 us -> 129 us
  other arithmetic: 220 us -> 80.4 us
  blocking collectives: 190 us -> 81.5 us
  starting transfers between devices: 14.1 us -> 107 us
    reduce_scatter x4 -> x7, waiting for transfers between devices: 2380 us -> 386 us  [the longest x1 107 us: shards(): lax.psum_scatter(dot(hidden, w_contract, ((1,), (1,))).astype(BF16), ('ct...]
    all_gather x5 -> x6, waiting for transfers between devices: 788 us -> 403 us  [the longest x1 123 us: shards(): w_feed = lax.all_gather(feed_in, 'fsdp', axis=0, tiled=True)]
    slice x227 -> x7, local copies, waits for them, and re-layouts: 342 us -> 2.26 us  [the longest x1 0.63 us: shards(): small[7]]
    ppermute x5 -> x20, waiting for transfers between devices: 0.01 us -> 195 us  [the longest x6 174 us: exchange_units(): lax.ppermute(piece, axis, [(s, (s + by) % length) for s in range(length)])]
    all_gather x8 -> x0, blocking collectives: 105 us -> none  [prefix(): everything = jax.tree.map(lambda part: lax.all_gather(part, axis), x)]
    pad x112 -> x0, local copies, waits for them, and re-layouts: 102 us -> none  [affine_state_sweep(): lax.associative_scan(merge_affine_maps, (forget_multipliers, sweep_increm...]
    ppermute x5 -> x20, starting transfers between devices: 13.6 us -> 105 us  [the longest x9 91.8 us: shifted(): return lax.ppermute(x, axis, pairs)]
    add x97 -> x3, other arithmetic: 72.6 us -> 3.82 us  [the longest x1 3.74 us: shards(): input_grad = join(residual_grad + norm_part).reshape(rows, length, width)]
  transfers between devices with their start and end apart: 18 -> 35, of which waited for: 11 -> 23; matrix products, arithmetic and copies ran while one was open for 14% -> 21% of each run, Pallas kernels for 0% -> 1%
where the time goes in v1:
time: 1690 us; the launch traced here: 1670 us
  waiting for transfers between devices  985 us (58%)
  matrix products  226 us (13%)
  local copies, waits for them, and re-layouts  129 us (8%)
  starting transfers between devices  107 us (6%)
  blocking collectives  81.5 us (5%)
  other arithmetic  80.4 us (5%)
  Pallas kernels  42.8 us (3%)
    dot_general x15, matrix products, dot(): return lax.dot_general(a, b, (dims, ((), ())), preferred_element_type=F32)  226 us
    ppermute x6, waiting for transfers between devices, exchange_units(): lax.ppermute(piece, axis, [(s, (s + by) % length) for s in range(length)])  174 us
    all_gather x1, waiting for transfers between devices, shards(): w_feed = lax.all_gather(feed_in, 'fsdp', axis=0, tiled=True)  123 us
    reduce_scatter x1, waiting for transfers between devices, shards(): lax.psum_scatter(dot(hidden, w_contract, ((1,), (1,))).astype(BF16), ('ct...  107 us
    all_gather x1, waiting for transfers between devices, shards(): lax.all_gather((residual * inverse_two * norm_gains[1]).astype(BF16), ('c...  101 us
    ppermute x9, starting transfers between devices, shifted(): return lax.ppermute(x, axis, pairs)  91.8 us
    reduce_scatter x1, waiting for transfers between devices, shards(): lax.psum_scatter(dot(expand_low, w_expand, ((1,), (1,))).astype(BF16), ('...  90.7 us
    reduce_scatter x2, waiting for transfers between devices, scatter(): part = lax.psum_scatter(grad, 'fsdp', scatter_dimension=0, tiled=True)  90.4 us
  transfers between devices with their start and end apart: 35, of which 23 were waited for; matrix products, arithmetic and copies ran while one was open for 21% of the time, Pallas kernels for 1%

profile of v1, /device:TPU:0, one launch (start us, length us, event | category | flops | bytes accessed | tf_op | source)
XLA Modules:
  0.0 1666.0 jit_solution(12314571342631693426)
XLA Ops:
  61.8 41.7 %collective-permute-done.6 = bf16[160,3072]{1,0:T(8,128)(2,1)S(1)} collective-permute-done((bf16[160,3072]{1,0:T(8,128)(2,1)S(1)}, bf16[160,3072]{1,0:T(8,128)(2,1)S(1)}, u32[]{:S(2)}, u32[]{:S(2)}) %collective-permute-start.6) | collective-permute-done | bytes 983072 | tf_op jit(solution)/shard_map/ppermute | solution.py:334
  103.5 48.2 %collective-permute-done.7 = bf16[160,3072]{1,0:T(8,128)(2,1)S(1)} collective-permute-done((bf16[160,3072]{1,0:T(8,128)(2,1)S(1)}, bf16[160,3072]{1,0:T(8,128)(2,1)S(1)}, u32[]{:S(2)}, u32[]{:S(2)}) %collective-permute-start.7) | collective-permute-done | bytes 983072 | tf_op jit(solution)/shard_map/ppermute | solution.py:334
  164.0 76.9 %collective-permute-start.1 = (s32[2,3]{1,0:T(2,128)S(1)}, s32[2,3]{1,0:T(2,128)S(1)}, u32[]{:S(2)}, u32[]{:S(2)}) collective-permute-start(s32[2,3]{1,0:T(2,128)S(1)} %slice.162), channel_id=1, source_target_pairs={{0,2},{2,4},{4,6},{1,3},{3,5},{5,7},{8,10},{10,12},{12,14},{9,11},... | collective-permute-start | bytes 80 | tf_op jit(solution)/shard_map/ppermute | solution.py:26
  253.1 49.4 %all-gather.9.cloned.1.call-done = bf16[256,2,1280]{2,0,1:T(8,128)(2,1)} async-done(((bf16[16,2,1280]{2,0,1:T(8,128)(2,1)}), bf16[256,2,1280]{2,0,1:T(8,128)(2,1)}) %all-gather.9.cloned.1.call-update) | async-done | bytes 1310736 | tf_op jit(solution)/shard_map/all_gather | solution.py:368
  341.9 59.1 %all-gather.11.cloned.1.call-done = bf16[2560,1280]{1,0:T(8,128)(2,1)} async-done(((bf16[160,1280]{1,0:T(8,128)(2,1)}), bf16[2560,1280]{1,0:T(8,128)(2,1)}) %all-gather.11.cloned.1.call-update) | async-done | bytes 6553616 | tf_op jit(solution)/shard_map/all_gather | solution.py:369
  427.5 122.8 %all-gather.15.cloned.1.call-done = bf16[2560,3072]{1,0:T(8,128)(2,1)} async-done(((bf16[640,3072]{1,0:T(8,128)(2,1)}), bf16[2560,3072]{1,0:T(8,128)(2,1)}) %all-gather.15.cloned.1.call-update) | async-done | bytes 15728656 | tf_op jit(solution)/shard_map/all_gather | solution.py:375
  550.3 101.5 %all-gather.13.cloned.1.call-done = bf16[2048,2560]{1,0:T(8,128)(2,1)} async-done(((bf16[256,2560]{1,0:T(8,128)(2,1)}), bf16[2048,2560]{1,0:T(8,128)(2,1)}) %all-gather.13.cloned.1.call-update) | async-done | bytes 10485776 | tf_op jit(solution)/shard_map/all_gather | solution.py:424
  651.8 29.4 %fusion.3 = f32[2048,2048]{0,1:T(8,128)} fusion(bf16[2048,2560]{1,0:T(8,128)(2,1)} %all-gather.13.cloned.1.call-done, bf16[2560,3072]{1,0:T(8,128)(2,1)} %all-gather.15.cloned.1.call-done), kind=kOutput, calls=%fused_computation.14 | convolution fusion | flops 21474836480 | bytes 37748736 | tf_op jit(solution)/shard_map/dot_general | solution.py:53
  681.1 69.9 %all-gather.17.cloned.1.call-done = bf16[2048,2560]{1,0:T(8,128)(2,1)} async-done(((bf16[256,2560]{1,0:T(8,128)(2,1)}), bf16[2048,2560]{1,0:T(8,128)(2,1)}) %all-gather.17.cloned.1.call-update) | async-done | bytes 10485776 | tf_op jit(solution)/shard_map/all_gather | solution.py:380
  751.1 24.1 %fusion.11 = (bf16[2048,1024]{0,1:T(8,128)(2,1)}, bf16[2048,1024]{0,1:T(8,128)(2,1)}, bf16[2048,1024]{0,1:T(8,128)(2,1)}) fusion(f32[2048,2048]{0,1:T(8,128)} %fusion.3, bf16[2048,2560]{1,0:T(8,128)(2,1)} %all-gather.17.cloned.1.call-done, bf16[2560,3072]{1,0:T(8,128)(2,1)} %all-gather.15.cloned.1.call-done), kind=kOutput, calls=%fused_computation.22 | convolution fusion | flops 10789847040 | bytes 45088768 | tf_op jit(solution)/shard_map/dot_general | solution.py:53
  775.2 29.1 %convolution_convert_fusion.1 = bf16[2048,2560]{1,0:T(8,128)(2,1)} fusion(bf16[2560,3072]{1,0:T(8,128)(2,1)} %all-gather.15.cloned.1.call-done, bf16[2048,1024]{0,1:T(8,128)(2,1)} %get-tuple-element.126, bf16[2048,1024]{0,1:T(8,128)(2,1)} %get-tuple-element.125), kind=kOutput, calls=%fused_computation.7 | convolution fusion | flops 21496856576 | bytes 29360128 | tf_op jit(solution)/shard_map/dot_general | solution.py:53
  804.4 16.9 %convolution_convert_fusion.3 = bf16[2048,2560]{1,0:T(8,128)(2,1)} fusion(bf16[2048,1024]{0,1:T(8,128)(2,1)} %get-tuple-element.127, bf16[2560,3072]{1,0:T(8,128)(2,1)} %all-gather.15.cloned.1.call-done), kind=kOutput, calls=%fused_computation.9 | convolution fusion | flops 10742661120 | bytes 19922944 | tf_op jit(solution)/shard_map/dot_general | solution.py:53
  821.5 90.7 %reduce-scatter.18.cloned.1.call-done = bf16[256,2560]{1,0:T(8,128)(2,1)} async-done(((bf16[2048,2560]{1,0:T(8,128)(2,1)}), bf16[256,2560]{1,0:T(8,128)(2,1)}) %reduce-scatter.18.cloned.1.call-update) | async-done | bytes 1310736 | tf_op jit(solution)/shard_map/reduce_scatter | solution.py:436
  915.8 106.6 %reduce-scatter.16.cloned.1.call-done = bf16[256,2560]{1,0:T(8,128)(2,1)} async-done(((bf16[2048,2560]{1,0:T(8,128)(2,1)}), bf16[256,2560]{1,0:T(8,128)(2,1)}) %reduce-scatter.16.cloned.1.call-update) | async-done | bytes 1310736 | tf_op jit(solution)/shard_map/reduce_scatter | solution.py:439
  1115.6 16.6 convolution_convert_fusion.4
  1132.2 26.9 %convolution_convert_fusion = bf16[2560,2048]{0,1:T(8,128)(2,1)} fusion(bf16[2048,2560]{1,0:T(8,128)(2,1)} %all-gather.13.cloned.1.call-done, bf16[2048,1024]{0,1:T(8,128)(2,1)S(1)} %copy-done.34, bf16[2048,1024]{0,1:T(8,128)(2,1)S(1)} %copy-done.33), kind=kOutput, calls=%fused_computation.6 | convolution fusion | flops 21496856576 | bytes 29360128 | tf_op jit(solution)/shard_map/dot_general | solution.py:53
  1159.2 17.7 %pad_maximum_fusion = bf16[2560,3072]{0,1:T(8,128)(2,1)} fusion(bf16[2560,1024]{0,1:T(8,128)(2,1)} %convolution_convert_fusion.4, bf16[2560,2048]{0,1:T(8,128)(2,1)} %convolution_convert_fusion), kind=kLoop, calls=%fused_computation.3 | loop fusion | flops 31457280 | bytes 31457280 | tf_op jit(solution)/shard_map/concatenate | solution.py:444
  1176.9 20.7 %copy.109 = bf16[2560,3072]{1,0:T(8,128)(2,1)} copy(bf16[2560,3072]{0,1:T(8,128)(2,1)} %pad_maximum_fusion) | data formatting | bytes 31457280
  1228.8 90.4 %reduce-scatter.20.cloned.1.call-done = bf16[640,2560]{1,0:T(8,128)(2,1)} async-done(((bf16[2560,2560]{1,0:T(8,128)(2,1)}), bf16[640,2560]{1,0:T(8,128)(2,1)}) %reduce-scatter.20.cloned.1.call-update) | async-done | bytes 3276816 | tf_op jit(solution)/shard_map/reduce_scatter | solution.py:483
  1322.8 77.5 %all-reduce.3 = (f32[2,2560]{1,0:T(2,128)S(1)}, f32[8,1280]{1,0:T(8,128)S(1)}) all-reduce(f32[2,2560]{1,0:T(2,128)S(1)} %pad_maximum_fusion.14, f32[8,1280]{1,0:T(8,128)S(1)} %get-tuple-element.37), channel_id=1, replica_groups=mesh['fsdp'=4,'ctx'=4,'tp'=2] {'fsdp','ctx'}, use_global_device_ids=true, to_apply=%region_8.10 | all-reduce | flops 15360 | bytes 122880 | tf_op jit(solution)/shard_map/psum | solution.py:491
  1408.3 82.0 %reduce-scatter.32.cloned.1.call-done = bf16[640,3072]{1,0:T(8,128)(2,1)} async-done(((bf16[2560,3072]{1,0:T(8,128)(2,1)}), bf16[640,3072]{1,0:T(8,128)(2,1)}) %reduce-scatter.32.cloned.1.call-update) | async-done | bytes 3932176 | tf_op jit(solution)/shard_map/reduce_scatter | solution.py:451
  1503.0 33.1 %collective-permute-done.17 = bf16[160,3072]{1,0:T(8,128)(2,1)S(1)} collective-permute-done((bf16[160,3072]{1,0:T(8,128)(2,1)S(1)}, bf16[160,3072]{1,0:T(8,128)(2,1)S(1)}, u32[]{:S(2)}, u32[]{:S(2)}) %collective-permute-start.17) | collective-permute-done | bytes 983072 | tf_op jit(solution)/shard_map/ppermute | solution.py:334
  1536.1 50.5 %collective-permute-done.18 = bf16[160,3072]{1,0:T(8,128)(2,1)S(1)} collective-permute-done((bf16[160,3072]{1,0:T(8,128)(2,1)S(1)}, bf16[160,3072]{1,0:T(8,128)(2,1)S(1)}, u32[]{:S(2)}, u32[]{:S(2)}) %collective-permute-start.18) | collective-permute-done | bytes 983072 | tf_op jit(solution)/shard_map/ppermute | solution.py:334
  1639.7 16.4 reduce-scatter.22.cloned.1.call-done
  (242 shorter events, 352.9 us)
Async XLA Ops:
  7.2 235.7 %all-gather.7.cloned.1.call-start = ((), (), s32[]{:S(2)}) async-start(), calls=%async_computation.9 | async-start | bytes 13926400 | tf_op jit(solution)/shard_map/all_gather | solution.py:367
  9.5 292.9 %all-gather.9.cloned.1.call-start = ((), (), s32[]{:S(2)}) async-start(), calls=%async_computation.10 | async-start | bytes 1392640 | tf_op jit(solution)/shard_map/all_gather | solution.py:368
  11.1 389.9 %all-gather.11.cloned.1.call-start = ((), (), s32[]{:S(2)}) async-start(), calls=%async_computation.11 | async-start | bytes 6963200 | tf_op jit(solution)/shard_map/all_gather | solution.py:369
  11.9 538.4 %all-gather.15.cloned.1.call-start = ((), (), s32[]{:S(2)}) async-start(), calls=%async_computation.13 | async-start | bytes 19660800 | tf_op jit(solution)/shard_map/all_gather | solution.py:375
  54.8 48.7 %collective-permute-start.6 = (bf16[160,3072]{1,0:T(8,128)(2,1)S(1)}, bf16[160,3072]{1,0:T(8,128)(2,1)S(1)}, u32[]{:S(2)}, u32[]{:S(2)}) collective-permute-start(bf16[160,3072]{1,0:T(8,128)(2,1)S(1)} %get-tuple-element.137), channel_id=1, source_target_pairs={{0,2},{2,4},{4,6},{6,0},{1,3},{3,5},{5,7},{7,1},{8,10},{10,12},{12... | collective-permute-start | bytes 2949128 | tf_op jit(solution)/shard_map/ppermute | solution.py:334
  57.8 93.9 %collective-permute-start.7 = (bf16[160,3072]{1,0:T(8,128)(2,1)S(1)}, bf16[160,3072]{1,0:T(8,128)(2,1)S(1)}, u32[]{:S(2)}, u32[]{:S(2)}) collective-permute-start(bf16[160,3072]{1,0:T(8,128)(2,1)S(1)} %get-tuple-element.136), channel_id=1, source_target_pairs={{0,4},{2,6},{4,0},{6,2},{1,5},{3,7},{5,1},{7,3},{8,12},{10,14},{12... | collective-permute-start | bytes 2949128 | tf_op jit(solution)/shard_map/ppermute | solution.py:334
  60.4 91.3 %collective-permute-start.8 = (bf16[160,3072]{1,0:T(8,128)(2,1)S(1)}, bf16[160,3072]{1,0:T(8,128)(2,1)S(1)}, u32[]{:S(2)}, u32[]{:S(2)}) collective-permute-start(bf16[160,3072]{1,0:T(8,128)(2,1)S(1)} %get-tuple-element.135), channel_id=1, source_target_pairs={{0,6},{2,0},{4,2},{6,4},{1,7},{3,1},{5,3},{7,5},{8,14},{10,8},{12,... | collective-permute-start | bytes 2949128 | tf_op jit(solution)/shard_map/ppermute | solution.py:334
  163.3 488.5 %all-gather.13.cloned.1.call-start = ((), (), s32[]{:S(2)}) async-start(), calls=%async_computation.12 | async-start | bytes 11796480 | tf_op jit(solution)/shard_map/all_gather | solution.py:424
  164.0 87.7 %collective-permute-start.1 = (s32[2,3]{1,0:T(2,128)S(1)}, s32[2,3]{1,0:T(2,128)S(1)}, u32[]{:S(2)}, u32[]{:S(2)}) collective-permute-start(s32[2,3]{1,0:T(2,128)S(1)} %slice.162), channel_id=1, source_target_pairs={{0,2},{2,4},{4,6},{1,3},{3,5},{5,7},{8,10},{10,12},{12,14},{9,11},... | collective-permute-start | bytes 80 | tf_op jit(solution)/shard_map/ppermute | solution.py:26
  424.1 327.0 %all-gather.17.cloned.1.call-start = ((), (), s32[]{:S(2)}) async-start(), calls=%async_computation.15 | async-start | bytes 11796480 | tf_op jit(solution)/shard_map/all_gather | solution.py:380
  427.0 485.3 %reduce-scatter.18.cloned.1.call-start = ((), (), s32[]{:S(2)}) async-start(), calls=%async_computation.16 | async-start | bytes 11796480 | tf_op jit(solution)/shard_map/reduce_scatter | solution.py:436
  804.3 218.1 %reduce-scatter.16.cloned.1.call-start = ((), (), s32[]{:S(2)}) async-start(), calls=%async_computation.14 | async-start | bytes 11796480 | tf_op jit(solution)/shard_map/reduce_scatter | solution.py:439
  821.3 337.8 %reduce-scatter.28.cloned.1.call-start = ((), (), s32[]{:S(2)}) async-start(), calls=%async_computation.21 | async-start | bytes 1638400
  1088.1 120.0 %reduce-scatter.24.cloned.1.call-start = ((), (), s32[]{:S(2)}) async-start(), calls=%async_computation.19 | async-start | bytes 8192000 | tf_op jit(solution)/shard_map/reduce_scatter | solution.py:483
  1096.7 222.5 %reduce-scatter.20.cloned.1.call-start = ((), (), s32[]{:S(2)}) async-start(), calls=%async_computation.17 | async-start | bytes 16384000 | tf_op jit(solution)/shard_map/reduce_scatter | solution.py:483
  1115.4 290.8 %reduce-scatter.30.cloned.1.call-start = ((), (), s32[]{:S(2)}) async-start(), calls=%async_computation.22 | async-start | bytes 409600
  1159.1 331.1 %reduce-scatter.32.cloned.1.call-start = ((), (), s32[]{:S(2)}) async-start(), calls=%async_computation.23 | async-start | bytes 19660800 | tf_op jit(solution)/shard_map/reduce_scatter | solution.py:451
  1197.6 440.1 %reduce-scatter.26.cloned.1.call-start = ((), (), s32[]{:S(2)}) async-start(), calls=%async_computation.20 | async-start | bytes 2048000 | tf_op jit(solution)/shard_map/reduce_scatter | solution.py:484
  1208.1 448.0 %reduce-scatter.22.cloned.1.call-start = ((), (), s32[]{:S(2)}) async-start(), calls=%async_computation.18 | async-start | bytes 4096000 | tf_op jit(solution)/shard_map/reduce_scatter | solution.py:484
  1208.4 110.8 %collective-permute-start.9 = (bf16[256,2560]{1,0:T(8,128)(2,1)}, bf16[256,2560]{1,0:T(8,128)(2,1)}, u32[]{:S(2)}, u32[]{:S(2)}) collective-permute-start(bf16[256,2560]{1,0:T(8,128)(2,1)} %get-tuple-element.142), channel_id=1, source_target_pairs={{0,1},{1,0},{2,3},{3,2},{4,5},{5,4},{6,7},{7,6},{8,9},{9,8},{10,11... | collective-permute-start | bytes 3932168 | tf_op jit(solution)/shard_map/ppermute | solution.py:31
  1228.6 269.4 %collective-permute-start.16 = (f32[256,2560]{1,0:T(8,128)S(1)}, f32[256,2560]{1,0:T(8,128)}, u32[]{:S(2)}, u32[]{:S(2)}) collective-permute-start(f32[256,2560]{1,0:T(8,128)S(1)} %subtract_add_fusion), channel_id=1, source_target_pairs={{0,1},{1,0},{2,3},{3,2},{4,5},{5,4},{6,7},{7,6},{8,9},{9,8},{10,11... | collective-permute-start | bytes 7864328 | tf_op jit(solution)/shard_map/ppermute | solution.py:31
  1492.6 43.4 %collective-permute-start.17 = (bf16[160,3072]{1,0:T(8,128)(2,1)S(1)}, bf16[160,3072]{1,0:T(8,128)(2,1)S(1)}, u32[]{:S(2)}, u32[]{:S(2)}) collective-permute-start(bf16[160,3072]{1,0:T(8,128)(2,1)S(1)} %get-tuple-element.133), channel_id=1, source_target_pairs={{0,2},{2,4},{4,6},{6,0},{1,3},{3,5},{5,7},{7,1},{8,10},{10,12},{12... | collective-permute-start | bytes 2949128 | tf_op jit(solution)/shard_map/ppermute | solution.py:334
  1494.2 92.4 %collective-permute-start.18 = (bf16[160,3072]{1,0:T(8,128)(2,1)S(1)}, bf16[160,3072]{1,0:T(8,128)(2,1)S(1)}, u32[]{:S(2)}, u32[]{:S(2)}) collective-permute-start(bf16[160,3072]{1,0:T(8,128)(2,1)S(1)} %get-tuple-element.132), channel_id=1, source_target_pairs={{0,4},{2,6},{4,0},{6,2},{1,5},{3,7},{5,1},{7,3},{8,12},{10,14},{12... | collective-permute-start | bytes 2949128 | tf_op jit(solution)/shard_map/ppermute | solution.py:334
  1496.6 90.0 %collective-permute-start.19 = (bf16[160,3072]{1,0:T(8,128)(2,1)S(1)}, bf16[160,3072]{1,0:T(8,128)(2,1)S(1)}, u32[]{:S(2)}, u32[]{:S(2)}) collective-permute-start(bf16[160,3072]{1,0:T(8,128)(2,1)S(1)} %get-tuple-element.131), channel_id=1, source_target_pairs={{0,6},{2,0},{4,2},{6,4},{1,7},{3,1},{5,3},{7,5},{8,14},{10,8},{12,... | collective-permute-start | bytes 2949128 | tf_op jit(solution)/shard_map/ppermute | solution.py:334
  (46 other events, 1091.9 us)
Sparse Core Ops, SparseCore 0:
  11.3 231.5 all-gather.6
  246.2 56.1 all-gather.8
  305.2 95.7 all-gather.10
  403.3 146.9 all-gather.14
  552.3 99.3 all-gather.12
  653.3 97.7 all-gather.16
  804.4 107.7 reduce-scatter.17
  914.6 107.7 reduce-scatter.15
  1088.2 27.4 reduce-scatter.27
  1118.6 72.3 reduce-scatter.23
  1194.2 124.9 reduce-scatter.19
  1321.3 20.0 reduce-scatter.29
  1344.5 145.7 reduce-scatter.31
  1492.4 87.1 reduce-scatter.25
  1581.9 74.0 reduce-scatter.21

commit v2 on v1

--- a/solution.py
+++ b/solution.py
@@ -315,6 +315,247 @@
     )(tprod, tsum, leaving, prod, total, state_in, coef, r, i, conv_low, x_branch, halo, masks, params, blocks)
 
 
+TILE = 256
+
+
+def tokens_spec(columns, tiles, first):
+    return pl.BlockSpec((TILE, columns), lambda m: ((m + first) % tiles, 0))
+
+
+def held(rows, columns):
+    return pl.BlockSpec((rows, columns), lambda m: (0, 0), pipeline_mode=pl.Buffered(1))
+
+
+def half_specs(columns, tiles):
+    mid = tiles // 2
+    return [
+        pl.BlockSpec((TILE, columns), lambda m: (jnp.maximum(m - mid, 0), 0)),
+        pl.BlockSpec((TILE, columns), lambda m: (jnp.minimum(m, mid - 1), 0)),
+    ]
+
+
+def store_half(first_ref, second_ref, tiles, value):
+    m = pl.program_id(0)
+
+    @pl.when(m < tiles // 2)
+    def _():
+        second_ref[...] = value
+
+    @pl.when(m >= tiles // 2)
+    def _():
+        first_ref[...] = value
+
+
+def feed_params():
+    return pltpu.CompilerParams(vmem_limit_bytes=56 * 1024 * 1024)
+
+
+def cost(flops, size):
+    return pl.CostEstimate(flops=flops, bytes_accessed=size, transcendentals=0)
+
+
+def forward_tile(x_ref, w_ref, hidden_ref, by_gate_ref, by_up_ref):
+    share = hidden_ref.shape[1]
+    x = x_ref[...]
+    value, slope = gelu_pair(dot(x, w_ref[:, :share], ((1,), (0,))))
+    up = dot(x, w_ref[:, share:], ((1,), (0,)))
+    hidden_ref[...] = (value * up).astype(BF16)
+    by_gate_ref[...] = up * slope
+    by_up_ref[...] = value
+
+
+def feed_forward(x, w_expand):
+    count, width = x.shape
+    share = w_expand.shape[1] // 2
+    tiles = count // TILE
+    tile = tokens_spec(share, tiles, 0)
+    return pl.pallas_call(
+        forward_tile,
+        grid=(tiles,),
+        in_specs=[tokens_spec(width, tiles, 0), held(width, 2 * share)],
+        out_specs=[tile] * 3,
+        out_shape=[
+            jax.ShapeDtypeStruct((count, share), BF16),
+            jax.ShapeDtypeStruct((count, share), F32),
+            jax.ShapeDtypeStruct((count, share), F32),
+        ],
+        compiler_params=feed_params(),
+        cost_estimate=cost(4 * count * width * share, 10 * count * share + 2 * count * width),
+        name="feed_forward",
+    )(x, w_expand)
+
+
+def feed_backward(feed_grad, by_gate, by_up, w_down, w_expand):
+    count, width = feed_grad.shape
+    share = w_down.shape[1]
+    tiles = count // TILE
+    mid = tiles // 2
+
+    def body(fg_ref, gate_ref, up_ref, wd_ref, we_ref, low_ref, first_ref, second_ref):
+        grad = dot(fg_ref[...], wd_ref[...], ((1,), (0,)))
+        gate = (grad * gate_ref[...]).astype(BF16)
+        up = (grad * up_ref[...]).astype(BF16)
+        low_ref[:, :share] = gate
+        low_ref[:, share:] = up
+        terms = dot(gate, we_ref[:, :share], ((1,), (1,))) + dot(up, we_ref[:, share:], ((1,), (1,)))
+        store_half(first_ref, second_ref, tiles, terms.astype(BF16))
+
+    tile = tokens_spec(share, tiles, mid)
+    return pl.pallas_call(
+        body,
+        grid=(tiles,),
+        in_specs=[tokens_spec(width, tiles, mid), tile, tile, held(width, share), held(width, 2 * share)],
+        out_specs=[tokens_spec(2 * share, tiles, mid)] + half_specs(width, tiles),
+        out_shape=[
+            jax.ShapeDtypeStruct((count, 2 * share), BF16),
+            jax.ShapeDtypeStruct((count // 2, width), BF16),
+            jax.ShapeDtypeStruct((count // 2, width), BF16),
+        ],
+        compiler_params=feed_params(),
+        cost_estimate=cost(6 * count * width * share, 12 * count * share + 4 * count * width),
+        name="feed_backward",
+    )(feed_grad, by_gate, by_up, w_down, w_expand)
+
+
+def feed_down(hidden, w_down):
+    count, share = hidden.shape
+    width = w_down.shape[0]
+    tiles = count // TILE
+
+    def body(h_ref, w_ref, first_ref, second_ref):
+        store_half(first_ref, second_ref, tiles, dot(h_ref[...], w_ref[...], ((1,), (1,))).astype(BF16))
+
+    return pl.pallas_call(
+        body,
+        grid=(tiles,),
+        in_specs=[tokens_spec(share, tiles, tiles // 2), held(width, share)],
+        out_specs=half_specs(width, tiles),
+        out_shape=[jax.ShapeDtypeStruct((count // 2, width), BF16)] * 2,
+        compiler_params=feed_params(),
+        cost_estimate=cost(2 * count * width * share, 2 * count * share + 2 * count * width),
+        name="feed_down",
+    )(hidden, w_down)
+
+
+def weight_grad(x, grad):
+    count, width = x.shape
+    columns = grad.shape[1]
+    deep, wide = 512, min(columns, 1024)
+
+    def body(x_ref, g_ref, out_ref):
+        out_ref[...] = dot(x_ref[...], g_ref[...], ((0,), (0,))).astype(BF16)
+
+    return pl.pallas_call(
+        body,
+        grid=(columns // wide, width // deep),
+        in_specs=[
+            pl.BlockSpec((count, deep), lambda n, m: (0, m)),
+            pl.BlockSpec((count, wide), lambda n, m: (0, n)),
+        ],
+        out_specs=pl.BlockSpec((deep, wide), lambda n, m: (m, n)),
+        out_shape=jax.ShapeDtypeStruct((width, columns), BF16),
+        compiler_params=feed_params(),
+        cost_estimate=cost(2 * count * width * columns, 2 * (count * width + count * columns + width * columns)),
+        name="weight_grad",
+    )(x, grad)
+
+
+def cross(x, axis, r):
+    return lax.ppermute(x, axis, [(i, i ^ r) for i in range(lax.axis_size(axis))])
+
+
+def total_over(x, axis):
+    r = 1
+    while r < lax.axis_size(axis):
+        x = x + cross(x, axis, r)
+        r *= 2
+    return x
+
+
+def after(x, done):
+    return lax.optimization_barrier((x, done))
+
+
+SQUARE = 4
+
+
+def token_axes():
+    return ("fsdp", "ctx") if lax.axis_size("fsdp") == SQUARE else ("ctx", "fsdp")
+
+
+def place(blocks, axis):
+    me = lax.axis_index(axis)
+    whole = jnp.zeros((len(blocks),) + blocks[0].shape, blocks[0].dtype)
+    for r, block in enumerate(blocks):
+        whole = lax.dynamic_update_index_in_dim(whole, block, me ^ r, 0)
+    return whole
+
+
+def near(x, axis):
+    mid = x.shape[0] // 2
+    one, two = cross(x, axis, 1), cross(x, axis, 2)
+    three = jnp.concatenate([cross(one[:mid], axis, 2), cross(two[mid:], axis, 1)], axis=0)
+    return [x, one, two, three]
+
+
+def near_sum(block, axis):
+    low = lambda v: v.astype(BF16)
+    wide = lambda v: v.astype(F32)
+    a1, a3 = cross(low(block(1, 0)), axis, 1), cross(low(block(3, 0)), axis, 1)
+    b2, b3 = cross(low(block(2, 1)), axis, 2), cross(low(block(3, 1)), axis, 2)
+    a2 = cross(low(wide(block(2, 0)) + wide(a3)), axis, 2)
+    b1 = cross(low(wide(block(1, 1)) + wide(b3)), axis, 1)
+    left = wide(block(0, 0)) + wide(a1) + wide(a2)
+    right = wide(block(0, 1)) + wide(b2) + wide(b1)
+    return jnp.concatenate([left, right], axis=1)
+
+
+def gather_rows(x):
+    if lax.axis_size("fsdp") != SQUARE:
+        return lax.all_gather(x, "fsdp", axis=0, tiled=True)
+    return place(near(x, "fsdp"), "fsdp").reshape(SQUARE * x.shape[0], x.shape[1])
+
+
+def scatter_rows(x):
+    if lax.axis_size("fsdp") != SQUARE:
+        return lax.psum_scatter(x, "fsdp", scatter_dimension=0, tiled=True).astype(F32)
+    me, rows, cols = lax.axis_index("fsdp"), x.shape[0] // SQUARE, x.shape[1] // 2
+    return near_sum(lambda r, h: lax.dynamic_slice(x, ((me ^ r) * rows, h * cols), (rows, cols)), "fsdp")
+
+
+def gather_tokens(x):
+    blocks = near(x, token_axes()[0])
+    return jnp.concatenate(blocks + [swap(block, "tp") for block in blocks], axis=0)
+
+
+def scatter_tokens(first, second):
+    theirs = swap(second, "tp")
+    mine = (first.astype(F32) + theirs.astype(F32)).astype(BF16)
+    rows, cols = mine.shape[0] // SQUARE, mine.shape[1] // 2
+    return near_sum(lambda r, h: mine[r * rows : (r + 1) * rows, h * cols : (h + 1) * cols], token_axes()[0])
+
+
+def trade(pieces):
+    axis = token_axes()[0]
+    me = lax.axis_index(axis)
+    return place([pieces(me)] + [cross(pieces(me ^ r), axis, r) for r in range(1, SQUARE)], axis)
+
+
+def gather_feed(local):
+    _, along = token_axes()
+    whole = lax.all_gather(local, along, axis=1 if along == "ctx" else 0, tiled=True)
+    return whole.reshape(-1, local.shape[2])
+
+
+def scatter_feed(grad):
+    _, along = token_axes()
+    if along == "ctx":
+        grad = grad.reshape(SQUARE, -1, grad.shape[1])
+        return lax.psum_scatter(grad, along, scatter_dimension=1, tiled=True)
+    part = lax.psum_scatter(grad, along, scatter_dimension=0, tiled=True)
+    return part.reshape(SQUARE, -1, grad.shape[1])
+
+
 def rms(values):
     return lax.rsqrt(jnp.mean(values * values, axis=-1, keepdims=True) + EPSILON)
 
@@ -324,17 +565,6 @@
     inner = jnp.mean(values * u, axis=-1, keepdims=True)
     gain_grad = jnp.sum(grad * values * inverse, axis=0)
     return inverse * u - values * (inverse * inverse * inverse) * inner, gain_grad
-
-
-def exchange_units(x, axis):
-    length, me = lax.axis_size(axis), lax.axis_index(axis)
-    got = [lax.dynamic_index_in_dim(x, me, 0, keepdims=False)]
-    for by in range(1, length):
-        piece = lax.dynamic_index_in_dim(x, (me + by) % length, 0, keepdims=False)
-        got.append(lax.ppermute(piece, axis, [(s, (s + by) % length) for s in range(length)]))
-    stacked = jnp.stack(got)
-    order = (me - jnp.arange(length)) % length
-    return jnp.take(stacked, order, axis=0)
 
 
 def shards(
@@ -344,13 +574,14 @@
     rows, length, width = block_input.shape
     depth = intake.shape[0]
     units = intake.shape[2]
+    gate_rows = gate_blocks.shape[0]
     hidden_units = contract.shape[1]
     tokens = rows * length
     ctx, tp = lax.axis_size("ctx"), lax.axis_size("tp")
     mine = lax.axis_index("tp")
     half = tokens // tp
-    share = -(-hidden_units // (ctx * 256)) * 256
-    padding = ctx * share - hidden_units
+    share = -(-hidden_units // (SQUARE * 256)) * 256
+    padding = SQUARE * share - hidden_units
 
     def own(x):
         return lax.dynamic_slice_in_dim(x, mine * half, half, 0)
@@ -364,20 +595,37 @@
             [jnp.where(mine == 0, x, theirs), jnp.where(mine == 0, theirs, x)], axis=0
         )
 
-    w_intake = lax.all_gather(intake.reshape(depth, 2 * units), ("fsdp", "ctx"), axis=0, tiled=True)
-    w_gates = lax.all_gather(gate_blocks, ("fsdp", "ctx"), axis=0, tiled=True)
-    w_outlet = lax.all_gather(outlet, ("fsdp", "ctx"), axis=0, tiled=True)
-
-    feed_in = jnp.concatenate([expand, contract[:, None, :]], axis=1)
-    feed_in = jnp.pad(feed_in, ((0, 0), (0, 0), (0, padding)))
-    feed_in = feed_in.reshape(depth, 3, ctx, share).transpose(2, 0, 1, 3).reshape(ctx, depth, 3 * share)
-    feed_in = exchange_units(feed_in, "ctx").reshape(ctx * depth, 3 * share)
-    w_feed = lax.all_gather(feed_in, "fsdp", axis=0, tiled=True)
-    w_expand, w_contract = w_feed[:, : 2 * share], w_feed[:, 2 * share :]
+    packed = jnp.concatenate(
+        [intake[:, 1], intake[:, 0], outlet, gate_blocks.reshape(2 * gate_rows, units)], axis=0
+    )
+    packed = lax.all_gather(packed, "ctx", axis=0)
+
+    def part(n, count):
+        return packed[:, n * depth : n * depth + count].reshape(ctx * count, units)
+
+    def cut(w):
+        w = jnp.pad(w, ((0, 0), (0, padding)))
+        return lambda p: lax.dynamic_slice_in_dim(w, p * share, share, 1)
+
+    down, gate_in, up_in = cut(contract), cut(expand[:, 0]), cut(expand[:, 1])
+    w_expand = trade(lambda p: jnp.concatenate([gate_in(p), up_in(p)], axis=1))
+    w_expand = gather_feed(w_expand)
+    local_down = trade(down)
 
     mask_rows = token_mask.astype(F32).reshape(tokens, 1)
     out_grad = own(cotangent.reshape(tokens, width)).astype(F32) * own(mask_rows)
-    feed_grad = lax.all_gather(out_grad.astype(BF16), ("ctx", "tp"), axis=0, tiled=True)
+    feed_grad = gather_tokens(out_grad.astype(BF16))
+
+    local_branch, local_down, feed_grad = lax.optimization_barrier((part(0, depth), local_down, feed_grad))
+    w_down = gather_feed(local_down)
+    w_branch = gather_rows(local_branch)
+    local_gates, w_branch = after(part(3, 2 * gate_rows), w_branch)
+    w_gates = gather_rows(local_gates)
+    local_gelu, w_gates = after(part(1, depth), w_gates)
+    blocks = w_gates.reshape(HEAD_W, 2, units).transpose(1, 0, 2)
+    w_gelu = gather_rows(local_gelu)
+    local_outlet, w_gelu = after(part(2, depth), w_gelu)
+    w_outlet = gather_rows(local_outlet)
 
     seg_next = segments + 1
     seg_before = shifted(seg_next[:, -3:], "ctx", 1)
@@ -402,11 +650,10 @@
     x = block_input.reshape(tokens, width).astype(F32)
     inverse_one = rms(x)
     normed = (x * inverse_one * norm_gains[0]).astype(BF16)
-    x_branch = dot(normed, w_intake[:, units:], ((1,), (0,))).astype(BF16).reshape(rows, length, units)
-    gelu_in = dot(normed, w_intake[:, :units], ((1,), (0,))).reshape(rows, length, units)
+    x_branch = dot(normed, w_branch, ((1,), (0,))).astype(BF16).reshape(rows, length, units)
+    gelu_in = dot(normed, w_gelu, ((1,), (0,))).reshape(rows, length, units)
     x_before = shifted(x_branch[:, -3:], "ctx", 1)
     halo = jnp.pad(x_before, ((0, 0), (5, 0), (0, 0))).astype(F32)
-    blocks = w_gates.transpose(1, 0, 2)
     conv_low, r, i, coef, prod, total = recurrent_forward(x_branch, halo, masks, params, blocks)
     ends = jnp.stack([prod[:, -1], total[:, -1]])
     entering = jnp.zeros((rows, units), F32)
@@ -421,41 +668,28 @@
     branch = dot(own(recurrent), w_outlet, ((1,), (1,))) + sent
     residual = own(x) + branch
     inverse_two = rms(residual)
-    normed_two = lax.all_gather(
-        (residual * inverse_two * norm_gains[1]).astype(BF16), ("ctx", "tp"), axis=0, tiled=True
+    normed_two = gather_tokens((residual * inverse_two * norm_gains[1]).astype(BF16))
+
+    def to_owners(part):
+        return trade(lambda p: lax.dynamic_index_in_dim(part, p, 0, keepdims=False))
+
+    hidden, by_gate, by_up = feed_forward(normed_two, w_expand)
+    down_part = scatter_feed(weight_grad(feed_grad, hidden))
+    low, n2g_own, n2g_other = feed_backward(feed_grad, by_gate, by_up, w_down, w_expand)
+    normed_two_grad = scatter_tokens(n2g_own, n2g_other)
+    expand_all = weight_grad(normed_two, low)
+    feed_own, feed_other = feed_down(hidden, w_down)
+    normed_two_grad, expand_all, feed_own, feed_other = lax.optimization_barrier(
+        (normed_two_grad, expand_all, feed_own, feed_other)
     )
-
-    expanded = dot(normed_two, w_expand, ((1,), (0,)))
-    gate, up = expanded[:, :share], expanded[:, share:]
-    value, slope = gelu_pair(gate)
-    hidden = (value * up).astype(BF16)
-    hidden_grad = dot(feed_grad, w_contract, ((1,), (0,)))
-    expand_low = jnp.concatenate(
-        [(hidden_grad * up * slope).astype(BF16), (hidden_grad * value).astype(BF16)], axis=1
-    )
-    normed_two_grad = lax.psum_scatter(
-        dot(expand_low, w_expand, ((1,), (1,))).astype(BF16), ("ctx", "tp"), scatter_dimension=0, tiled=True
-    ).astype(F32)
-    feed_out = lax.psum_scatter(
-        dot(hidden, w_contract, ((1,), (1,))).astype(BF16), ("ctx", "tp"), scatter_dimension=0, tiled=True
-    ).astype(F32)
+    expand_part = scatter_feed(expand_all)
+    feed_out = scatter_tokens(feed_own, feed_other)
     block_output = join((residual + feed_out).astype(BF16)).reshape(rows, length, width)
-
-    feed_weight_grad = jnp.concatenate(
-        [
-            dot(normed_two, expand_low, ((0,), (0,))).astype(BF16),
-            dot(feed_grad, hidden, ((0,), (0,))).astype(BF16),
-        ],
-        axis=1,
-    )
-    feed_part = lax.psum_scatter(feed_weight_grad, "fsdp", scatter_dimension=0, tiled=True)
-    feed_part = exchange_units(feed_part.reshape(ctx, depth, 3 * share), "ctx")
-    feed_part = feed_part.reshape(ctx, depth, 3, share).transpose(1, 2, 0, 3).reshape(depth, 3, ctx * share)
-    feed_part = feed_part[:, :, :hidden_units].astype(F32)
 
     norm_part, gain_two = rms_back(residual, inverse_two, norm_gains[1], normed_two_grad)
     residual_grad = out_grad + norm_part
     branch_grad = join(residual_grad.astype(BF16))
+
     outlet_grad = dot(branch_grad, recurrent, ((0,), (0,))).astype(BF16)
     rec_grad = dot(branch_grad, w_outlet, ((1,), (0,))).reshape(rows, length, units)
     gelu_grad, tprod, tsum = recurrent_adjoint(rec_grad, gelu_in, coef, prod, total, state_in)
@@ -470,26 +704,45 @@
     )
     from_next = shifted(before[:, 5:], "ctx", -1)
     branch_x = branch_x + jnp.pad(from_next, ((0, 0), (length - 3, 0), (0, 0)))
-    intake_low = jnp.concatenate([gelu_grad, branch_x.astype(BF16)], axis=2).reshape(tokens, 2 * units)
-
-    sent = swap(dot(other(intake_low), w_intake, ((1,), (1,))), "tp")
-    normed_grad = dot(own(intake_low), w_intake, ((1,), (1,))) + sent
+    gelu_low = gelu_grad.reshape(tokens, units)
+    branch_low = branch_x.astype(BF16).reshape(tokens, units)
+
+    def input_terms(pick):
+        return dot(pick(branch_low), w_branch, ((1,), (1,))) + dot(pick(gelu_low), w_gelu, ((1,), (1,)))
+
+    gelu_part = scatter_rows(dot(normed, gelu_low, ((0,), (0,))).astype(BF16)).astype(BF16)
+    outlet_part = scatter_rows(outlet_grad).astype(BF16)
+    branch_part = scatter_rows(dot(normed, branch_low, ((0,), (0,))).astype(BF16)).astype(BF16)
+    blocks_part = scatter_rows(blocks_grad.transpose(1, 0, 2).reshape(2 * HEAD_W, units)).astype(BF16)
+
+    def scatter_ctx(parts):
+        parts = jnp.concatenate([p.reshape(ctx, -1, units) for p in parts], axis=1)
+        return lax.psum_scatter(parts, "ctx", scatter_dimension=0, tiled=False).astype(F32)
+
+    gelu_part, expand_part = after(gelu_part, expand_part)
+    early = scatter_ctx([gelu_part, outlet_part])
+    branch_part, early = after(branch_part, early)
+    late = scatter_ctx([branch_part, blocks_part])
+
+    down_part = to_owners(down_part)
+    expand_part = to_owners(expand_part)
+
+    def columns(part, n):
+        return jnp.concatenate([part[p, :, n * share : (n + 1) * share] for p in range(SQUARE)], axis=1)[
+            :, :hidden_units
+        ].astype(F32)
+
+    contract_grad = columns(down_part, 0)
+    expand_grad = jnp.stack([columns(expand_part, 0), columns(expand_part, 1)], axis=1)
+
+    sent = swap(input_terms(other), "tp")
+    normed_grad = input_terms(own) + sent
     norm_part, gain_one = rms_back(own(x), own(inverse_one), norm_gains[0], normed_grad)
     input_grad = join(residual_grad + norm_part).reshape(rows, length, width)
 
-    intake_grad = dot(normed, intake_low, ((0,), (0,))).astype(BF16)
-
-    def scatter(grad):
-        part = lax.psum_scatter(grad, "fsdp", scatter_dimension=0, tiled=True)
-        return lax.psum_scatter(part, "ctx", scatter_dimension=0, tiled=True).astype(F32)
-
-    outlet_part = scatter(outlet_grad)
-    blocks_part = scatter(blocks_grad.transpose(1, 0, 2).reshape(HEAD_W, 2 * units)).reshape(-1, 2, units)
-    intake_part = scatter(intake_grad).reshape(depth, 2, units)
-
-    gains = jnp.stack([gain_one, gain_two])
-    gains, small = lax.psum((gains, small), ("fsdp", "ctx"))
-    gains = lax.psum(gains, "tp")
+    gains = jnp.concatenate([gain_one, gain_two]).reshape(-1, units)
+    small = total_over(total_over(jnp.concatenate([small, gains], axis=0), "fsdp"), "ctx")
+    gains = total_over(small[8:], "tp").reshape(2, width)
     return (
         block_output,
         input_grad,
@@ -498,11 +751,11 @@
         small[4],
         small[5:7],
         small[7],
-        intake_part,
-        blocks_part,
-        outlet_part,
-        feed_part[:, :2],
-        feed_part[:, 2],
+        jnp.stack([early[:depth], late[:depth]], axis=1),
+        late[depth:].reshape(gate_rows, 2, units),
+        early[depth:],
+        expand_grad,
+        contract_grad,
     )
 
 

time: 1690 us -> 1010 us (0.60); the launches traced: 1670 us -> 1010 us
  waiting for transfers between devices: 985 us -> 423 us
  matrix products: 226 us -> 59 us
  Pallas kernels: 42.8 us -> 180 us
  blocking collectives: 81.5 us -> 0 us
    all_gather x6 -> x3, waiting for transfers between devices: 403 us -> 6.22 us  [the longest x2 6.22 us: gather_feed(): lax.all_gather(local, along, axis=1 if along == 'ctx' else 0, tiled=True)]
    reduce_scatter x7 -> x4, waiting for transfers between devices: 386 us -> 5.53 us  [the longest x2 5.49 us: scatter_ctx(): lax.psum_scatter(parts, 'ctx', scatter_dimension=0, tiled=False).astype(F32)]
    ppermute x6 -> x77, waiting for transfers between devices: 174 us -> 394 us  [cross(): lax.ppermute(x, axis, [(i, i ^ r) for i in range(lax.axis_size(axis))])]
    dot_general x15 -> x12, matrix products: 226 us -> 59 us  [dot(): return lax.dot_general(a, b, (dims, ((), ())), preferred_element_type=F32)]
    pallas_call x0 -> x5, Pallas kernels: none -> 137 us  [the longest x1 44.8 us: feed_backward(): pl.pallas_call(body, grid=(tiles,), in_specs=[tokens_spec(width, tiles, m...]
    psum x2 -> x0, blocking collectives: 81.5 us -> none  [the longest x1 77.5 us: shards(): gains, small = lax.psum((gains, small), ('fsdp', 'ctx'))]
    ppermute x6 -> x77, starting transfers between devices: 12.3 us -> 83.2 us  [cross(): lax.ppermute(x, axis, [(i, i ^ r) for i in range(lax.axis_size(axis))])]
    ppermute x9, starting transfers between devices: 91.8 us -> 24.1 us  [shifted(): return lax.ppermute(x, axis, pairs)]
  transfers between devices with their start and end apart: 35 -> 108, of which waited for: 23 -> 48; matrix products, arithmetic and copies ran while one was open for 21% -> 25% of each run, Pallas kernels for 1% -> 13%
where the time goes in v2:
time: 1010 us
  waiting for transfers between devices  423 us (42%)
  Pallas kernels  180 us (18%)
  local copies, waits for them, and re-layouts  130 us (13%)
  starting transfers between devices  110 us (11%)
  other arithmetic  90.4 us (9%)
  matrix products  59 us (6%)
  between operations  16.1 us (2%)
    ppermute x77, waiting for transfers between devices, cross(): lax.ppermute(x, axis, [(i, i ^ r) for i in range(lax.axis_size(axis))])  394 us
    ppermute x77, starting transfers between devices, cross(): lax.ppermute(x, axis, [(i, i ^ r) for i in range(lax.axis_size(axis))])  83.2 us
    dot_general x12, matrix products, dot(): return lax.dot_general(a, b, (dims, ((), ())), preferred_element_type=F32)  59 us
    unnamed x167, local copies, waits for them, and re-layouts  45.3 us
    pallas_call x1, Pallas kernels, feed_backward(): pl.pallas_call(body, grid=(tiles,), in_specs=[tokens_spec(width, tiles, m...  44.8 us
    pallas_call x2, Pallas kernels, weight_grad(): pl.pallas_call(body, grid=(columns // wide, width // deep), in_specs=[pl....  44.2 us
    pallas_call x1, Pallas kernels, feed_forward(): pl.pallas_call(forward_tile, grid=(tiles,), in_specs=[tokens_spec(width,...  30.3 us
    ppermute x9, starting transfers between devices, shifted(): return lax.ppermute(x, axis, pairs)  24.1 us
  transfers between devices with their start and end apart: 108, of which 48 were waited for; matrix products, arithmetic and copies ran while one was open for 25% of the time, Pallas kernels for 13%

profile of v2, /device:TPU:0, one launch (start us, length us, event | category | flops | bytes accessed | tf_op | source)
XLA Modules:
  0.0 1007.4 jit_solution(17141365859789862882)
XLA Ops:
  35.0 21.1 %collective-permute-done = bf16[160,1024]{1,0:T(8,128)(2,1)} collective-permute-done((bf16[160,1024]{1,0:T(8,128)(2,1)}, bf16[160,1024]{1,0:T(8,128)(2,1)}, u32[]{:S(2)}, u32[]{:S(2)}) %collective-permute-start) | collective-permute-done | bytes 327712 | tf_op jit(solution)/shard_map/ppermute | solution.py:464
  80.2 16.6 %collective-permute-done.42 = bf16[160,2048]{1,0:T(8,128)(2,1)} collective-permute-done((bf16[160,2048]{1,0:T(8,128)(2,1)}, bf16[160,2048]{1,0:T(8,128)(2,1)}, u32[]{:S(2)}, u32[]{:S(2)}) %collective-permute-start.42) | collective-permute-done | bytes 655392 | tf_op jit(solution)/shard_map/ppermute | solution.py:464
  142.6 32.4 %collective-permute-done.12 = bf16[640,1280]{1,0:T(8,128)(2,1)} collective-permute-done((bf16[640,1280]{1,0:T(8,128)(2,1)}, bf16[640,1280]{1,0:T(8,128)(2,1)}, u32[]{:S(2)}, u32[]{:S(2)}) %collective-permute-start.12) | collective-permute-done | bytes 1638432 | tf_op jit(solution)/shard_map/ppermute | solution.py:464
  183.0 12.9 %collective-permute-done.14 = bf16[320,1280]{1,0:T(8,128)(2,1)S(1)} collective-permute-done((bf16[320,1280]{1,0:T(8,128)(2,1)S(1)}, bf16[320,1280]{1,0:T(8,128)(2,1)S(1)}, u32[]{:S(2)}, u32[]{:S(2)}) %collective-permute-start.14) | collective-permute-done | bytes 819232 | tf_op jit(solution)/shard_map/ppermute | solution.py:464
  221.8 15.7 %recurrent_forward.1 = (bf16[2,256,1280]{2,1,0:T(8,128)(2,1)S(1)}, f32[2,256,1280]{2,1,0:T(8,128)}, f32[2,256,1280]{2,1,0:T(8,128)}, f32[2,256,1280]{2,1,0:T(8,1...) custom-call(bf16[2,256,1280]{2,1,0:T(8,128)(2,1)S(1)} %bitcast.224, f32[2,8,1280]{2,1,0:T(8,128)S(1)} %pad_convert_fusion.halo_ref, ...), custom_call_target="tpu_custom_call" | custom-call | flops 671088640 | bytes 15728640 | tf_op jit(solution)/shard_map/recurrent_forward/pallas_call | solution.py:153
  260.6 12.1 %collective-permute-done.27 = bf16[320,1280]{1,0:T(8,128)(2,1)S(1)} collective-permute-done((bf16[320,1280]{1,0:T(8,128)(2,1)S(1)}, bf16[320,1280]{1,0:T(8,128)(2,1)S(1)}, u32[]{:S(2)}, u32[]{:S(2)}) %collective-permute-start.27) | collective-permute-done | bytes 819232 | tf_op jit(solution)/shard_map/ppermute | solution.py:464
  285.8 25.8 %collective-permute-done.29 = bf16[640,1280]{1,0:T(8,128)(2,1)S(1)} collective-permute-done((bf16[640,1280]{1,0:T(8,128)(2,1)S(1)}, bf16[640,1280]{1,0:T(8,128)(2,1)S(1)}, u32[]{:S(2)}, u32[]{:S(2)}) %collective-permute-start.29) | collective-permute-done | bytes 1638432 | tf_op jit(solution)/shard_map/ppermute | solution.py:464
  312.8 13.9 %collective-permute-done.31 = bf16[320,1280]{1,0:T(8,128)(2,1)S(1)} collective-permute-done((bf16[320,1280]{1,0:T(8,128)(2,1)S(1)}, bf16[320,1280]{1,0:T(8,128)(2,1)S(1)}, u32[]{:S(2)}, u32[]{:S(2)}) %collective-permute-start.31) | collective-permute-done | bytes 819232 | tf_op jit(solution)/shard_map/ppermute | solution.py:464
  346.7 29.8 %collective-permute-done.33 = bf16[256,2560]{1,0:T(8,128)(2,1)S(1)} collective-permute-done((bf16[256,2560]{1,0:T(8,128)(2,1)S(1)}, bf16[256,2560]{1,0:T(8,128)(2,1)S(1)}, u32[]{:S(2)}, u32[]{:S(2)}) %collective-permute-start.33) | collective-permute-done | bytes 1310752 | tf_op jit(solution)/shard_map/ppermute | solution.py:464
  381.2 11.4 %collective-permute-done.35 = bf16[128,2560]{1,0:T(8,128)(2,1)S(1)} collective-permute-done((bf16[128,2560]{1,0:T(8,128)(2,1)S(1)}, bf16[128,2560]{1,0:T(8,128)(2,1)S(1)}, u32[]{:S(2)}, u32[]{:S(2)}) %collective-permute-start.35) | collective-permute-done | bytes 655392 | tf_op jit(solution)/shard_map/ppermute | solution.py:464
  399.6 30.3 %feed_forward.1 = (bf16[2048,1024]{1,0:T(8,128)(2,1)}, f32[2048,1024]{1,0:T(8,128)}, f32[2048,1024]{1,0:T(8,128)}) custom-call(bf16[2048,2560]{1,0:T(8,128)(2,1)} %constant_dynamic-update-slice_fusion.9.x_ref, bf16[2560,2048]{1,0:T(8,128)(2,1)} %bitcast.286), custom_call_target="tpu_custom_call" | custom-call | flops 21474836480 | bytes 31457280 | tf_op jit(solution)/shard_map/feed_forward/pallas_call | solution.py:372
  436.1 44.8 %feed_backward.1 = (bf16[2048,2048]{1,0:T(8,128)(2,1)}, bf16[1024,2560]{1,0:T(8,128)(2,1)}, bf16[1024,2560]{1,0:T(8,128)(2,1)}) custom-call(bf16[2048,2560]{1,0:T(8,128)(2,1)} %constant_dynamic-update-slice_fusion.fg_ref.x_ref, f32[2048,1024]{1,0:T(8,128)} %get-tuple-element.60.gate_ref, f32[2048,1024]{1,0:T(8,128)} %get-tuple-element.61.up_ref, ...), custom_call_target="tpu_custom_call" | custom-call | flops 32212254720 | bytes 46137344 | tf_op jit(solution)/shard_map/feed_backward/pallas_call | solution.py:404
  480.8 15.7 %weight_grad.3 = bf16[2560,1024]{1,0:T(8,128)(2,1)} custom-call(bf16[2048,2560]{1,0:T(8,128)(2,1)} %constant_dynamic-update-slice_fusion.fg_ref.x_ref, bf16[2048,1024]{1,0:T(8,128)(2,1)} %get-tuple-element.66.h_ref.g_ref), custom_call_target="tpu_custom_call" | custom-call | flops 10737418240 | bytes 19922944 | tf_op jit(solution)/shard_map/weight_grad/pallas_call | solution.py:448
  506.1 14.0 %collective-permute-done.46 = bf16[256,1280]{1,0:T(8,128)(2,1)S(1)} collective-permute-done((bf16[256,1280]{1,0:T(8,128)(2,1)S(1)}, bf16[256,1280]{1,0:T(8,128)(2,1)S(1)}, u32[]{:S(2)}, u32[]{:S(2)}) %collective-permute-start.46) | collective-permute-done | bytes 655392 | tf_op jit(solution)/shard_map/ppermute | solution.py:464
  521.8 28.5 %weight_grad.2 = bf16[2560,2048]{1,0:T(8,128)(2,1)} custom-call(bf16[2048,2560]{1,0:T(8,128)(2,1)} %constant_dynamic-update-slice_fusion.9.x_ref, bf16[2048,2048]{1,0:T(8,128)(2,1)} %get-tuple-element.65.g_ref), custom_call_target="tpu_custom_call" | custom-call | flops 21474836480 | bytes 29360128 | tf_op jit(solution)/shard_map/weight_grad/pallas_call | solution.py:448
  554.1 17.9 %feed_down.1 = (bf16[1024,2560]{1,0:T(8,128)(2,1)}, bf16[1024,2560]{1,0:T(8,128)(2,1)}) custom-call(bf16[2048,1024]{1,0:T(8,128)(2,1)} %get-tuple-element.66.h_ref.g_ref, bf16[2560,1024]{1,0:T(8,128)(2,1)} %bitcast.289), custom_call_target="tpu_custom_call" | custom-call | flops 10737418240 | bytes 14680064 | tf_op jit(solution)/shard_map/feed_down/pallas_call | solution.py:428
  594.7 14.1 %collective-permute-done.53 = bf16[256,1280]{1,0:T(8,128)(2,1)S(1)} collective-permute-done((bf16[256,1280]{1,0:T(8,128)(2,1)S(1)}, bf16[256,1280]{1,0:T(8,128)(2,1)S(1)}, u32[]{:S(2)}, u32[]{:S(2)}) %collective-permute-start.53) | collective-permute-done | bytes 655392 | tf_op jit(solution)/shard_map/ppermute | solution.py:464
  668.5 13.5 %recurrent_adjoint.1 = (bf16[2,256,1280]{2,1,0:T(8,128)(2,1)S(1)}, f32[2,256,1280]{2,1,0:T(8,128)S(1)}, f32[2,256,1280]{2,1,0:T(8,128)}) custom-call(f32[2,256,1280]{2,1,0:T(8,128)} %fusion.68.rg_ref, f32[2,256,1280]{2,1,0:T(8,128)} %get-tuple-element.274.gelu_ref, f32[2,256,1280]{2,1,0:T(8,128)} %get-tuple-element.72.a_ref, ...), custom_call_target="tpu_custom_call" | custom-call | flops 19660800 | bytes 20971520 | tf_op jit(solution)/shard_map/recurrent_adjoint/pallas_call | solution.py:199
  712.2 13.4 %recurrent_backward.1 = (f32[2,256,1280]{2,1,0:T(8,128)}, f32[2,8,1280]{2,1,0:T(8,128)S(1)}, f32[8,1280]{1,0:T(8,128)S(1)}, bf16[2,256,1280]{2,1,0:T(8,128)(2,1)S(1)}) custom-call(f32[2,256,1280]{2,1,0:T(8,128)} %copy-done.2, f32[2,256,1280]{2,1,0:T(8,128)} %get-tuple-element.74.tsum_ref, f32[2,8,1280]{2,1,0:T(8,128)S(1)} %broadcast_in_dim.158.leave_ref, ...), custom_call_target="tpu_custom_call" | custom-call | flops 1342177280 | bytes 26214400 | tf_op jit(solution)/shard_map/recurrent_backward/pallas_call | solution.py:282
  760.9 21.4 %collective-permute-done.85 = bf16[640,640]{1,0:T(8,128)(2,1)S(1)} collective-permute-done((bf16[640,640]{1,0:T(8,128)(2,1)S(1)}, bf16[640,640]{1,0:T(8,128)(2,1)S(1)}, u32[]{:S(2)}, u32[]{:S(2)}) %collective-permute-start.85) | collective-permute-done | bytes 819232 | tf_op jit(solution)/shard_map/ppermute | solution.py:464
  788.1 11.8 %collective-permute-done.79 = bf16[640,640]{0,1:T(8,128)(2,1)S(1)} collective-permute-done((bf16[640,640]{0,1:T(8,128)(2,1)S(1)}, bf16[640,640]{0,1:T(8,128)(2,1)S(1)}, u32[]{:S(2)}, u32[]{:S(2)}) %collective-permute-start.79) | collective-permute-done | bytes 819232 | tf_op jit(solution)/shard_map/ppermute | solution.py:464
  875.1 14.0 %collective-permute-done.73 = bf16[640,640]{0,1:T(8,128)(2,1)S(1)} collective-permute-done((bf16[640,640]{0,1:T(8,128)(2,1)S(1)}, bf16[640,640]{0,1:T(8,128)(2,1)S(1)}, u32[]{:S(2)}, u32[]{:S(2)}) %collective-permute-start.73) | collective-permute-done | bytes 819232 | tf_op jit(solution)/shard_map/ppermute | solution.py:464
  896.6 18.4 %collective-permute-done.66 = f32[12,1280]{1,0:T(8,128)S(1)} collective-permute-done((f32[12,1280]{1,0:T(8,128)S(1)}, f32[12,1280]{1,0:T(8,128)S(1)}, u32[]{:S(2)}, u32[]{:S(2)}) %collective-permute-start.66) | collective-permute-done | bytes 61472 | tf_op jit(solution)/shard_map/ppermute | solution.py:464
  964.0 13.2 %collective-permute-done.96 = bf16[160,2048]{1,0:T(8,128)(2,1)} collective-permute-done((bf16[160,2048]{1,0:T(8,128)(2,1)}, bf16[160,2048]{1,0:T(8,128)(2,1)}, u32[]{:S(2)}, u32[]{:S(2)}) %collective-permute-start.96) | collective-permute-done | bytes 655392 | tf_op jit(solution)/shard_map/ppermute | solution.py:464
  (567 shorter events, 528.7 us)
Async XLA Ops:
  7.2 124.2 %all-gather.9.cloned.1.call-start = ((), (), s32[]{:S(2)}) async-start(), calls=%async_computation.10 | async-start | bytes 6553600 | tf_op jit(solution)/shard_map/all_gather | solution.py:601
  12.3 387.3 %all-gather.5.cloned.1.call-start = ((), (), s32[]{:S(2)}) async-start(), calls=%async_computation.4 | async-start | bytes 13107200 | tf_op jit(solution)/shard_map/all_gather | solution.py:546
  16.2 87.1 %collective-permute-start.3 = (bf16[256,2560]{1,0:T(8,128)(2,1)}, bf16[256,2560]{1,0:T(8,128)(2,1)}, u32[]{:S(2)}, u32[]{:S(2)}) collective-permute-start(bf16[256,2560]{1,0:T(8,128)(2,1)} %get-tuple-element.175), channel_id=1, source_target_pairs={{0,8},{8,0},{16,24},{24,16},{1,9},{9,1},{17,25},{25,17},{2,10},{10... | collective-permute-start | bytes 3932168 | tf_op jit(solution)/shard_map/ppermute | solution.py:464
  19.2 87.2 %collective-permute-start.4 = (bf16[256,2560]{1,0:T(8,128)(2,1)}, bf16[256,2560]{1,0:T(8,128)(2,1)}, u32[]{:S(2)}, u32[]{:S(2)}) collective-permute-start(bf16[256,2560]{1,0:T(8,128)(2,1)} %get-tuple-element.175), channel_id=1, source_target_pairs={{0,16},{8,24},{16,0},{24,8},{1,17},{9,25},{17,1},{25,9},{2,18},{10... | collective-permute-start | bytes 3932168 | tf_op jit(solution)/shard_map/ppermute | solution.py:464
  62.8 62.4 %collective-permute-start.7 = (bf16[256,2560]{1,0:T(8,128)(2,1)}, bf16[256,2560]{1,0:T(8,128)(2,1)}, u32[]{:S(2)}, u32[]{:S(2)}) collective-permute-start(bf16[256,2560]{1,0:T(8,128)(2,1)} %get-tuple-element.175), channel_id=1, source_target_pairs={{0,1},{1,0},{2,3},{3,2},{4,5},{5,4},{6,7},{7,6},{8,9},{9,8},{10,11... | collective-permute-start | bytes 3932168 | tf_op jit(solution)/shard_map/ppermute | solution.py:31
  103.0 333.0 %all-gather.7.cloned.1.call-start = ((), (), s32[]{:S(2)}) async-start(), calls=%async_computation.5 | async-start | bytes 6553600 | tf_op jit(solution)/shard_map/all_gather | solution.py:546
  334.8 298.0 %reduce-scatter.11.cloned.1.call-start = ((), (), s32[]{:S(2)}) async-start(), calls=%async_computation.9 | async-start | bytes 6553600 | tf_op jit(solution)/shard_map/reduce_scatter | solution.py:554
  346.7 48.2 %collective-permute-start.37 = (bf16[256,2560]{1,0:T(8,128)(2,1)S(1)}, bf16[256,2560]{1,0:T(8,128)(2,1)S(1)}, u32[]{:S(2)}, u32[]{:S(2)}) collective-permute-start(bf16[256,2560]{1,0:T(8,128)(2,1)S(1)} %get-tuple-element.173), channel_id=1, source_target_pairs={{0,1},{1,0},{2,3},{3,2},{4,5},{5,4},{6,7},{7,6},{8,9},{9,8},{10,11... | collective-permute-start | bytes 3932168 | tf_op jit(solution)/shard_map/ppermute | solution.py:31
  496.6 336.4 %reduce-scatter.5.cloned.1.call-start = ((), (), s32[]{:S(2)}) async-start(), calls=%async_computation.6 | async-start | bytes 13107200 | tf_op jit(solution)/shard_map/reduce_scatter | solution.py:554
  504.0 46.8 %collective-permute-start.45 = (bf16[256,1280]{1,0:T(8,128)(2,1)S(1)}, bf16[256,1280]{1,0:T(8,128)(2,1)S(1)}, u32[]{:S(2)}, u32[]{:S(2)}) collective-permute-start(bf16[256,1280]{1,0:T(8,128)(2,1)S(1)} %get-tuple-element.204), channel_id=1, source_target_pairs={{0,8},{8,0},{16,24},{24,16},{1,9},{9,1},{17,25},{25,17},{2,10},{10... | collective-permute-start | bytes 1966088 | tf_op jit(solution)/shard_map/ppermute | solution.py:464
  504.6 46.3 %collective-permute-start.49 = (bf16[256,1280]{1,0:T(8,128)(2,1)S(1)}, bf16[256,1280]{1,0:T(8,128)(2,1)S(1)}, u32[]{:S(2)}, u32[]{:S(2)}) collective-permute-start(bf16[256,1280]{1,0:T(8,128)(2,1)S(1)} %get-tuple-element.205), channel_id=1, source_target_pairs={{0,16},{8,24},{16,0},{24,8},{1,17},{9,25},{17,1},{25,9},{2,18},{10... | collective-permute-start | bytes 1966088 | tf_op jit(solution)/shard_map/ppermute | solution.py:464
  575.4 371.3 %reduce-scatter.7.cloned.1.call-start = ((), (), s32[]{:S(2)}) async-start(), calls=%async_computation.7 | async-start | bytes 4096000 | tf_op jit(solution)/shard_map/reduce_scatter | solution.py:720
  696.8 47.2 %collective-permute-start.84 = (bf16[640,640]{1,0:T(8,128)(2,1)}, bf16[640,640]{1,0:T(8,128)(2,1)}, u32[]{:S(2)}, u32[]{:S(2)}) collective-permute-start(bf16[640,640]{1,0:T(8,128)(2,1)} %get-tuple-element.187), channel_id=1, source_target_pairs={{0,8},{8,0},{16,24},{24,16},{1,9},{9,1},{17,25},{25,17},{2,10},{10... | collective-permute-start | bytes 2457608 | tf_op jit(solution)/shard_map/ppermute | solution.py:464
  697.4 58.0 %collective-permute-start.83 = (bf16[640,640]{1,0:T(8,128)(2,1)}, bf16[640,640]{1,0:T(8,128)(2,1)}, u32[]{:S(2)}, u32[]{:S(2)}) collective-permute-start(bf16[640,640]{1,0:T(8,128)(2,1)} %get-tuple-element.184), channel_id=1, source_target_pairs={{0,8},{8,0},{16,24},{24,16},{1,9},{9,1},{17,25},{25,17},{2,10},{10... | collective-permute-start | bytes 2457608 | tf_op jit(solution)/shard_map/ppermute | solution.py:464
  710.9 49.4 %collective-permute-start.87 = (bf16[640,640]{1,0:T(8,128)(2,1)}, bf16[640,640]{1,0:T(8,128)(2,1)}, u32[]{:S(2)}, u32[]{:S(2)}) collective-permute-start(bf16[640,640]{1,0:T(8,128)(2,1)} %get-tuple-element.185), channel_id=1, source_target_pairs={{0,16},{8,24},{16,0},{24,8},{1,17},{9,25},{17,1},{25,9},{2,18},{10... | collective-permute-start | bytes 2457608 | tf_op jit(solution)/shard_map/ppermute | solution.py:464
  735.1 52.5 %collective-permute-start.77 = (bf16[640,640]{0,1:T(8,128)(2,1)}, bf16[640,640]{0,1:T(8,128)(2,1)S(1)}, u32[]{:S(2)}, u32[]{:S(2)}) collective-permute-start(bf16[640,640]{0,1:T(8,128)(2,1)} %get-tuple-element.178), channel_id=1, source_target_pairs={{0,8},{8,0},{16,24},{24,16},{1,9},{9,1},{17,25},{25,17},{2,10},{10... | collective-permute-start | bytes 2457608 | tf_op jit(solution)/shard_map/ppermute | solution.py:464
  760.3 57.1 %collective-permute-start.86 = (bf16[640,640]{1,0:T(8,128)(2,1)S(1)}, bf16[640,640]{1,0:T(8,128)(2,1)S(1)}, u32[]{:S(2)}, u32[]{:S(2)}) collective-permute-start(bf16[640,640]{1,0:T(8,128)(2,1)S(1)} %copy-done.43), channel_id=1, source_target_pairs={{0,16},{8,24},{16,0},{24,8},{1,17},{9,25},{17,1},{25,9},{2,18},{10... | collective-permute-start | bytes 2457608 | tf_op jit(solution)/shard_map/ppermute | solution.py:464
  782.3 48.1 %collective-permute-start.80 = (bf16[640,640]{0,1:T(8,128)(2,1)S(1)}, bf16[640,640]{0,1:T(8,128)(2,1)S(1)}, u32[]{:S(2)}, u32[]{:S(2)}) collective-permute-start(bf16[640,640]{0,1:T(8,128)(2,1)S(1)} %copy-done.44), channel_id=1, source_target_pairs={{0,16},{8,24},{16,0},{24,8},{1,17},{9,25},{17,1},{25,9},{2,18},{10... | collective-permute-start | bytes 2457608 | tf_op jit(solution)/shard_map/ppermute | solution.py:464
  787.6 67.9 %collective-permute-start.64 = (f32[256,2560]{1,0:T(8,128)}, f32[256,2560]{1,0:T(8,128)}, u32[]{:S(2)}, u32[]{:S(2)}) collective-permute-start(f32[256,2560]{1,0:T(8,128)} %convolution_add_fusion), channel_id=1, source_target_pairs={{0,1},{1,0},{2,3},{3,2},{4,5},{5,4},{6,7},{7,6},{8,9},{9,8},{10,11... | collective-permute-start | bytes 7864328 | tf_op jit(solution)/shard_map/ppermute | solution.py:31
  818.4 73.8 %collective-permute-start.89 = (bf16[128,640]{1,0:T(8,128)(2,1)}, bf16[128,640]{1,0:T(8,128)(2,1)}, u32[]{:S(2)}, u32[]{:S(2)}) collective-permute-start(bf16[128,640]{1,0:T(8,128)(2,1)} %get-tuple-element.244), channel_id=1, source_target_pairs={{0,8},{8,0},{16,24},{24,16},{1,9},{9,1},{17,25},{25,17},{2,10},{10... | collective-permute-start | bytes 491528 | tf_op jit(solution)/shard_map/ppermute | solution.py:464
  830.4 62.2 %collective-permute-start.93 = (bf16[128,640]{1,0:T(8,128)(2,1)}, bf16[128,640]{1,0:T(8,128)(2,1)}, u32[]{:S(2)}, u32[]{:S(2)}) collective-permute-start(bf16[128,640]{1,0:T(8,128)(2,1)} %get-tuple-element.245), channel_id=1, source_target_pairs={{0,16},{8,24},{16,0},{24,8},{1,17},{9,25},{17,1},{25,9},{2,18},{10... | collective-permute-start | bytes 491528 | tf_op jit(solution)/shard_map/ppermute | solution.py:464
  838.4 156.6 %reduce-scatter.9.cloned.1.call-start = ((), (), s32[]{:S(2)}) async-start(), calls=%async_computation.8 | async-start | bytes 2457600 | tf_op jit(solution)/shard_map/reduce_scatter | solution.py:720
  868.0 47.3 %collective-permute-start.92 = (bf16[128,640]{1,0:T(8,128)(2,1)S(1)}, bf16[128,640]{1,0:T(8,128)(2,1)S(1)}, u32[]{:S(2)}, u32[]{:S(2)}) collective-permute-start(bf16[128,640]{1,0:T(8,128)(2,1)S(1)} %get-tuple-element.246), channel_id=1, source_target_pairs={{0,16},{8,24},{16,0},{24,8},{1,17},{9,25},{17,1},{25,9},{2,18},{10... | collective-permute-start | bytes 491528 | tf_op jit(solution)/shard_map/ppermute | solution.py:464
  889.1 46.9 %collective-permute-start.65 = (f32[256,2560]{1,0:T(8,128)S(1)}, f32[256,2560]{1,0:T(8,128)}, u32[]{:S(2)}, u32[]{:S(2)}) collective-permute-start(f32[256,2560]{1,0:T(8,128)S(1)} %subtract_add_fusion), channel_id=1, source_target_pairs={{0,1},{1,0},{2,3},{3,2},{4,5},{5,4},{6,7},{7,6},{8,9},{9,8},{10,11... | collective-permute-start | bytes 7864328 | tf_op jit(solution)/shard_map/ppermute | solution.py:31
  (156 other events, 2844.6 us)
Sparse Core Ops, SparseCore 0:
  12.4 100.7 all-gather.8
  114.8 182.2 all-gather.4
  335.0 101.0 all-gather.6
  496.7 92.2 reduce-scatter.10
  591.1 180.6 reduce-scatter.4
  838.5 62.9 reduce-scatter.6
  954.7 40.3 reduce-scatter.8

commit v3 on v2

--- a/solution.py
+++ b/solution.py
@@ -164,11 +164,7 @@
         out_shape=[jax.ShapeDtypeStruct((rows, length, units), BF16)] + [big] * 5,
         scratch_shapes=[pltpu.VMEM((rows, length + 8, HEAD_W), F32), scan, scan, scan, scan],
         compiler_params=pltpu.CompilerParams(vmem_limit_bytes=48 * 1024 * 1024),
-        cost_estimate=pl.CostEstimate(
-            flops=4 * rows * length * units * HEAD_W,
-            bytes_accessed=24 * rows * length * units,
-            transcendentals=8 * rows * length * units,
-        ),
+        cost_estimate=cost(),
         name="recurrent_forward",
     )(x_branch, halo, masks, params, blocks)
 
@@ -204,11 +200,7 @@
         out_shape=[jax.ShapeDtypeStruct((rows, length, units), BF16), big, big],
         scratch_shapes=[longer, scan, scan, scan],
         compiler_params=pltpu.CompilerParams(vmem_limit_bytes=48 * 1024 * 1024),
-        cost_estimate=pl.CostEstimate(
-            flops=30 * rows * length * units,
-            bytes_accessed=32 * rows * length * units,
-            transcendentals=rows * length * units,
-        ),
+        cost_estimate=cost(),
         name="recurrent_adjoint",
     )(rec_grad, gelu_in, coef, prod, total, state_in)
 
@@ -306,11 +298,7 @@
             pltpu.VMEM((rows, length + 16, HEAD_W), F32),
         ],
         compiler_params=pltpu.CompilerParams(vmem_limit_bytes=48 * 1024 * 1024),
-        cost_estimate=pl.CostEstimate(
-            flops=8 * rows * length * units * HEAD_W,
-            bytes_accessed=40 * rows * length * units,
-            transcendentals=4 * rows * length * units,
-        ),
+        cost_estimate=cost(),
         name="recurrent_backward",
     )(tprod, tsum, leaving, prod, total, state_in, coef, r, i, conv_low, x_branch, halo, masks, params, blocks)
 
@@ -322,8 +310,8 @@
     return pl.BlockSpec((TILE, columns), lambda m: ((m + first) % tiles, 0))
 
 
-def held(rows, columns):
-    return pl.BlockSpec((rows, columns), lambda m: (0, 0), pipeline_mode=pl.Buffered(1))
+def held(rows, columns, at=0):
+    return pl.BlockSpec((rows, columns), lambda m: (0, at), pipeline_mode=pl.Buffered(1))
 
 
 def half_specs(columns, tiles):
@@ -350,44 +338,78 @@
     return pltpu.CompilerParams(vmem_limit_bytes=56 * 1024 * 1024)
 
 
-def cost(flops, size):
-    return pl.CostEstimate(flops=flops, bytes_accessed=size, transcendentals=0)
-
-
-def forward_tile(x_ref, w_ref, hidden_ref, by_gate_ref, by_up_ref):
-    share = hidden_ref.shape[1]
-    x = x_ref[...]
-    value, slope = gelu_pair(dot(x, w_ref[:, :share], ((1,), (0,))))
-    up = dot(x, w_ref[:, share:], ((1,), (0,)))
-    hidden_ref[...] = (value * up).astype(BF16)
-    by_gate_ref[...] = up * slope
-    by_up_ref[...] = value
-
-
-def feed_forward(x, w_expand):
-    count, width = x.shape
-    share = w_expand.shape[1] // 2
-    tiles = count // TILE
+def cost():
+    return pl.CostEstimate(flops=1, bytes_accessed=1, transcendentals=0)
+
+
+def feed_forward(pieces, w_feed):
+    width = pieces[0].shape[1]
+    share = w_feed.shape[1] // 3
+    part = TILE // 2
+    halves = []
+    for n, piece in enumerate(pieces):
+        halves += [(n, at) for at in range(0, piece.shape[0], part)]
+    tiles = len(halves) // 2
+    count = tiles * TILE
+
+    def body(*refs):
+        xs, (w_ref, all_ref, hidden_ref, by_gate_ref, by_up_ref, held_x, sems) = refs[: len(pieces)], refs[len(pieces) :]
+        m = pl.program_id(0)
+
+        def fetch(tile, slot):
+            for at in range(tiles):
+
+                @pl.when(tile == at)
+                def _():
+                    for h in range(2):
+                        n, row = halves[2 * at + h]
+                        pltpu.make_async_copy(
+                            xs[n].at[pl.ds(row, part)], held_x.at[slot, pl.ds(h * part, part)], sems.at[slot, h]
+                        ).start()
+
+        @pl.when(m == 0)
+        def _():
+            fetch(0, 0)
+
+        @pl.when(m + 1 < tiles)
+        def _():
+            fetch(m + 1, (m + 1) % 2)
+
+        slot = m % 2
+        for h in range(2):
+            pltpu.make_async_copy(
+                xs[0].at[pl.ds(0, part)], held_x.at[slot, pl.ds(h * part, part)], sems.at[slot, h]
+            ).wait()
+        x = held_x[slot]
+        all_ref[...] = x
+        value, slope = gelu_pair(dot(x, w_ref[:, :share], ((1,), (0,))))
+        up = dot(x, w_ref[:, share:], ((1,), (0,)))
+        hidden_ref[...] = (value * up).astype(BF16)
+        by_gate_ref[...] = up * slope
+        by_up_ref[...] = value
+
     tile = tokens_spec(share, tiles, 0)
     return pl.pallas_call(
-        forward_tile,
+        body,
         grid=(tiles,),
-        in_specs=[tokens_spec(width, tiles, 0), held(width, 2 * share)],
-        out_specs=[tile] * 3,
+        in_specs=[pl.BlockSpec(memory_space=pl.ANY)] * len(pieces) + [held(width, 2 * share)],
+        out_specs=[tokens_spec(width, tiles, 0)] + [tile] * 3,
         out_shape=[
+            jax.ShapeDtypeStruct((count, width), BF16),
             jax.ShapeDtypeStruct((count, share), BF16),
             jax.ShapeDtypeStruct((count, share), F32),
             jax.ShapeDtypeStruct((count, share), F32),
         ],
+        scratch_shapes=[pltpu.VMEM((2, TILE, width), BF16), pltpu.SemaphoreType.DMA((2, 2))],
         compiler_params=feed_params(),
-        cost_estimate=cost(4 * count * width * share, 10 * count * share + 2 * count * width),
+        cost_estimate=cost(),
         name="feed_forward",
-    )(x, w_expand)
-
-
-def feed_backward(feed_grad, by_gate, by_up, w_down, w_expand):
+    )(*pieces, w_feed)
+
+
+def feed_backward(feed_grad, by_gate, by_up, w_feed):
     count, width = feed_grad.shape
-    share = w_down.shape[1]
+    share = w_feed.shape[1] // 3
     tiles = count // TILE
     mid = tiles // 2
 
@@ -404,7 +426,7 @@
     return pl.pallas_call(
         body,
         grid=(tiles,),
-        in_specs=[tokens_spec(width, tiles, mid), tile, tile, held(width, share), held(width, 2 * share)],
+        in_specs=[tokens_spec(width, tiles, mid), tile, tile, held(width, share, 2), held(width, 2 * share)],
         out_specs=[tokens_spec(2 * share, tiles, mid)] + half_specs(width, tiles),
         out_shape=[
             jax.ShapeDtypeStruct((count, 2 * share), BF16),
@@ -412,14 +434,14 @@
             jax.ShapeDtypeStruct((count // 2, width), BF16),
         ],
         compiler_params=feed_params(),
-        cost_estimate=cost(6 * count * width * share, 12 * count * share + 4 * count * width),
+        cost_estimate=cost(),
         name="feed_backward",
-    )(feed_grad, by_gate, by_up, w_down, w_expand)
-
-
-def feed_down(hidden, w_down):
+    )(feed_grad, by_gate, by_up, w_feed, w_feed)
+
+
+def feed_down(hidden, w_feed):
     count, share = hidden.shape
-    width = w_down.shape[0]
+    width = w_feed.shape[0]
     tiles = count // TILE
 
     def body(h_ref, w_ref, first_ref, second_ref):
@@ -428,36 +450,86 @@
     return pl.pallas_call(
         body,
         grid=(tiles,),
-        in_specs=[tokens_spec(share, tiles, tiles // 2), held(width, share)],
+        in_specs=[tokens_spec(share, tiles, tiles // 2), held(width, share, 2)],
         out_specs=half_specs(width, tiles),
         out_shape=[jax.ShapeDtypeStruct((count // 2, width), BF16)] * 2,
         compiler_params=feed_params(),
-        cost_estimate=cost(2 * count * width * share, 2 * count * share + 2 * count * width),
+        cost_estimate=cost(),
         name="feed_down",
-    )(hidden, w_down)
-
-
-def weight_grad(x, grad):
+    )(hidden, w_feed)
+
+
+def weight_grad(x, grad, into=None, at=0, blocks=1):
     count, width = x.shape
     columns = grad.shape[1]
-    deep, wide = 512, min(columns, 1024)
-
-    def body(x_ref, g_ref, out_ref):
-        out_ref[...] = dot(x_ref[...], g_ref[...], ((0,), (0,))).astype(BF16)
+    deep, wide = 512 if count > 1024 else width // 2, columns // blocks
+
+    def body(x_ref, g_ref, *rest):
+        rest[-1][...] = dot(x_ref[...], g_ref[...], ((0,), (0,))).astype(BF16)
 
     return pl.pallas_call(
         body,
-        grid=(columns // wide, width // deep),
+        grid=(width // deep,),
         in_specs=[
-            pl.BlockSpec((count, deep), lambda n, m: (0, m)),
-            pl.BlockSpec((count, wide), lambda n, m: (0, n)),
-        ],
-        out_specs=pl.BlockSpec((deep, wide), lambda n, m: (m, n)),
+            pl.BlockSpec((count, deep), lambda m: (0, m)),
+            pl.BlockSpec((count, wide), lambda m: (0, at), pipeline_mode=pl.Buffered(1)),
+        ]
+        + ([] if into is None else [pl.BlockSpec(memory_space=pl.ANY)]),
+        out_specs=pl.BlockSpec((deep, wide), lambda m: (m, at)),
         out_shape=jax.ShapeDtypeStruct((width, columns), BF16),
+        input_output_aliases={} if into is None else {2: 0},
         compiler_params=feed_params(),
-        cost_estimate=cost(2 * count * width * columns, 2 * (count * width + count * columns + width * columns)),
+        cost_estimate=cost(),
         name="weight_grad",
-    )(x, grad)
+    )(x, grad, *([] if into is None else [into]))
+
+
+ORDER = (1, 3, 2, 0)
+
+
+def weight_grad_parts(x, grad, places, extra=None):
+    count, width = x.shape
+    columns = grad.shape[1]
+    rows, cols = width // SQUARE, columns // 2
+    more = 0 if extra is None else extra.shape[0] // SQUARE
+    each = rows + more
+
+    def body(places_ref, x_ref, g_ref, *rest):
+        left_ref, right_ref, two_ref, one_ref, own_left, own_right = rest[-6:]
+        targets = [
+            ((left_ref, 0), (one_ref, 0)),
+            ((left_ref, each), (right_ref, 0)),
+            ((two_ref, 0), (right_ref, each)),
+            ((own_left, 0), (own_right, 0)),
+        ]
+        value = dot(x_ref[...], g_ref[...], ((0,), (0,))).astype(BF16)
+        for n in range(SQUARE):
+
+            @pl.when(pl.program_id(0) == n)
+            def _():
+                for h, (ref, at) in enumerate(targets[n]):
+                    ref[pl.ds(at, rows), :] = value[:, h * cols : (h + 1) * cols]
+                    if more:
+                        ref[pl.ds(at + rows, more), :] = rest[0][:, h * cols : (h + 1) * cols]
+
+    sizes = [2 * each, 2 * each] + [each] * 4
+    return pl.pallas_call(
+        body,
+        grid_spec=pltpu.PrefetchScalarGridSpec(
+            num_scalar_prefetch=1,
+            grid=(SQUARE,),
+            in_specs=[
+                pl.BlockSpec((count, rows), lambda n, places_ref: (0, places_ref[n])),
+                pl.BlockSpec((count, columns), lambda n, places_ref: (0, 0)),
+            ]
+            + ([pl.BlockSpec((more, columns), lambda n, places_ref: (places_ref[n], 0))] if more else []),
+            out_specs=[pl.BlockSpec((size, cols), lambda n, places_ref: (0, 0)) for size in sizes],
+        ),
+        out_shape=[jax.ShapeDtypeStruct((size, cols), BF16) for size in sizes],
+        compiler_params=feed_params(),
+        cost_estimate=cost(),
+        name="weight_grad_parts",
+    )(places, x, grad, *([extra] if more else []))
 
 
 def cross(x, axis, r):
@@ -483,56 +555,102 @@
     return ("fsdp", "ctx") if lax.axis_size("fsdp") == SQUARE else ("ctx", "fsdp")
 
 
+def together(*values):
+    return lax.optimization_barrier(values)
+
+
 def place(blocks, axis):
     me = lax.axis_index(axis)
-    whole = jnp.zeros((len(blocks),) + blocks[0].shape, blocks[0].dtype)
+    first = blocks[0]
+    whole = jnp.zeros((len(blocks),) + first.shape, first.dtype)
     for r, block in enumerate(blocks):
-        whole = lax.dynamic_update_index_in_dim(whole, block, me ^ r, 0)
+        at = 0
+        for piece in block if isinstance(block, list) else [block]:
+            whole = lax.dynamic_update_slice(whole, piece[None], (me ^ r, at) + (0,) * (piece.ndim - 1))
+            at += piece.shape[0]
     return whole
 
 
+def near_blocks(x, axis):
+    return list(together(cross(x, axis, 1), cross(x, axis, 2)))
+
+
+def far_block(got, axis):
+    mid = got[0].shape[0] // 2
+    halves = together(got[0][:mid], got[1][mid:])
+    return [cross(halves[0], axis, 2), cross(halves[1], axis, 1)]
+
+
 def near(x, axis):
-    mid = x.shape[0] // 2
-    one, two = cross(x, axis, 1), cross(x, axis, 2)
-    three = jnp.concatenate([cross(one[:mid], axis, 2), cross(two[mid:], axis, 1)], axis=0)
-    return [x, one, two, three]
-
-
-def near_sum(block, axis):
-    low = lambda v: v.astype(BF16)
-    wide = lambda v: v.astype(F32)
-    a1, a3 = cross(low(block(1, 0)), axis, 1), cross(low(block(3, 0)), axis, 1)
-    b2, b3 = cross(low(block(2, 1)), axis, 2), cross(low(block(3, 1)), axis, 2)
-    a2 = cross(low(wide(block(2, 0)) + wide(a3)), axis, 2)
-    b1 = cross(low(wide(block(1, 1)) + wide(b3)), axis, 1)
-    left = wide(block(0, 0)) + wide(a1) + wide(a2)
-    right = wide(block(0, 1)) + wide(b2) + wide(b1)
+    got = near_blocks(x, axis)
+    return [x] + got + [far_block(got, axis)]
+
+
+def low(v):
+    return v.astype(BF16)
+
+
+def wide(v):
+    return v.astype(F32)
+
+
+def near_send(parts, axis):
+    return together(cross(parts[0], axis, 1), cross(parts[1], axis, 2))
+
+
+def near_middle(parts, got):
+    rows = got[0].shape[0] // 2
+    return together(low(wide(parts[2]) + wide(got[0][rows:])), low(wide(parts[3]) + wide(got[1][:rows])))
+
+
+def near_second(sums, axis):
+    return together(cross(sums[0], axis, 2), cross(sums[1], axis, 1))
+
+
+def near_last(parts, got, more):
+    rows = got[0].shape[0] // 2
+    left = wide(parts[4]) + wide(got[0][:rows]) + wide(more[0])
+    right = wide(parts[5]) + wide(got[1][rows:]) + wide(more[1])
     return jnp.concatenate([left, right], axis=1)
 
 
-def gather_rows(x):
+def gather_in_turn(arrays):
     if lax.axis_size("fsdp") != SQUARE:
-        return lax.all_gather(x, "fsdp", axis=0, tiled=True)
-    return place(near(x, "fsdp"), "fsdp").reshape(SQUARE * x.shape[0], x.shape[1])
-
-
-def scatter_rows(x):
+        return [lax.all_gather(x, "fsdp", axis=0) for x in arrays]
+    results = []
+    for x in arrays:
+        if results:
+            x, results[-1] = together(x, results[-1])
+        results.append(near(x, "fsdp"))
+    return results
+
+
+def rows_of(blocks, start, stop):
     if lax.axis_size("fsdp") != SQUARE:
-        return lax.psum_scatter(x, "fsdp", scatter_dimension=0, tiled=True).astype(F32)
-    me, rows, cols = lax.axis_index("fsdp"), x.shape[0] // SQUARE, x.shape[1] // 2
-    return near_sum(lambda r, h: lax.dynamic_slice(x, ((me ^ r) * rows, h * cols), (rows, cols)), "fsdp")
-
-
-def gather_tokens(x):
-    blocks = near(x, token_axes()[0])
-    return jnp.concatenate(blocks + [swap(block, "tp") for block in blocks], axis=0)
-
-
-def scatter_tokens(first, second):
-    theirs = swap(second, "tp")
-    mine = (first.astype(F32) + theirs.astype(F32)).astype(BF16)
-    rows, cols = mine.shape[0] // SQUARE, mine.shape[1] // 2
-    return near_sum(lambda r, h: mine[r * rows : (r + 1) * rows, h * cols : (h + 1) * cols], token_axes()[0])
+        return blocks[:, :, start:stop].reshape(-1, blocks.shape[-1])
+    cut = lambda v: v[:, start:stop]
+    whole = place([[cut(v) for v in block] if isinstance(block, list) else cut(block) for block in blocks], "fsdp")
+    return whole.reshape(-1, whole.shape[-1])
+
+
+def token_pieces(x):
+    axis = token_axes()[0]
+    theirs = swap(x, "tp")
+    got = near_blocks(x, axis)
+    far = far_block(got, axis)
+    got_theirs = [swap(v, "tp") for v in got]
+    far_theirs = [swap(v, "tp") for v in far]
+    return [got[0], *far, got[1], x, got_theirs[0], *far_theirs, got_theirs[1], theirs]
+
+
+def token_parts(first, theirs):
+    rows, cols = first.shape[0] // SQUARE, first.shape[1] // 2
+
+    def part(start, stop, half):
+        here = (slice(start * rows, stop * rows), slice(half * cols, (half + 1) * cols))
+        return low(wide(first[here]) + wide(theirs[here]))
+
+    return together(part(0, 2, 0), part(1, 3, 1), part(2, 3, 0), part(0, 1, 1), part(3, 4, 0), part(3, 4, 1))
 
 
 def trade(pieces):
@@ -595,37 +713,26 @@
             [jnp.where(mine == 0, x, theirs), jnp.where(mine == 0, theirs, x)], axis=0
         )
 
-    packed = jnp.concatenate(
-        [intake[:, 1], intake[:, 0], outlet, gate_blocks.reshape(2 * gate_rows, units)], axis=0
-    )
-    packed = lax.all_gather(packed, "ctx", axis=0)
-
-    def part(n, count):
-        return packed[:, n * depth : n * depth + count].reshape(ctx * count, units)
+    first = jnp.concatenate([intake[:, 1], gate_blocks.reshape(2 * gate_rows, units)], axis=0)
+    first = lax.all_gather(first, "ctx", axis=0)
+    second = lax.all_gather(jnp.concatenate([intake[:, 0], outlet], axis=0), "ctx", axis=0)
 
     def cut(w):
         w = jnp.pad(w, ((0, 0), (0, padding)))
         return lambda p: lax.dynamic_slice_in_dim(w, p * share, share, 1)
 
     down, gate_in, up_in = cut(contract), cut(expand[:, 0]), cut(expand[:, 1])
-    w_expand = trade(lambda p: jnp.concatenate([gate_in(p), up_in(p)], axis=1))
-    w_expand = gather_feed(w_expand)
-    local_down = trade(down)
+    w_feed = gather_feed(trade(lambda p: jnp.concatenate([gate_in(p), up_in(p), down(p)], axis=1)))
 
     mask_rows = token_mask.astype(F32).reshape(tokens, 1)
     out_grad = own(cotangent.reshape(tokens, width)).astype(F32) * own(mask_rows)
-    feed_grad = gather_tokens(out_grad.astype(BF16))
-
-    local_branch, local_down, feed_grad = lax.optimization_barrier((part(0, depth), local_down, feed_grad))
-    w_down = gather_feed(local_down)
-    w_branch = gather_rows(local_branch)
-    local_gates, w_branch = after(part(3, 2 * gate_rows), w_branch)
-    w_gates = gather_rows(local_gates)
-    local_gelu, w_gates = after(part(1, depth), w_gates)
-    blocks = w_gates.reshape(HEAD_W, 2, units).transpose(1, 0, 2)
-    w_gelu = gather_rows(local_gelu)
-    local_outlet, w_gelu = after(part(2, depth), w_gelu)
-    w_outlet = gather_rows(local_outlet)
+    local_feed_grad = out_grad.astype(BF16)
+
+    got_first, got_gelu, got_outlet = gather_in_turn([first, second[:, :depth], second[:, depth:]])
+    w_branch = rows_of(got_first, 0, depth)
+    blocks = rows_of(got_first, depth, first.shape[1]).reshape(HEAD_W, 2, units).transpose(1, 0, 2)
+    w_gelu = rows_of(got_gelu, 0, depth)
+    w_outlet = rows_of(got_outlet, 0, depth)
 
     seg_next = segments + 1
     seg_before = shifted(seg_next[:, -3:], "ctx", 1)
@@ -668,30 +775,42 @@
     branch = dot(own(recurrent), w_outlet, ((1,), (1,))) + sent
     residual = own(x) + branch
     inverse_two = rms(residual)
-    normed_two = gather_tokens((residual * inverse_two * norm_gains[1]).astype(BF16))
+    normed_two = token_pieces((residual * inverse_two * norm_gains[1]).astype(BF16))
 
     def to_owners(part):
         return trade(lambda p: lax.dynamic_index_in_dim(part, p, 0, keepdims=False))
 
-    hidden, by_gate, by_up = feed_forward(normed_two, w_expand)
-    down_part = scatter_feed(weight_grad(feed_grad, hidden))
-    low, n2g_own, n2g_other = feed_backward(feed_grad, by_gate, by_up, w_down, w_expand)
-    normed_two_grad = scatter_tokens(n2g_own, n2g_other)
-    expand_all = weight_grad(normed_two, low)
-    feed_own, feed_other = feed_down(hidden, w_down)
-    normed_two_grad, expand_all, feed_own, feed_other = lax.optimization_barrier(
-        (normed_two_grad, expand_all, feed_own, feed_other)
-    )
+    local_feed_grad, normed_two = together(local_feed_grad, normed_two)
+    feed_grad = jnp.concatenate(token_pieces(local_feed_grad), axis=0)
+    normed_two, hidden, by_gate, by_up = feed_forward(normed_two, w_feed)
+    down_grad = weight_grad(feed_grad, hidden)
+    by_gate, down_grad = after(by_gate, down_grad)
+    down_part = scatter_feed(down_grad)
+    expand_low, n2g_own, n2g_other = feed_backward(feed_grad, by_gate, by_up, w_feed)
+
+    group = token_axes()[0]
+    theirs = swap(n2g_other, "tp")
+    parts, expand_low = after(token_parts(n2g_own, theirs), expand_low)
+    got = near_send(parts, group)
+    expand_all = weight_grad(normed_two, expand_low)
+    got, expand_all = after(got, expand_all)
+    sums, hidden = after(near_middle(parts, got), hidden)
+    more = near_second(sums, group)
+    feed_own, feed_other = feed_down(hidden, w_feed)
+    more, (feed_own, feed_other) = after(more, (feed_own, feed_other))
+    normed_two_grad = near_last(parts, got, more)
     expand_part = scatter_feed(expand_all)
-    feed_out = scatter_tokens(feed_own, feed_other)
-    block_output = join((residual + feed_out).astype(BF16)).reshape(rows, length, width)
+    feed_theirs = swap(feed_other, "tp")
 
     norm_part, gain_two = rms_back(residual, inverse_two, norm_gains[1], normed_two_grad)
     residual_grad = out_grad + norm_part
     branch_grad = join(residual_grad.astype(BF16))
 
-    outlet_grad = dot(branch_grad, recurrent, ((0,), (0,))).astype(BF16)
+    square = lax.axis_size("fsdp") == SQUARE
+    places = lax.axis_index("fsdp").astype(jnp.int32) ^ jnp.array(ORDER, jnp.int32)
     rec_grad = dot(branch_grad, w_outlet, ((1,), (0,))).reshape(rows, length, units)
+    feed_parts, rec_grad = after(token_parts(feed_own, feed_theirs), rec_grad)
+    feed_got = near_send(feed_parts, group)
     gelu_grad, tprod, tsum = recurrent_adjoint(rec_grad, gelu_in, coef, prod, total, state_in)
     heads = jnp.stack([coef[:, 0] * tprod[:, 0], coef[:, 0] * tsum[:, 0]])
     leaving = jnp.zeros((rows, units), F32)
@@ -699,33 +818,72 @@
         head = shifted(heads, "ctx", -by)
         leaving = head[1] + head[0] * leaving
     leaving = jnp.broadcast_to(leaving[:, None], (rows, 8, units))
+    gelu_low = gelu_grad.reshape(tokens, units)
+    branch_grad, gelu_low = after(branch_grad, gelu_low)
+    if square:
+        outlet_parts = weight_grad_parts(branch_grad, recurrent, places)
+    else:
+        outlet_parts = weight_grad(branch_grad, recurrent)
+    outlet_parts, tprod, feed_got = together(outlet_parts, tprod, feed_got)
+    feed_sums = near_middle(feed_parts, feed_got)
+    feed_sums, tprod = after(feed_sums, tprod)
+    feed_more = near_second(feed_sums, group)
+    if square:
+        outlet_got = near_send(outlet_parts, "fsdp")
     branch_x, before, small, blocks_grad = recurrent_backward(
         tprod, tsum, leaving, prod, total, state_in, coef, r, i, conv_low, x_branch, halo, masks, params, blocks
     )
+    gelu_low, small = after(gelu_low, small)
+    if square:
+        gelu_parts = weight_grad_parts(normed, gelu_low, places)
+    else:
+        gelu_parts = weight_grad(normed, gelu_low)
     from_next = shifted(before[:, 5:], "ctx", -1)
     branch_x = branch_x + jnp.pad(from_next, ((0, 0), (length - 3, 0), (0, 0)))
-    gelu_low = gelu_grad.reshape(tokens, units)
-    branch_low = branch_x.astype(BF16).reshape(tokens, units)
+    branch_low, gelu_parts = together(branch_x.astype(BF16).reshape(tokens, units), gelu_parts)
+    blocks_rows = blocks_grad.transpose(1, 0, 2).reshape(2 * HEAD_W, units)
+    if square:
+        branch_parts = weight_grad_parts(normed, branch_low, places, blocks_rows)
+        outlet_got, branch_parts, feed_more = together(outlet_got, branch_parts, feed_more)
+        outlet_sums, gelu_parts = after(near_middle(outlet_parts, outlet_got), gelu_parts)
+        outlet_more, gelu_got = near_second(outlet_sums, "fsdp"), near_send(gelu_parts, "fsdp")
+    else:
+        branch_parts = weight_grad(normed, branch_low)
 
     def input_terms(pick):
         return dot(pick(branch_low), w_branch, ((1,), (1,))) + dot(pick(gelu_low), w_gelu, ((1,), (1,)))
 
-    gelu_part = scatter_rows(dot(normed, gelu_low, ((0,), (0,))).astype(BF16)).astype(BF16)
-    outlet_part = scatter_rows(outlet_grad).astype(BF16)
-    branch_part = scatter_rows(dot(normed, branch_low, ((0,), (0,))).astype(BF16)).astype(BF16)
-    blocks_part = scatter_rows(blocks_grad.transpose(1, 0, 2).reshape(2 * HEAD_W, units)).astype(BF16)
-
-    def scatter_ctx(parts):
-        parts = jnp.concatenate([p.reshape(ctx, -1, units) for p in parts], axis=1)
-        return lax.psum_scatter(parts, "ctx", scatter_dimension=0, tiled=False).astype(F32)
-
-    gelu_part, expand_part = after(gelu_part, expand_part)
-    early = scatter_ctx([gelu_part, outlet_part])
-    branch_part, early = after(branch_part, early)
-    late = scatter_ctx([branch_part, blocks_part])
+    theirs = input_terms(other)
+    normed_grad = input_terms(own) + swap(theirs, "tp")
+    norm_part, gain_one = rms_back(own(x), own(inverse_one), norm_gains[0], normed_grad)
+    input_own = residual_grad + norm_part
+    if square:
+        gelu_got, outlet_more, input_own = together(gelu_got, outlet_more, input_own)
+        early = [low(near_last(outlet_parts, outlet_got, outlet_more))]
+        gelu_sums, branch_parts = together(near_middle(gelu_parts, gelu_got), branch_parts)
+        gelu_more, branch_got = near_second(gelu_sums, "fsdp"), near_send(branch_parts, "fsdp")
+        early.append(low(near_last(gelu_parts, gelu_got, gelu_more)))
+    else:
+        early = [lax.psum_scatter(v, "fsdp", scatter_dimension=0, tiled=True) for v in (outlet_parts, gelu_parts)]
+    early = jnp.concatenate([v.reshape(ctx, depth, units) for v in early], axis=2)
+    early, expand_part = after(early, expand_part)
+    if square:
+        branch_got, early = together(branch_got, early)
+        late = low(near_last(branch_parts, branch_got, near_second(near_middle(branch_parts, branch_got), "fsdp")))
+        late = [late[: ctx * depth], late[ctx * depth :]]
+    else:
+        late = [lax.psum_scatter(v, "fsdp", scatter_dimension=0, tiled=True) for v in (branch_parts, blocks_rows)]
+    late = jnp.concatenate([v.reshape(ctx, -1, units) for v in late], axis=1)
+
+    early = lax.psum_scatter(early, "ctx", scatter_dimension=0, tiled=False)
+    late, early = after(late, early)
+    late = wide(lax.psum_scatter(late, "ctx", scatter_dimension=0, tiled=False))
 
     down_part = to_owners(down_part)
     expand_part = to_owners(expand_part)
+    feed_out = near_last(feed_parts, feed_got, feed_more)
+    block_output = join(low(residual + feed_out)).reshape(rows, length, width)
+    input_grad = join(input_own).reshape(rows, length, width)
 
     def columns(part, n):
         return jnp.concatenate([part[p, :, n * share : (n + 1) * share] for p in range(SQUARE)], axis=1)[
@@ -734,11 +892,6 @@
 
     contract_grad = columns(down_part, 0)
     expand_grad = jnp.stack([columns(expand_part, 0), columns(expand_part, 1)], axis=1)
-
-    sent = swap(input_terms(other), "tp")
-    normed_grad = input_terms(own) + sent
-    norm_part, gain_one = rms_back(own(x), own(inverse_one), norm_gains[0], normed_grad)
-    input_grad = join(residual_grad + norm_part).reshape(rows, length, width)
 
     gains = jnp.concatenate([gain_one, gain_two]).reshape(-1, units)
     small = total_over(total_over(jnp.concatenate([small, gains], axis=0), "fsdp"), "ctx")
@@ -751,9 +904,9 @@
         small[4],
         small[5:7],
         small[7],
-        jnp.stack([early[:depth], late[:depth]], axis=1),
+        jnp.stack([wide(early[:, units:]), late[:depth]], axis=1),
         late[depth:].reshape(gate_rows, 2, units),
-        early[depth:],
+        wide(early[:, :units]),
         expand_grad,
         contract_grad,
     )

time: 1010 us -> 967 us (0.957)
  waiting for transfers between devices: 423 us -> 377 us
  Pallas kernels: 180 us -> 222 us
  local copies, waits for them, and re-layouts: 130 us -> 101 us
  starting transfers between devices: 110 us -> 89 us
  other arithmetic: 90.4 us -> 103 us
  matrix products: 59 us -> 46.9 us
    ppermute x77 -> x54, waiting for transfers between devices: 394 us -> 311 us  [cross(): lax.ppermute(x, axis, [(i, i ^ r) for i in range(lax.axis_size(axis))])]
    pallas_call x3 -> x6, Pallas kernels: 74.5 us -> 115 us  [the longest x2 43.9 us: weight_grad(): pl.pallas_call(body, grid=(width // deep,), in_specs=[pl.BlockSpec((count...]
    all_gather x1 -> x2, waiting for transfers between devices: 0.01 us -> 23.1 us  [the longest x1 23.1 us: shards(): first = lax.all_gather(first, 'ctx', axis=0)]
    unnamed x167 -> x204, local copies, waits for them, and re-layouts: 45.3 us -> 28.4 us
    convert_element_type x11 -> x22, other arithmetic: 23.1 us -> 39.9 us  [the longest x15 30.9 us: low(): return v.astype(BF16)]
    ppermute x77 -> x54, starting transfers between devices: 83.2 us -> 67.5 us  [cross(): lax.ppermute(x, axis, [(i, i ^ r) for i in range(lax.axis_size(axis))])]
    dot_general x12 -> x9, matrix products: 59 us -> 46.9 us  [dot(): return lax.dot_general(a, b, (dims, ((), ())), preferred_element_type=F32)]
    reduce_scatter x2, waiting for transfers between devices: 5.49 us -> 15.7 us  [the longest x1 13.8 us: shards(): late = wide(lax.psum_scatter(late, 'ctx', scatter_dimension=0, tiled=False))]
  transfers between devices with their start and end apart: 108 -> 87, of which waited for: 48 -> 42; matrix products, arithmetic and copies ran while one was open for 25% -> 24% of each run, Pallas kernels for 13% -> 17%
where the time goes in v3:
time: 967 us; the launch traced here: 956 us
  waiting for transfers between devices  377 us (39%)
  Pallas kernels  222 us (23%)
  other arithmetic  103 us (11%)
  local copies, waits for them, and re-layouts  101 us (10%)
  starting transfers between devices  89 us (9%)
  matrix products  46.9 us (5%)
  between operations  16.4 us (2%)
    ppermute x54, waiting for transfers between devices, cross(): lax.ppermute(x, axis, [(i, i ^ r) for i in range(lax.axis_size(axis))])  311 us
    ppermute x54, starting transfers between devices, cross(): lax.ppermute(x, axis, [(i, i ^ r) for i in range(lax.axis_size(axis))])  67.5 us
    dot_general x9, matrix products, dot(): return lax.dot_general(a, b, (dims, ((), ())), preferred_element_type=F32)  46.9 us
    pallas_call x1, Pallas kernels, feed_backward(): pl.pallas_call(body, grid=(tiles,), in_specs=[tokens_spec(width, tiles, m...  45.7 us
    pallas_call x2, Pallas kernels, weight_grad(): pl.pallas_call(body, grid=(width // deep,), in_specs=[pl.BlockSpec((count...  43.9 us
    pallas_call x1, Pallas kernels, feed_forward(): pl.pallas_call(body, grid=(tiles,), in_specs=[pl.BlockSpec(memory_space=p...  39.9 us
    pallas_call x3, Pallas kernels, weight_grad_parts(): pl.pallas_call(body, grid_spec=pltpu.PrefetchScalarGridSpec(num_scalar_pr...  31.5 us
    convert_element_type x15, other arithmetic, low(): return v.astype(BF16)  30.9 us
  transfers between devices with their start and end apart: 87, of which 42 were waited for; matrix products, arithmetic and copies ran while one was open for 24% of the time, Pallas kernels for 17%

profile of v3, /device:TPU:0, one launch (start us, length us, event | category | flops | bytes accessed | tf_op | source)
XLA Modules:
  0.0 956.0 jit_solution(13670639756101550024)
XLA Ops:
  36.2 23.1 %all-gather.10.cloned.1.call-done = bf16[768,1280]{1,0:T(8,128)(2,1)} async-done(((bf16[192,1280]{1,0:T(8,128)(2,1)}), bf16[768,1280]{1,0:T(8,128)(2,1)}) %all-gather.10.cloned.1.call-update) | async-done | bytes 1966096 | tf_op jit(solution)/shard_map/all_gather | solution.py:717
  72.0 33.2 %collective-permute-done = bf16[4,192,1280]{2,1,0:T(8,128)(2,1)S(1)} collective-permute-done((bf16[4,192,1280]{2,1,0:T(8,128)(2,1)}, bf16[4,192,1280]{2,1,0:T(8,128)(2,1)S(1)}, u32[]{:S(2)}, u32[]{:S(2)}) %collective-permute-start) | collective-permute-done | bytes 1966112 | tf_op jit(solution)/shard_map/ppermute | solution.py:536
  105.2 21.2 %collective-permute-done.1 = bf16[4,192,1280]{2,1,0:T(8,128)(2,1)} collective-permute-done((bf16[4,192,1280]{2,1,0:T(8,128)(2,1)}, bf16[4,192,1280]{2,1,0:T(8,128)(2,1)}, u32[]{:S(2)}, u32[]{:S(2)}) %collective-permute-start.1) | collective-permute-done | bytes 1966112 | tf_op jit(solution)/shard_map/ppermute | solution.py:536
  138.3 13.6 %collective-permute-done.2 = bf16[2,192,1280]{2,1,0:T(8,128)(2,1)S(1)} collective-permute-done((bf16[2,192,1280]{2,1,0:T(8,128)(2,1)}, bf16[2,192,1280]{2,1,0:T(8,128)(2,1)S(1)}, u32[]{:S(2)}, u32[]{:S(2)}) %collective-permute-start.2) | collective-permute-done | bytes 983072 | tf_op jit(solution)/shard_map/ppermute | solution.py:536
  171.2 15.7 %recurrent_forward.1 = (bf16[2,256,1280]{2,1,0:T(8,128)(2,1)S(1)}, f32[2,256,1280]{2,1,0:T(8,128)}, f32[2,256,1280]{2,1,0:T(8,128)}, f32[2,256,1280]{2,1,0:T(8,1...) custom-call(bf16[2,256,1280]{2,1,0:T(8,128)(2,1)S(1)} %bitcast.207, f32[2,8,1280]{2,1,0:T(8,128)S(1)} %pad_convert_fusion.halo_ref, ...), custom_call_target="tpu_custom_call" | custom-call | flops 1 | bytes 1 | tf_op jit(solution)/shard_map/recurrent_forward/pallas_call | solution.py:153
  232.8 16.7 %collective-permute-done.13 = bf16[4,160,1280]{2,1,0:T(8,128)(2,1)S(1)} collective-permute-done((bf16[4,160,1280]{2,1,0:T(8,128)(2,1)}, bf16[4,160,1280]{2,1,0:T(8,128)(2,1)S(1)}, u32[]{:S(2)}, u32[]{:S(2)}) %collective-permute-start.13) | collective-permute-done | bytes 1638432 | tf_op jit(solution)/shard_map/ppermute | solution.py:536
  281.4 29.0 %collective-permute-done.18.refs_0_ = bf16[256,2560]{1,0:T(8,128)(2,1)S(1)} collective-permute-done((bf16[256,2560]{1,0:T(8,128)(2,1)S(1)}, bf16[256,2560]{1,0:T(8,128)(2,1)S(1)}, u32[]{:S(2)}, u32[]{:S(2)}) %collective-permute-start.18) | collective-permute-done | bytes 1310752 | tf_op jit(solution)/shard_map/ppermute | solution.py:536
  313.5 14.2 %collective-permute-done.20.refs_1_ = bf16[128,2560]{1,0:T(8,128)(2,1)S(1)} collective-permute-done((bf16[128,2560]{1,0:T(8,128)(2,1)S(1)}, bf16[128,2560]{1,0:T(8,128)(2,1)S(1)}, u32[]{:S(2)}, u32[]{:S(2)}) %collective-permute-start.20) | collective-permute-done | bytes 655392 | tf_op jit(solution)/shard_map/ppermute | solution.py:536
  332.4 29.3 %collective-permute-done.27 = bf16[256,2560]{1,0:T(8,128)(2,1)S(1)} collective-permute-done((bf16[256,2560]{1,0:T(8,128)(2,1)S(1)}, bf16[256,2560]{1,0:T(8,128)(2,1)S(1)}, u32[]{:S(2)}, u32[]{:S(2)}) %collective-permute-start.27) | collective-permute-done | bytes 1310752 | tf_op jit(solution)/shard_map/ppermute | solution.py:536
  388.1 14.6 %all-gather.6.cloned.1.call-done = bf16[4,640,3072]{2,1,0:T(8,128)(2,1)} async-done(((bf16[4,160,3072]{2,1,0:T(8,128)(2,1)}), bf16[4,640,3072]{2,1,0:T(8,128)(2,1)}) %all-gather.6.cloned.1.call-update) | async-done | bytes 15728656 | tf_op jit(solution)/shard_map/all_gather | solution.py:664
  402.6 39.9 %feed_forward.1 = (bf16[2048,2560]{1,0:T(8,128)(2,1)}, bf16[2048,1024]{1,0:T(8,128)(2,1)}, f32[2048,1024]{1,0:T(8,128)}, f32[2048,1024]{1,0:T(8,128)}) custom-call(bf16[256,2560]{1,0:T(8,128)(2,1)} %copy-done.26, bf16[128,2560]{1,0:T(8,128)(2,1)} %copy-done.70, bf16[128,2560]{1,0:T(8,128)(2,1)} %copy-done.71, bf16[256,2560]{1,0:T(8,128)(2,1)} %copy-done.27, ...), custom_call_target="tpu_custom_call" | custom-call | flops 1 | bytes 1 | tf_op jit(solution)/shard_map/feed_forward/pallas_call | solution.py:392
  442.5 15.7 %weight_grad.2 = bf16[2560,1024]{1,0:T(8,128)(2,1)} custom-call(bf16[2048,2560]{1,0:T(8,128)(2,1)} %constant_dynamic-update-slice_fusion.x_ref.fg_ref, bf16[2048,1024]{1,0:T(8,128)(2,1)} %get-tuple-element.298.g_ref.h_ref), custom_call_target="tpu_custom_call" | custom-call | flops 1 | bytes 1 | tf_op jit(solution)/shard_map/weight_grad/pallas_call | solution.py:470
  458.3 45.7 %feed_backward.1 = (bf16[2048,2048]{1,0:T(8,128)(2,1)}, bf16[1024,2560]{1,0:T(8,128)(2,1)}, bf16[1024,2560]{1,0:T(8,128)(2,1)}) custom-call(bf16[2048,2560]{1,0:T(8,128)(2,1)} %constant_dynamic-update-slice_fusion.x_ref.fg_ref, f32[2048,1024]{1,0:T(8,128)} %get-tuple-element.271.gate_ref, f32[2048,1024]{1,0:T(8,128)} %get-tuple-element.272.up_ref, ...), custom_call_target="tpu_custom_call" | custom-call | flops 1 | bytes 1 | tf_op jit(solution)/shard_map/feed_backward/pallas_call | solution.py:426
  520.2 28.1 %weight_grad.3 = bf16[2560,2048]{1,0:T(8,128)(2,1)} custom-call(bf16[2048,2560]{1,0:T(8,128)(2,1)} %get-tuple-element.287.x_ref, bf16[2048,2048]{1,0:T(8,128)(2,1)} %get-tuple-element.288.g_ref), custom_call_target="tpu_custom_call" | custom-call | flops 1 | bytes 1 | tf_op jit(solution)/shard_map/weight_grad/pallas_call | solution.py:470
  554.5 18.3 %feed_down.1 = (bf16[1024,2560]{1,0:T(8,128)(2,1)}, bf16[1024,2560]{1,0:T(8,128)(2,1)}) custom-call(bf16[2048,1024]{1,0:T(8,128)(2,1)} %get-tuple-element.298.g_ref.h_ref, bf16[2560,3072]{1,0:T(8,128)(2,1)} %bitcast.216), custom_call_target="tpu_custom_call" | custom-call | flops 1 | bytes 1 | tf_op jit(solution)/shard_map/feed_down/pallas_call | solution.py:450
  603.3 13.7 %recurrent_adjoint.1 = (bf16[2,256,1280]{2,1,0:T(8,128)(2,1)S(1)}, f32[2,256,1280]{2,1,0:T(8,128)S(1)}, f32[2,256,1280]{2,1,0:T(8,128)}) custom-call(f32[2,256,1280]{2,1,0:T(8,128)} %fusion.54.rg_ref, f32[2,256,1280]{2,1,0:T(8,128)} %get-tuple-element.593.gelu_ref, f32[2,256,1280]{2,1,0:T(8,128)} %get-tuple-element.315.a_ref, ...), custom_call_target="tpu_custom_call" | custom-call | flops 1 | bytes 1 | tf_op jit(solution)/shard_map/recurrent_adjoint/pallas_call | solution.py:195
  646.4 13.5 %recurrent_backward.1 = (f32[2,256,1280]{2,1,0:T(8,128)}, f32[2,8,1280]{2,1,0:T(8,128)S(1)}, f32[8,1280]{1,0:T(8,128)S(1)}, bf16[2,256,1280]{2,1,0:T(8,128)(2,1)S(1)}) custom-call(f32[2,256,1280]{2,1,0:T(8,128)} %copy-done.2, f32[2,256,1280]{2,1,0:T(8,128)} %get-tuple-element.341.tsum_ref, f32[2,8,1280]{2,1,0:T(8,128)S(1)} %broadcast_in_dim.164.leave_ref, ...), custom_call_target="tpu_custom_call" | custom-call | flops 1 | bytes 1 | tf_op jit(solution)/shard_map/recurrent_backward/pallas_call | solution.py:274
  726.0 12.0 %collective-permute-done.59 = bf16[640,640]{1,0:T(8,128)(2,1)S(1)} collective-permute-done((bf16[640,640]{1,0:T(8,128)(2,1)S(1)}, bf16[640,640]{1,0:T(8,128)(2,1)S(1)}, u32[]{:S(2)}, u32[]{:S(2)}) %collective-permute-start.59) | collective-permute-done | bytes 819232 | tf_op jit(solution)/shard_map/ppermute | solution.py:536
  752.2 19.4 %collective-permute-done.57 = bf16[1280,640]{1,0:T(8,128)(2,1)} collective-permute-done((bf16[1280,640]{1,0:T(8,128)(2,1)}, bf16[1280,640]{1,0:T(8,128)(2,1)}, u32[]{:S(2)}, u32[]{:S(2)}) %collective-permute-start.57) | collective-permute-done | bytes 1638432 | tf_op jit(solution)/shard_map/ppermute | solution.py:536
  782.8 13.0 %collective-permute-done.70 = bf16[640,640]{1,0:T(8,128)(2,1)S(1)} collective-permute-done((bf16[640,640]{1,0:T(8,128)(2,1)S(1)}, bf16[640,640]{1,0:T(8,128)(2,1)S(1)}, u32[]{:S(2)}, u32[]{:S(2)}) %collective-permute-start.70) | collective-permute-done | bytes 819232 | tf_op jit(solution)/shard_map/ppermute | solution.py:536
  801.6 31.8 %collective-permute-done.68 = bf16[1536,640]{1,0:T(8,128)(2,1)} collective-permute-done((bf16[1536,640]{1,0:T(8,128)(2,1)}, bf16[1536,640]{1,0:T(8,128)(2,1)}, u32[]{:S(2)}, u32[]{:S(2)}) %collective-permute-start.68) | collective-permute-done | bytes 1966112 | tf_op jit(solution)/shard_map/ppermute | solution.py:536
  879.8 12.8 %collective-permute-done.72 = bf16[768,640]{1,0:T(8,128)(2,1)S(1)} collective-permute-done((bf16[768,640]{1,0:T(8,128)(2,1)S(1)}, bf16[768,640]{1,0:T(8,128)(2,1)S(1)}, u32[]{:S(2)}, u32[]{:S(2)}) %collective-permute-start.72) | collective-permute-done | bytes 983072 | tf_op jit(solution)/shard_map/ppermute | solution.py:536
  908.8 12.8 %collective-permute-done.76 = bf16[160,2048]{1,0:T(8,128)(2,1)S(1)} collective-permute-done((bf16[160,2048]{1,0:T(8,128)(2,1)S(1)}, bf16[160,2048]{1,0:T(8,128)(2,1)S(1)}, u32[]{:S(2)}, u32[]{:S(2)}) %collective-permute-start.76) | collective-permute-done | bytes 655392 | tf_op jit(solution)/shard_map/ppermute | solution.py:536
  929.6 13.8 %reduce-scatter.9.cloned.1.call-done = bf16[1,192,1280]{2,1,0:T(8,128)(2,1)} async-done(((bf16[4,192,1280]{2,1,0:T(8,128)(2,1)}), bf16[1,192,1280]{2,1,0:T(8,128)(2,1)}) %reduce-scatter.9.cloned.1.call-update) | async-done | bytes 491536 | tf_op jit(solution)/shard_map/reduce_scatter | solution.py:880
  (552 shorter events, 438.5 us)
Async XLA Ops:
  7.2 52.1 %all-gather.10.cloned.1.call-start = ((), (), s32[]{:S(2)}) async-start(), calls=%async_computation.10 | async-start | bytes 2457600 | tf_op jit(solution)/shard_map/all_gather | solution.py:717
  12.9 121.6 %all-gather.8.cloned.1.call-start = ((), (), s32[]{:S(2)}) async-start(), calls=%async_computation.9 | async-start | bytes 4096000 | tf_op jit(solution)/shard_map/all_gather | solution.py:718
  13.0 52.9 %collective-permute-start.5 = (s32[2,3]{1,0:T(2,128)S(1)}, s32[2,3]{1,0:T(2,128)S(1)}, u32[]{:S(2)}, u32[]{:S(2)}) collective-permute-start(s32[2,3]{1,0:T(2,128)S(1)} %slice.492), channel_id=1, source_target_pairs={{0,2},{2,4},{4,6},{1,3},{3,5},{5,7},{8,10},{10,12},{12,14},{9,11},... | collective-permute-start | bytes 80 | tf_op jit(solution)/shard_map/ppermute | solution.py:26
  26.0 41.5 %collective-permute-start.36 = (bf16[160,3072]{1,0:T(8,128)(2,1)}, bf16[160,3072]{1,0:T(8,128)(2,1)}, u32[]{:S(2)}, u32[]{:S(2)}) collective-permute-start(bf16[160,3072]{1,0:T(8,128)(2,1)} %pad_maximum_fusion.16), channel_id=1, source_target_pairs={{0,8},{8,0},{16,24},{24,16},{1,9},{9,1},{17,25},{25,17},{2,10},{10... | collective-permute-start | bytes 2949128 | tf_op jit(solution)/shard_map/ppermute | solution.py:536
  28.5 374.1 %all-gather.6.cloned.1.call-start = ((), (), s32[]{:S(2)}) async-start(), calls=%async_computation.4 | async-start | bytes 19660800 | tf_op jit(solution)/shard_map/all_gather | solution.py:664
  59.3 45.9 %collective-permute-start = (bf16[4,192,1280]{2,1,0:T(8,128)(2,1)}, bf16[4,192,1280]{2,1,0:T(8,128)(2,1)S(1)}, u32[]{:S(2)}, u32[]{:S(2)}) collective-permute-start(bf16[4,192,1280]{2,1,0:T(8,128)(2,1)} %bitcast.257), channel_id=1, source_target_pairs={{0,8},{8,0},{16,24},{24,16},{1,9},{9,1},{17,25},{25,17},{2,10},{10... | collective-permute-start | bytes 5898248 | tf_op jit(solution)/shard_map/ppermute | solution.py:536
  60.8 65.7 %collective-permute-start.1 = (bf16[4,192,1280]{2,1,0:T(8,128)(2,1)}, bf16[4,192,1280]{2,1,0:T(8,128)(2,1)}, u32[]{:S(2)}, u32[]{:S(2)}) collective-permute-start(bf16[4,192,1280]{2,1,0:T(8,128)(2,1)} %bitcast.258), channel_id=1, source_target_pairs={{0,16},{8,24},{16,0},{24,8},{1,17},{9,25},{17,1},{25,9},{2,18},{10... | collective-permute-start | bytes 5898248 | tf_op jit(solution)/shard_map/ppermute | solution.py:536
  65.9 66.2 %collective-permute-start.38 = (bf16[160,3072]{1,0:T(8,128)(2,1)}, bf16[160,3072]{1,0:T(8,128)(2,1)}, u32[]{:S(2)}, u32[]{:S(2)}) collective-permute-start(bf16[160,3072]{1,0:T(8,128)(2,1)} %pad_maximum_fusion.18), channel_id=1, source_target_pairs={{0,24},{8,16},{16,8},{24,0},{1,25},{9,17},{17,9},{25,1},{2,26},{10... | collective-permute-start | bytes 2949128 | tf_op jit(solution)/shard_map/ppermute | solution.py:536
  134.4 490.1 %reduce-scatter.11.cloned.1.call-start = ((), (), s32[]{:S(2)}) async-start(), calls=%async_computation.8 | async-start | bytes 6553600 | tf_op jit(solution)/shard_map/reduce_scatter | solution.py:672
  458.3 375.1 %reduce-scatter.5.cloned.1.call-start = ((), (), s32[]{:S(2)}) async-start(), calls=%async_computation.5 | async-start | bytes 13107200 | tf_op jit(solution)/shard_map/reduce_scatter | solution.py:672
  549.5 349.9 %reduce-scatter.7.cloned.1.call-start = ((), (), s32[]{:S(2)}) async-start(), calls=%async_computation.6 | async-start | bytes 4096000 | tf_op jit(solution)/shard_map/reduce_scatter | solution.py:878
  601.1 41.0 %collective-permute-start.46 = (bf16[512,1280]{1,0:T(8,128)(2,1)}, bf16[512,1280]{1,0:T(8,128)(2,1)}, u32[]{:S(2)}, u32[]{:S(2)}) collective-permute-start(bf16[512,1280]{1,0:T(8,128)(2,1)} %get-tuple-element.325), channel_id=1, source_target_pairs={{0,8},{8,0},{16,24},{24,16},{1,9},{9,1},{17,25},{25,17},{2,10},{10... | collective-permute-start | bytes 3932168 | tf_op jit(solution)/shard_map/ppermute | solution.py:536
  602.7 39.4 %collective-permute-start.47 = (bf16[512,1280]{1,0:T(8,128)(2,1)}, bf16[512,1280]{1,0:T(8,128)(2,1)}, u32[]{:S(2)}, u32[]{:S(2)}) collective-permute-start(bf16[512,1280]{1,0:T(8,128)(2,1)} %get-tuple-element.326), channel_id=1, source_target_pairs={{0,16},{8,24},{16,0},{24,8},{1,17},{9,25},{17,1},{25,9},{2,18},{10... | collective-permute-start | bytes 3932168 | tf_op jit(solution)/shard_map/ppermute | solution.py:536
  639.4 46.7 %collective-permute-start.78 = (bf16[160,1024]{1,0:T(8,128)(2,1)}, bf16[160,1024]{1,0:T(8,128)(2,1)}, u32[]{:S(2)}, u32[]{:S(2)}) collective-permute-start(bf16[160,1024]{1,0:T(8,128)(2,1)} %get-tuple-element.561), channel_id=1, source_target_pairs={{0,16},{8,24},{16,0},{24,8},{1,17},{9,25},{17,1},{25,9},{2,18},{10... | collective-permute-start | bytes 983048 | tf_op jit(solution)/shard_map/ppermute | solution.py:536
  640.5 50.8 %collective-permute-start.79 = (bf16[160,1024]{1,0:T(8,128)(2,1)}, bf16[160,1024]{1,0:T(8,128)(2,1)}, u32[]{:S(2)}, u32[]{:S(2)}) collective-permute-start(bf16[160,1024]{1,0:T(8,128)(2,1)} %get-tuple-element.560), channel_id=1, source_target_pairs={{0,24},{8,16},{16,8},{24,0},{1,25},{9,17},{17,9},{25,1},{2,26},{10... | collective-permute-start | bytes 983048 | tf_op jit(solution)/shard_map/ppermute | solution.py:536
  662.1 51.7 %collective-permute-start.48 = (bf16[1280,640]{1,0:T(8,128)(2,1)}, bf16[1280,640]{1,0:T(8,128)(2,1)}, u32[]{:S(2)}, u32[]{:S(2)}) collective-permute-start(bf16[1280,640]{1,0:T(8,128)(2,1)} %get-tuple-element.330), channel_id=1, source_target_pairs={{0,8},{8,0},{16,24},{24,16},{1,9},{9,1},{17,25},{25,17},{2,10},{10... | collective-permute-start | bytes 4915208 | tf_op jit(solution)/shard_map/ppermute | solution.py:536
  663.1 50.7 %collective-permute-start.49 = (bf16[1280,640]{1,0:T(8,128)(2,1)}, bf16[1280,640]{1,0:T(8,128)(2,1)}, u32[]{:S(2)}, u32[]{:S(2)}) collective-permute-start(bf16[1280,640]{1,0:T(8,128)(2,1)} %get-tuple-element.331), channel_id=1, source_target_pairs={{0,16},{8,24},{16,0},{24,8},{1,17},{9,25},{17,1},{25,9},{2,18},{10... | collective-permute-start | bytes 4915208 | tf_op jit(solution)/shard_map/ppermute | solution.py:536
  686.1 53.1 %collective-permute-start.61 = (f32[256,2560]{1,0:T(8,128)}, f32[256,2560]{1,0:T(8,128)}, u32[]{:S(2)}, u32[]{:S(2)}) collective-permute-start(f32[256,2560]{1,0:T(8,128)} %convolution_add_fusion), channel_id=1, source_target_pairs={{0,1},{1,0},{2,3},{3,2},{4,5},{5,4},{6,7},{7,6},{8,9},{9,8},{10,11... | collective-permute-start | bytes 7864328 | tf_op jit(solution)/shard_map/ppermute | solution.py:31
  719.4 52.2 %collective-permute-start.57 = (bf16[1280,640]{1,0:T(8,128)(2,1)}, bf16[1280,640]{1,0:T(8,128)(2,1)}, u32[]{:S(2)}, u32[]{:S(2)}) collective-permute-start(bf16[1280,640]{1,0:T(8,128)(2,1)} %get-tuple-element.383), channel_id=1, source_target_pairs={{0,8},{8,0},{16,24},{24,16},{1,9},{9,1},{17,25},{25,17},{2,10},{10... | collective-permute-start | bytes 4915208 | tf_op jit(solution)/shard_map/ppermute | solution.py:536
  720.0 51.6 %collective-permute-start.58 = (bf16[1280,640]{1,0:T(8,128)(2,1)}, bf16[1280,640]{1,0:T(8,128)(2,1)}, u32[]{:S(2)}, u32[]{:S(2)}) collective-permute-start(bf16[1280,640]{1,0:T(8,128)(2,1)} %get-tuple-element.384), channel_id=1, source_target_pairs={{0,16},{8,24},{16,0},{24,8},{1,17},{9,25},{17,1},{25,9},{2,18},{10... | collective-permute-start | bytes 4915208 | tf_op jit(solution)/shard_map/ppermute | solution.py:536
  776.5 56.8 %collective-permute-start.68 = (bf16[1536,640]{1,0:T(8,128)(2,1)}, bf16[1536,640]{1,0:T(8,128)(2,1)}, u32[]{:S(2)}, u32[]{:S(2)}) collective-permute-start(bf16[1536,640]{1,0:T(8,128)(2,1)} %get-tuple-element.406), channel_id=1, source_target_pairs={{0,8},{8,0},{16,24},{24,16},{1,9},{9,1},{17,25},{25,17},{2,10},{10... | collective-permute-start | bytes 5898248 | tf_op jit(solution)/shard_map/ppermute | solution.py:536
  777.6 55.8 %collective-permute-start.69 = (bf16[1536,640]{1,0:T(8,128)(2,1)}, bf16[1536,640]{1,0:T(8,128)(2,1)}, u32[]{:S(2)}, u32[]{:S(2)}) collective-permute-start(bf16[1536,640]{1,0:T(8,128)(2,1)} %get-tuple-element.407), channel_id=1, source_target_pairs={{0,16},{8,24},{16,0},{24,8},{1,17},{9,25},{17,1},{25,9},{2,18},{10... | collective-permute-start | bytes 5898248 | tf_op jit(solution)/shard_map/ppermute | solution.py:536
  778.6 58.1 %collective-permute-start.64 = (f32[12,1280]{1,0:T(8,128)S(1)}, f32[12,1280]{1,0:T(8,128)S(1)}, u32[]{:S(2)}, u32[]{:S(2)}) collective-permute-start(f32[12,1280]{1,0:T(8,128)S(1)} %fusion.48), channel_id=1, source_target_pairs={{0,16},{8,24},{16,0},{24,8},{1,17},{9,25},{17,1},{25,9},{2,18},{10... | collective-permute-start | bytes 184328 | tf_op jit(solution)/shard_map/ppermute | solution.py:536
  833.4 109.9 %reduce-scatter.9.cloned.1.call-start = ((), (), s32[]{:S(2)}) async-start(), calls=%async_computation.7 | async-start | bytes 2457600 | tf_op jit(solution)/shard_map/reduce_scatter | solution.py:880
  (155 other events, 2488.1 us)
Sparse Core Ops, SparseCore 0:
  13.0 46.2 all-gather.9
  61.4 64.4 all-gather.7
  134.5 268.1 all-gather.5
  458.4 93.9 reduce-scatter.10
  554.6 180.6 reduce-scatter.4
  833.5 65.7 reduce-scatter.6
  901.7 41.6 reduce-scatter.8

commit v4 on v3

--- a/solution.py
+++ b/solution.py
@@ -484,6 +484,38 @@
     )(x, grad, *([] if into is None else [into]))
 
 
+def unit_terms(pairs, order):
+    count = pairs[0][0].shape[0] // 2
+    units, width = pairs[0][0].shape[1], pairs[0][1].shape[0]
+    refs = 2 * len(pairs)
+
+    def body(order_ref, *rest):
+        total = dot(rest[0][...], rest[1][...], ((1,), (1,)))
+        for n in range(2, refs, 2):
+            total = total + dot(rest[n][...], rest[n + 1][...], ((1,), (1,)))
+        for n in range(2):
+
+            @pl.when(pl.program_id(0) == n)
+            def _():
+                rest[refs + n][...] = total
+
+    rows = pl.BlockSpec((count, units), lambda n, order_ref: (order_ref[n], 0))
+    weights = pl.BlockSpec((width, units), lambda n, order_ref: (0, 0), pipeline_mode=pl.Buffered(1))
+    return pl.pallas_call(
+        body,
+        grid_spec=pltpu.PrefetchScalarGridSpec(
+            num_scalar_prefetch=1,
+            grid=(2,),
+            in_specs=[rows, weights] * len(pairs),
+            out_specs=[pl.BlockSpec((count, width), lambda n, order_ref: (0, 0))] * 2,
+        ),
+        out_shape=[jax.ShapeDtypeStruct((count, width), F32)] * 2,
+        compiler_params=feed_params(),
+        cost_estimate=cost(),
+        name="unit_terms",
+    )(order, *[v for pair in pairs for v in pair])
+
+
 ORDER = (1, 3, 2, 0)
 
 
@@ -532,6 +564,18 @@
     )(places, x, grad, *([extra] if more else []))
 
 
+def carried(own, axis, step):
+    near_map = shifted(own, axis, step)
+    both = jnp.stack([near_map[0] * own[0], own[0] * near_map[1] + own[1]])
+    result, reach = near_map, 2
+    while reach < lax.axis_size(axis):
+        far = shifted(both, axis, step * reach)
+        result = jnp.stack([result[0] * far[0], result[0] * far[1] + result[1]])
+        both = jnp.stack([both[0] * far[0], both[0] * far[1] + both[1]])
+        reach *= 2
+    return result[1]
+
+
 def cross(x, axis, r):
     return lax.ppermute(x, axis, [(i, i ^ r) for i in range(lax.axis_size(axis))])
 
@@ -614,15 +658,18 @@
     return jnp.concatenate([left, right], axis=1)
 
 
-def gather_in_turn(arrays):
+def gather_in_turn(arrays, ready):
     if lax.axis_size("fsdp") != SQUARE:
-        return [lax.all_gather(x, "fsdp", axis=0) for x in arrays]
+        return [lax.all_gather(x, "fsdp", axis=0) for x in arrays], ready
     results = []
     for x in arrays:
         if results:
             x, results[-1] = together(x, results[-1])
-        results.append(near(x, "fsdp"))
-    return results
+        got = near_blocks(x, "fsdp")
+        if not results:
+            got, ready = together(got, ready)
+        results.append([x] + got + [far_block(got, "fsdp")])
+    return results, ready
 
 
 def rows_of(blocks, start, stop):
@@ -650,7 +697,7 @@
         here = (slice(start * rows, stop * rows), slice(half * cols, (half + 1) * cols))
         return low(wide(first[here]) + wide(theirs[here]))
 
-    return together(part(0, 2, 0), part(1, 3, 1), part(2, 3, 0), part(0, 1, 1), part(3, 4, 0), part(3, 4, 1))
+    return [part(0, 2, 0), part(1, 3, 1)], [part(2, 3, 0), part(0, 1, 1), part(3, 4, 0), part(3, 4, 1)]
 
 
 def trade(pieces):
@@ -722,13 +769,16 @@
         return lambda p: lax.dynamic_slice_in_dim(w, p * share, share, 1)
 
     down, gate_in, up_in = cut(contract), cut(expand[:, 0]), cut(expand[:, 1])
-    w_feed = gather_feed(trade(lambda p: jnp.concatenate([gate_in(p), up_in(p), down(p)], axis=1)))
+    local_feed = trade(lambda p: jnp.concatenate([gate_in(p), up_in(p), down(p)], axis=1))
 
     mask_rows = token_mask.astype(F32).reshape(tokens, 1)
     out_grad = own(cotangent.reshape(tokens, width)).astype(F32) * own(mask_rows)
     local_feed_grad = out_grad.astype(BF16)
 
-    got_first, got_gelu, got_outlet = gather_in_turn([first, second[:, :depth], second[:, depth:]])
+    (got_first, got_gelu, got_outlet), local_feed = gather_in_turn(
+        [first, second[:, :depth], second[:, depth:]], local_feed
+    )
+    w_feed = gather_feed(local_feed)
     w_branch = rows_of(got_first, 0, depth)
     blocks = rows_of(got_first, depth, first.shape[1]).reshape(HEAD_W, 2, units).transpose(1, 0, 2)
     w_gelu = rows_of(got_gelu, 0, depth)
@@ -763,10 +813,7 @@
     halo = jnp.pad(x_before, ((0, 0), (5, 0), (0, 0))).astype(F32)
     conv_low, r, i, coef, prod, total = recurrent_forward(x_branch, halo, masks, params, blocks)
     ends = jnp.stack([prod[:, -1], total[:, -1]])
-    entering = jnp.zeros((rows, units), F32)
-    for by in range(ctx - 1, 0, -1):
-        end = shifted(ends, "ctx", by)
-        entering = end[1] + end[0] * entering
+    entering = carried(ends, "ctx", 1)
     state_in = jnp.broadcast_to(entering[:, None], (rows, 8, units))
     states = total + prod * entering[:, None]
     recurrent = (states * jax.nn.gelu(gelu_in, approximate=True)).astype(BF16).reshape(tokens, units)
@@ -790,8 +837,10 @@
 
     group = token_axes()[0]
     theirs = swap(n2g_other, "tp")
-    parts, expand_low = after(token_parts(n2g_own, theirs), expand_low)
+    parts, kept = token_parts(n2g_own, theirs)
+    parts, expand_low = after(parts, expand_low)
     got = near_send(parts, group)
+    parts = parts + kept
     expand_all = weight_grad(normed_two, expand_low)
     got, expand_all = after(got, expand_all)
     sums, hidden = after(near_middle(parts, got), hidden)
@@ -799,6 +848,7 @@
     feed_own, feed_other = feed_down(hidden, w_feed)
     more, (feed_own, feed_other) = after(more, (feed_own, feed_other))
     normed_two_grad = near_last(parts, got, more)
+    expand_all, down_part = after(expand_all, down_part)
     expand_part = scatter_feed(expand_all)
     feed_theirs = swap(feed_other, "tp")
 
@@ -808,82 +858,85 @@
 
     square = lax.axis_size("fsdp") == SQUARE
     places = lax.axis_index("fsdp").astype(jnp.int32) ^ jnp.array(ORDER, jnp.int32)
-    rec_grad = dot(branch_grad, w_outlet, ((1,), (0,))).reshape(rows, length, units)
-    feed_parts, rec_grad = after(token_parts(feed_own, feed_theirs), rec_grad)
+    feed_parts, feed_kept = token_parts(feed_own, feed_theirs)
+    feed_parts, branch_grad = after(feed_parts, branch_grad)
     feed_got = near_send(feed_parts, group)
-    gelu_grad, tprod, tsum = recurrent_adjoint(rec_grad, gelu_in, coef, prod, total, state_in)
-    heads = jnp.stack([coef[:, 0] * tprod[:, 0], coef[:, 0] * tsum[:, 0]])
-    leaving = jnp.zeros((rows, units), F32)
-    for by in range(ctx - 1, 0, -1):
-        head = shifted(heads, "ctx", -by)
-        leaving = head[1] + head[0] * leaving
-    leaving = jnp.broadcast_to(leaving[:, None], (rows, 8, units))
-    gelu_low = gelu_grad.reshape(tokens, units)
-    branch_grad, gelu_low = after(branch_grad, gelu_low)
+    feed_parts = feed_parts + feed_kept
     if square:
         outlet_parts = weight_grad_parts(branch_grad, recurrent, places)
     else:
         outlet_parts = weight_grad(branch_grad, recurrent)
-    outlet_parts, tprod, feed_got = together(outlet_parts, tprod, feed_got)
-    feed_sums = near_middle(feed_parts, feed_got)
-    feed_sums, tprod = after(feed_sums, tprod)
-    feed_more = near_second(feed_sums, group)
-    if square:
-        outlet_got = near_send(outlet_parts, "fsdp")
-    branch_x, before, small, blocks_grad = recurrent_backward(
-        tprod, tsum, leaving, prod, total, state_in, coef, r, i, conv_low, x_branch, halo, masks, params, blocks
-    )
-    gelu_low, small = after(gelu_low, small)
+    outlet_parts, branch_grad = after(outlet_parts, branch_grad)
+    outlet_got = near_send(outlet_parts, "fsdp") if square else outlet_parts
+    rec_grad = dot(branch_grad, w_outlet, ((1,), (0,))).reshape(rows, length, units)
+    gelu_grad, tprod, tsum = recurrent_adjoint(rec_grad, gelu_in, coef, prod, total, state_in)
+    gelu_low = gelu_grad.reshape(tokens, units)
     if square:
         gelu_parts = weight_grad_parts(normed, gelu_low, places)
     else:
         gelu_parts = weight_grad(normed, gelu_low)
+    feed_got, outlet_got, gelu_parts, tprod, tsum = together(feed_got, outlet_got, gelu_parts, tprod, tsum)
+    feed_sums = near_middle(feed_parts, feed_got)
+    if square:
+        outlet_sums, gelu_parts, tprod = together(near_middle(outlet_parts, outlet_got), gelu_parts, tprod)
+        outlet_more, gelu_got = near_second(outlet_sums, "fsdp"), near_send(gelu_parts, "fsdp")
+    heads = jnp.stack([coef[:, 0] * tprod[:, 0], coef[:, 0] * tsum[:, 0]])
+    leaving = carried(heads, "ctx", -1)
+    leaving = jnp.broadcast_to(leaving[:, None], (rows, 8, units))
+    branch_x, before, small, blocks_grad = recurrent_backward(
+        tprod, tsum, leaving, prod, total, state_in, coef, r, i, conv_low, x_branch, halo, masks, params, blocks
+    )
     from_next = shifted(before[:, 5:], "ctx", -1)
     branch_x = branch_x + jnp.pad(from_next, ((0, 0), (length - 3, 0), (0, 0)))
-    branch_low, gelu_parts = together(branch_x.astype(BF16).reshape(tokens, units), gelu_parts)
+    branch_low = branch_x.astype(BF16).reshape(tokens, units)
     blocks_rows = blocks_grad.transpose(1, 0, 2).reshape(2 * HEAD_W, units)
     if square:
         branch_parts = weight_grad_parts(normed, branch_low, places, blocks_rows)
-        outlet_got, branch_parts, feed_more = together(outlet_got, branch_parts, feed_more)
-        outlet_sums, gelu_parts = after(near_middle(outlet_parts, outlet_got), gelu_parts)
-        outlet_more, gelu_got = near_second(outlet_sums, "fsdp"), near_send(gelu_parts, "fsdp")
+        gelu_got, outlet_more, branch_parts, branch_low = together(gelu_got, outlet_more, branch_parts, branch_low)
+        gelu_sums, branch_parts, branch_low = together(near_middle(gelu_parts, gelu_got), branch_parts, branch_low)
+        gelu_more, branch_got = near_second(gelu_sums, "fsdp"), near_send(branch_parts, "fsdp")
+        outlet_part = low(near_last(outlet_parts, outlet_got, outlet_more))
     else:
         branch_parts = weight_grad(normed, branch_low)
-
-    def input_terms(pick):
-        return dot(pick(branch_low), w_branch, ((1,), (1,))) + dot(pick(gelu_low), w_gelu, ((1,), (1,)))
-
-    theirs = input_terms(other)
-    normed_grad = input_terms(own) + swap(theirs, "tp")
+        outlet_part, gelu_part = [
+            lax.psum_scatter(v, "fsdp", scatter_dimension=0, tiled=True) for v in (outlet_got, gelu_parts)
+        ]
+        branch_got = branch_parts
+    theirs, ours = unit_terms(
+        [(branch_low, w_branch), (gelu_low, w_gelu)], jnp.stack([1 - mine, mine]).astype(jnp.int32)
+    )
+    def scatter_ctx(v):
+        return lax.psum_scatter(v, "ctx", scatter_dimension=0, tiled=False)
+
+    outlet_part, expand_part = after(outlet_part, expand_part)
+    outlet_part = scatter_ctx(outlet_part.reshape(ctx, depth, units))
+    if square:
+        gelu_more, branch_got, theirs, ours, outlet_part = together(gelu_more, branch_got, theirs, ours, outlet_part)
+        gelu_part = low(near_last(gelu_parts, gelu_got, gelu_more))
+        late_sums, gelu_part = after(near_middle(branch_parts, branch_got), gelu_part)
+        late_more = near_second(late_sums, "fsdp")
+    else:
+        gelu_part, outlet_part = after(gelu_part, outlet_part)
+    gelu_part = scatter_ctx(gelu_part.reshape(ctx, depth, units))
+    if square:
+        late = low(near_last(branch_parts, branch_got, late_more))
+        late = [late[: ctx * depth], late[ctx * depth :]]
+    else:
+        late = [lax.psum_scatter(v, "fsdp", scatter_dimension=0, tiled=True) for v in (branch_got, blocks_rows)]
+    late = jnp.concatenate([v.reshape(ctx, -1, units) for v in late], axis=1)
+    normed_grad = ours + swap(theirs, "tp")
     norm_part, gain_one = rms_back(own(x), own(inverse_one), norm_gains[0], normed_grad)
     input_own = residual_grad + norm_part
-    if square:
-        gelu_got, outlet_more, input_own = together(gelu_got, outlet_more, input_own)
-        early = [low(near_last(outlet_parts, outlet_got, outlet_more))]
-        gelu_sums, branch_parts = together(near_middle(gelu_parts, gelu_got), branch_parts)
-        gelu_more, branch_got = near_second(gelu_sums, "fsdp"), near_send(branch_parts, "fsdp")
-        early.append(low(near_last(gelu_parts, gelu_got, gelu_more)))
-    else:
-        early = [lax.psum_scatter(v, "fsdp", scatter_dimension=0, tiled=True) for v in (outlet_parts, gelu_parts)]
-    early = jnp.concatenate([v.reshape(ctx, depth, units) for v in early], axis=2)
-    early, expand_part = after(early, expand_part)
-    if square:
-        branch_got, early = together(branch_got, early)
-        late = low(near_last(branch_parts, branch_got, near_second(near_middle(branch_parts, branch_got), "fsdp")))
-        late = [late[: ctx * depth], late[ctx * depth :]]
-    else:
-        late = [lax.psum_scatter(v, "fsdp", scatter_dimension=0, tiled=True) for v in (branch_parts, blocks_rows)]
-    late = jnp.concatenate([v.reshape(ctx, -1, units) for v in late], axis=1)
-
-    early = lax.psum_scatter(early, "ctx", scatter_dimension=0, tiled=False)
-    late, early = after(late, early)
-    late = wide(lax.psum_scatter(late, "ctx", scatter_dimension=0, tiled=False))
+    late, gelu_part, expand_part, down_part, input_own, gain_one, feed_sums = together(
+        late, gelu_part, expand_part, down_part, input_own, gain_one, feed_sums
+    )
+    late = wide(scatter_ctx(late))
+    input_grad = join(input_own).reshape(rows, length, width)
+    feed_out = near_last(feed_parts, feed_got, near_second(feed_sums, group))
+    block_output = join(low(residual + feed_out)).reshape(rows, length, width)
 
     down_part = to_owners(down_part)
     expand_part = to_owners(expand_part)
-    feed_out = near_last(feed_parts, feed_got, feed_more)
-    block_output = join(low(residual + feed_out)).reshape(rows, length, width)
-    input_grad = join(input_own).reshape(rows, length, width)
 
     def columns(part, n):
         return jnp.concatenate([part[p, :, n * share : (n + 1) * share] for p in range(SQUARE)], axis=1)[
@@ -904,9 +957,9 @@
         small[4],
         small[5:7],
         small[7],
-        jnp.stack([wide(early[:, units:]), late[:depth]], axis=1),
+        jnp.stack([wide(gelu_part), late[:depth]], axis=1),
         late[depth:].reshape(gate_rows, 2, units),
-        wide(early[:, :units]),
+        wide(outlet_part),
         expand_grad,
         contract_grad,
     )

time: 967 us -> 950 us (0.982)
  matrix products: 46.9 us -> 27.3 us
    dot_general x9 -> x5, matrix products: 46.9 us -> 27.3 us  [dot(): return lax.dot_general(a, b, (dims, ((), ())), preferred_element_type=F32)]
    ppermute x9 -> x7, waiting for transfers between devices: 1.69 us -> 17.9 us  [shifted(): return lax.ppermute(x, axis, pairs)]
    pallas_call x0 -> x1, Pallas kernels: none -> 15.7 us  [unit_terms(): pl.pallas_call(body, grid_spec=pltpu.PrefetchScalarGridSpec(num_scalar_pr...]
    reduce_scatter x2 -> x3, waiting for transfers between devices: 15.7 us -> 1.65 us  [scatter_ctx(): return lax.psum_scatter(v, 'ctx', scatter_dimension=0, tiled=False)]
    ppermute x54, waiting for transfers between devices: 311 us -> 298 us  [cross(): lax.ppermute(x, axis, [(i, i ^ r) for i in range(lax.axis_size(axis))])]
    ppermute x9 -> x7, starting transfers between devices: 19.3 us -> 25.1 us  [shifted(): return lax.ppermute(x, axis, pairs)]
    convert_element_type x15 -> x11, other arithmetic: 30.9 us -> 27.9 us  [low(): return v.astype(BF16)]
    unnamed x204 -> x176, local copies, waits for them, and re-layouts: 28.4 us -> 30.9 us
  transfers between devices with their start and end apart: 87 -> 86, of which waited for: 42 -> 45; matrix products, arithmetic and copies ran while one was open for 24% -> 22% of each run, Pallas kernels for 17% -> 19%
where the time goes in v4:
time: 950 us; the launch traced here: 938 us
  waiting for transfers between devices  375 us (39%)
  Pallas kernels  229 us (24%)
  local copies, waits for them, and re-layouts  103 us (11%)
  other arithmetic  99.3 us (10%)
  starting transfers between devices  89.5 us (9%)
  matrix products  27.3 us (3%)
  between operations  16.1 us (2%)
    ppermute x54, waiting for transfers between devices, cross(): lax.ppermute(x, axis, [(i, i ^ r) for i in range(lax.axis_size(axis))])  298 us
    ppermute x54, starting transfers between devices, cross(): lax.ppermute(x, axis, [(i, i ^ r) for i in range(lax.axis_size(axis))])  61.8 us
    pallas_call x1, Pallas kernels, feed_backward(): pl.pallas_call(body, grid=(tiles,), in_specs=[tokens_spec(width, tiles, m...  45.8 us
    pallas_call x2, Pallas kernels, weight_grad(): pl.pallas_call(body, grid=(width // deep,), in_specs=[pl.BlockSpec((count...  43.8 us
    pallas_call x3, Pallas kernels, weight_grad_parts(): pl.pallas_call(body, grid_spec=pltpu.PrefetchScalarGridSpec(num_scalar_pr...  31.4 us
    pallas_call x1, Pallas kernels, feed_forward(): pl.pallas_call(body, grid=(tiles,), in_specs=[pl.BlockSpec(memory_space=p...  31.2 us
    unnamed x176, local copies, waits for them, and re-layouts  30.9 us
    dynamic_update_slice x29, local copies, waits for them, and re-layouts, place(): lax.dynamic_update_slice(whole, piece[None], (me ^ r, at) + (0,) * (piece...  29.3 us
  transfers between devices with their start and end apart: 86, of which 45 were waited for; matrix products, arithmetic and copies ran while one was open for 22% of the time, Pallas kernels for 19%

profile of v4, /device:TPU:0, one launch (start us, length us, event | category | flops | bytes accessed | tf_op | source)
XLA Modules:
  0.0 938.2 jit_solution(6741936196014486517)
XLA Ops:
  40.4 18.9 %all-gather.10.cloned.1.call-done = bf16[768,1280]{1,0:T(8,128)(2,1)} async-done(((bf16[192,1280]{1,0:T(8,128)(2,1)}), bf16[768,1280]{1,0:T(8,128)(2,1)}) %all-gather.10.cloned.1.call-update) | async-done | bytes 1966096 | tf_op jit(solution)/shard_map/all_gather | solution.py:764
  74.7 34.1 %collective-permute-done = bf16[4,192,1280]{2,1,0:T(8,128)(2,1)S(1)} collective-permute-done((bf16[4,192,1280]{2,1,0:T(8,128)(2,1)}, bf16[4,192,1280]{2,1,0:T(8,128)(2,1)S(1)}, u32[]{:S(2)}, u32[]{:S(2)}) %collective-permute-start) | collective-permute-done | bytes 1966112 | tf_op jit(solution)/shard_map/ppermute | solution.py:580
  161.9 15.8 %recurrent_forward.1 = (bf16[2,256,1280]{2,1,0:T(8,128)(2,1)S(1)}, f32[2,256,1280]{2,1,0:T(8,128)}, f32[2,256,1280]{2,1,0:T(8,128)}, f32[2,256,1280]{2,1,0:T(8,1...) custom-call(bf16[2,256,1280]{2,1,0:T(8,128)(2,1)S(1)} %bitcast.210, f32[2,8,1280]{2,1,0:T(8,128)S(1)} %pad_convert_fusion.halo_ref, ...), custom_call_target="tpu_custom_call" | custom-call | flops 1 | bytes 1 | tf_op jit(solution)/shard_map/recurrent_forward/pallas_call | solution.py:153
  225.6 16.6 %collective-permute-done.15 = bf16[4,160,1280]{2,1,0:T(8,128)(2,1)S(1)} collective-permute-done((bf16[4,160,1280]{2,1,0:T(8,128)(2,1)}, bf16[4,160,1280]{2,1,0:T(8,128)(2,1)S(1)}, u32[]{:S(2)}, u32[]{:S(2)}) %collective-permute-start.15) | collective-permute-done | bytes 1638432 | tf_op jit(solution)/shard_map/ppermute | solution.py:580
  247.1 13.6 %collective-permute-done.17 = bf16[2,160,1280]{2,1,0:T(8,128)(2,1)S(1)} collective-permute-done((bf16[2,160,1280]{2,1,0:T(8,128)(2,1)S(1)}, bf16[2,160,1280]{2,1,0:T(8,128)(2,1)S(1)}, u32[]{:S(2)}, u32[]{:S(2)}) %collective-permute-start.17) | collective-permute-done | bytes 819232 | tf_op jit(solution)/shard_map/ppermute | solution.py:580
  278.5 29.1 %collective-permute-done.20.refs_0_ = bf16[256,2560]{1,0:T(8,128)(2,1)S(1)} collective-permute-done((bf16[256,2560]{1,0:T(8,128)(2,1)S(1)}, bf16[256,2560]{1,0:T(8,128)(2,1)S(1)}, u32[]{:S(2)}, u32[]{:S(2)}) %collective-permute-start.20) | collective-permute-done | bytes 1310752 | tf_op jit(solution)/shard_map/ppermute | solution.py:580
  310.6 13.2 %collective-permute-done.22.refs_1_ = bf16[128,2560]{1,0:T(8,128)(2,1)S(1)} collective-permute-done((bf16[128,2560]{1,0:T(8,128)(2,1)S(1)}, bf16[128,2560]{1,0:T(8,128)(2,1)S(1)}, u32[]{:S(2)}, u32[]{:S(2)}) %collective-permute-start.22) | collective-permute-done | bytes 655392 | tf_op jit(solution)/shard_map/ppermute | solution.py:580
  329.2 28.6 %collective-permute-done.29 = bf16[256,2560]{1,0:T(8,128)(2,1)S(1)} collective-permute-done((bf16[256,2560]{1,0:T(8,128)(2,1)S(1)}, bf16[256,2560]{1,0:T(8,128)(2,1)S(1)}, u32[]{:S(2)}, u32[]{:S(2)}) %collective-permute-start.29) | collective-permute-done | bytes 1310752 | tf_op jit(solution)/shard_map/ppermute | solution.py:580
  362.6 12.3 %collective-permute-done.31 = bf16[128,2560]{1,0:T(8,128)(2,1)S(1)} collective-permute-done((bf16[128,2560]{1,0:T(8,128)(2,1)S(1)}, bf16[128,2560]{1,0:T(8,128)(2,1)S(1)}, u32[]{:S(2)}, u32[]{:S(2)}) %collective-permute-start.31) | collective-permute-done | bytes 655392 | tf_op jit(solution)/shard_map/ppermute | solution.py:580
  384.8 13.5 %all-gather.6.cloned.1.call-done = bf16[4,640,3072]{2,1,0:T(8,128)(2,1)} async-done(((bf16[4,160,3072]{2,1,0:T(8,128)(2,1)}), bf16[4,640,3072]{2,1,0:T(8,128)(2,1)}) %all-gather.6.cloned.1.call-update) | async-done | bytes 15728656 | tf_op jit(solution)/shard_map/all_gather | solution.py:711
  398.3 31.2 %feed_forward.1 = (bf16[2048,2560]{1,0:T(8,128)(2,1)}, bf16[2048,1024]{1,0:T(8,128)(2,1)}, f32[2048,1024]{1,0:T(8,128)}, f32[2048,1024]{1,0:T(8,128)}) custom-call(bf16[256,2560]{1,0:T(8,128)(2,1)} %copy-done.24, bf16[128,2560]{1,0:T(8,128)(2,1)} %copy-done.59, bf16[128,2560]{1,0:T(8,128)(2,1)} %copy-done.60, bf16[256,2560]{1,0:T(8,128)(2,1)} %copy-done.25, ...), custom_call_target="tpu_custom_call" | custom-call | flops 1 | bytes 1 | tf_op jit(solution)/shard_map/feed_forward/pallas_call | solution.py:392
  429.5 15.7 %weight_grad.2 = bf16[2560,1024]{1,0:T(8,128)(2,1)} custom-call(bf16[2048,2560]{1,0:T(8,128)(2,1)} %constant_dynamic-update-slice_fusion.x_ref.fg_ref, bf16[2048,1024]{1,0:T(8,128)(2,1)} %get-tuple-element.287.g_ref.h_ref), custom_call_target="tpu_custom_call" | custom-call | flops 1 | bytes 1 | tf_op jit(solution)/shard_map/weight_grad/pallas_call | solution.py:470
  445.2 45.8 %feed_backward.1 = (bf16[2048,2048]{1,0:T(8,128)(2,1)}, bf16[1024,2560]{1,0:T(8,128)(2,1)}, bf16[1024,2560]{1,0:T(8,128)(2,1)}) custom-call(bf16[2048,2560]{1,0:T(8,128)(2,1)} %constant_dynamic-update-slice_fusion.x_ref.fg_ref, f32[2048,1024]{1,0:T(8,128)} %get-tuple-element.268.gate_ref, f32[2048,1024]{1,0:T(8,128)} %get-tuple-element.269.up_ref, ...), custom_call_target="tpu_custom_call" | custom-call | flops 1 | bytes 1 | tf_op jit(solution)/shard_map/feed_backward/pallas_call | solution.py:426
  507.1 28.1 %weight_grad.3 = bf16[2560,2048]{1,0:T(8,128)(2,1)} custom-call(bf16[2048,2560]{1,0:T(8,128)(2,1)} %get-tuple-element.277.x_ref, bf16[2048,2048]{1,0:T(8,128)(2,1)} %get-tuple-element.278.g_ref), custom_call_target="tpu_custom_call" | custom-call | flops 1 | bytes 1 | tf_op jit(solution)/shard_map/weight_grad/pallas_call | solution.py:470
  544.9 18.0 %feed_down.1 = (bf16[1024,2560]{1,0:T(8,128)(2,1)}, bf16[1024,2560]{1,0:T(8,128)(2,1)}) custom-call(bf16[2048,1024]{1,0:T(8,128)(2,1)} %get-tuple-element.287.g_ref.h_ref, bf16[2560,3072]{1,0:T(8,128)(2,1)} %bitcast.218), custom_call_target="tpu_custom_call" | custom-call | flops 1 | bytes 1 | tf_op jit(solution)/shard_map/feed_down/pallas_call | solution.py:450
  606.5 13.7 %recurrent_adjoint.1 = (bf16[2,256,1280]{2,1,0:T(8,128)(2,1)S(1)}, f32[2,256,1280]{2,1,0:T(8,128)S(1)}, f32[2,256,1280]{2,1,0:T(8,128)}) custom-call(f32[2,256,1280]{2,1,0:T(8,128)} %fusion.37.rg_ref, f32[2,256,1280]{2,1,0:T(8,128)} %get-tuple-element.571.gelu_ref, f32[2,256,1280]{2,1,0:T(8,128)} %get-tuple-element.310.a_ref, ...), custom_call_target="tpu_custom_call" | custom-call | flops 1 | bytes 1 | tf_op jit(solution)/shard_map/recurrent_adjoint/pallas_call | solution.py:195
  631.7 27.2 %collective-permute-done.45 = bf16[512,1280]{1,0:T(8,128)(2,1)} collective-permute-done((bf16[512,1280]{1,0:T(8,128)(2,1)}, bf16[512,1280]{1,0:T(8,128)(2,1)}, u32[]{:S(2)}, u32[]{:S(2)}) %collective-permute-start.45) | collective-permute-done | bytes 1310752 | tf_op jit(solution)/shard_map/ppermute | solution.py:580
  678.4 13.5 %recurrent_backward.1 = (f32[2,256,1280]{2,1,0:T(8,128)}, f32[2,8,1280]{2,1,0:T(8,128)S(1)}, f32[8,1280]{1,0:T(8,128)S(1)}, bf16[2,256,1280]{2,1,0:T(8,128)(2,1)S(1)}) custom-call(f32[2,256,1280]{2,1,0:T(8,128)} %copy-done.1, f32[2,256,1280]{2,1,0:T(8,128)} %get-tuple-element.344.tsum_ref, f32[2,8,1280]{2,1,0:T(8,128)S(1)} %broadcast_in_dim.161.leave_ref, ...), custom_call_target="tpu_custom_call" | custom-call | flops 1 | bytes 1 | tf_op jit(solution)/shard_map/recurrent_backward/pallas_call | solution.py:274
  708.6 10.9 %weight_grad_parts.5 = (bf16[1536,640]{1,0:T(8,128)(2,1)}, bf16[1536,640]{1,0:T(8,128)(2,1)}, bf16[768,640]{1,0:T(8,128)(2,1)}, bf16[768,640]{1,0:T(8,128)(2,1)}...) custom-call(s32[4]{0:T(128)} %broadcast_xor_fusion.places_ref, bf16[512,2560]{1,0:T(8,128)(2,1)} %multiply_convert_fusion.x_ref, ...), custom_call_target="tpu_custom_call" | custom-call | flops 1 | bytes 1 | tf_op jit(solution)/shard_map/weight_grad_parts/pallas_call | solution.py:548
  734.7 15.7 %unit_terms.1 = (f32[256,2560]{1,0:T(8,128)}, f32[256,2560]{1,0:T(8,128)}) custom-call(s32[2]{0:T(128)} %pad_add_fusion.1.order_ref, bf16[512,1280]{1,0:T(8,128)(2,1)} %bitcast.232, bf16[2560,1280]{1,0:T(8,128)(2,1)} %bitcast.224, bf16[512,1280]{1,0:T(8,128)(2,1)} %bitcast.213, bf16[2560,1280]{1,0:T(8,128)(2,1)} %bitcast.226), custom_call_target="tpu_custom_call" | custom-call | flops 1 | bytes 1 | tf_op jit(solution)/shard_map/unit_terms/pallas_call | solution.py:504
  750.4 40.8 %collective-permute-done.56 = bf16[640,640]{1,0:T(8,128)(2,1)S(1)} collective-permute-done((bf16[640,640]{1,0:T(8,128)(2,1)S(1)}, bf16[640,640]{1,0:T(8,128)(2,1)S(1)}, u32[]{:S(2)}, u32[]{:S(2)}) %collective-permute-start.56) | collective-permute-done | bytes 819232 | tf_op jit(solution)/shard_map/ppermute | solution.py:580
  807.1 18.0 %collective-permute-done.60 = bf16[768,640]{1,0:T(8,128)(2,1)S(1)} collective-permute-done((bf16[768,640]{1,0:T(8,128)(2,1)}, bf16[768,640]{1,0:T(8,128)(2,1)S(1)}, u32[]{:S(2)}, u32[]{:S(2)}) %collective-permute-start.60) | collective-permute-done | bytes 983072 | tf_op jit(solution)/shard_map/ppermute | solution.py:580
  883.1 13.0 %collective-permute-done.73 = bf16[160,2048]{1,0:T(8,128)(2,1)} collective-permute-done((bf16[160,2048]{1,0:T(8,128)(2,1)}, bf16[160,2048]{1,0:T(8,128)(2,1)}, u32[]{:S(2)}, u32[]{:S(2)}) %collective-permute-start.73) | collective-permute-done | bytes 655392 | tf_op jit(solution)/shard_map/ppermute | solution.py:580
  897.6 12.0 %collective-permute-done.63 = bf16[256,1280]{1,0:T(8,128)(2,1)S(1)} collective-permute-done((bf16[256,1280]{1,0:T(8,128)(2,1)}, bf16[256,1280]{1,0:T(8,128)(2,1)S(1)}, u32[]{:S(2)}, u32[]{:S(2)}) %collective-permute-start.63) | collective-permute-done | bytes 655392 | tf_op jit(solution)/shard_map/ppermute | solution.py:580
  (521 shorter events, 423.0 us)
Async XLA Ops:
  7.2 52.1 %all-gather.10.cloned.1.call-start = ((), (), s32[]{:S(2)}) async-start(), calls=%async_computation.12 | async-start | bytes 2457600 | tf_op jit(solution)/shard_map/all_gather | solution.py:764
  12.9 113.1 %all-gather.8.cloned.1.call-start = ((), (), s32[]{:S(2)}) async-start(), calls=%async_computation.11 | async-start | bytes 4096000 | tf_op jit(solution)/shard_map/all_gather | solution.py:765
  27.2 371.1 %all-gather.6.cloned.1.call-start = ((), (), s32[]{:S(2)}) async-start(), calls=%async_computation.5 | async-start | bytes 19660800 | tf_op jit(solution)/shard_map/all_gather | solution.py:711
  29.6 87.3 %collective-permute-start.8 = (s32[2,3]{1,0:T(2,128)S(1)}, s32[2,3]{1,0:T(2,128)S(1)}, u32[]{:S(2)}, u32[]{:S(2)}) collective-permute-start(s32[2,3]{1,0:T(2,128)S(1)} %slice.464), channel_id=1, source_target_pairs={{0,2},{2,4},{4,6},{1,3},{3,5},{5,7},{8,10},{10,12},{12,14},{9,11},... | collective-permute-start | bytes 80 | tf_op jit(solution)/shard_map/ppermute | solution.py:26
  59.3 49.5 %collective-permute-start = (bf16[4,192,1280]{2,1,0:T(8,128)(2,1)}, bf16[4,192,1280]{2,1,0:T(8,128)(2,1)S(1)}, u32[]{:S(2)}, u32[]{:S(2)}) collective-permute-start(bf16[4,192,1280]{2,1,0:T(8,128)(2,1)} %bitcast.248), channel_id=1, source_target_pairs={{0,8},{8,0},{16,24},{24,16},{1,9},{9,1},{17,25},{25,17},{2,10},{10... | collective-permute-start | bytes 5898248 | tf_op jit(solution)/shard_map/ppermute | solution.py:580
  60.8 50.5 %collective-permute-start.1 = (bf16[4,192,1280]{2,1,0:T(8,128)(2,1)}, bf16[4,192,1280]{2,1,0:T(8,128)(2,1)}, u32[]{:S(2)}, u32[]{:S(2)}) collective-permute-start(bf16[4,192,1280]{2,1,0:T(8,128)(2,1)} %bitcast.249), channel_id=1, source_target_pairs={{0,16},{8,24},{16,0},{24,8},{1,17},{9,25},{17,1},{25,9},{2,18},{10... | collective-permute-start | bytes 5898248 | tf_op jit(solution)/shard_map/ppermute | solution.py:580
  129.9 409.0 %reduce-scatter.6.cloned.1.call-start = ((), (), s32[]{:S(2)}) async-start(), calls=%async_computation.6 | async-start | bytes 6553600 | tf_op jit(solution)/shard_map/reduce_scatter | solution.py:719
  445.2 282.0 %reduce-scatter.8.cloned.1.call-start = ((), (), s32[]{:S(2)}) async-start(), calls=%async_computation.7 | async-start | bytes 13107200 | tf_op jit(solution)/shard_map/reduce_scatter | solution.py:719
  538.9 253.5 %reduce-scatter.10.cloned.1.call-start = ((), (), s32[]{:S(2)}) async-start(), calls=%async_computation.8 | async-start | bytes 2048000 | tf_op jit(solution)/shard_map/reduce_scatter | solution.py:909
  592.4 66.6 %collective-permute-start.47 = (bf16[1280,640]{1,0:T(8,128)(2,1)}, bf16[1280,640]{1,0:T(8,128)(2,1)}, u32[]{:S(2)}, u32[]{:S(2)}) collective-permute-start(bf16[1280,640]{1,0:T(8,128)(2,1)} %get-tuple-element.305), channel_id=1, source_target_pairs={{0,8},{8,0},{16,24},{24,16},{1,9},{9,1},{17,25},{25,17},{2,10},{10... | collective-permute-start | bytes 4915208 | tf_op jit(solution)/shard_map/ppermute | solution.py:580
  592.8 66.1 %collective-permute-start.48 = (bf16[1280,640]{1,0:T(8,128)(2,1)}, bf16[1280,640]{1,0:T(8,128)(2,1)}, u32[]{:S(2)}, u32[]{:S(2)}) collective-permute-start(bf16[1280,640]{1,0:T(8,128)(2,1)} %get-tuple-element.306), channel_id=1, source_target_pairs={{0,16},{8,24},{16,0},{24,8},{1,17},{9,25},{17,1},{25,9},{2,18},{10... | collective-permute-start | bytes 4915208 | tf_op jit(solution)/shard_map/ppermute | solution.py:580
  593.4 65.5 %collective-permute-start.45 = (bf16[512,1280]{1,0:T(8,128)(2,1)}, bf16[512,1280]{1,0:T(8,128)(2,1)}, u32[]{:S(2)}, u32[]{:S(2)}) collective-permute-start(bf16[512,1280]{1,0:T(8,128)(2,1)} %get-tuple-element.294), channel_id=1, source_target_pairs={{0,8},{8,0},{16,24},{24,16},{1,9},{9,1},{17,25},{25,17},{2,10},{10... | collective-permute-start | bytes 3932168 | tf_op jit(solution)/shard_map/ppermute | solution.py:580
  594.9 64.1 %collective-permute-start.46 = (bf16[512,1280]{1,0:T(8,128)(2,1)}, bf16[512,1280]{1,0:T(8,128)(2,1)}, u32[]{:S(2)}, u32[]{:S(2)}) collective-permute-start(bf16[512,1280]{1,0:T(8,128)(2,1)} %get-tuple-element.295), channel_id=1, source_target_pairs={{0,16},{8,24},{16,0},{24,8},{1,17},{9,25},{17,1},{25,9},{2,18},{10... | collective-permute-start | bytes 3932168 | tf_op jit(solution)/shard_map/ppermute | solution.py:580
  666.1 56.3 %collective-permute-start.49 = (bf16[1280,640]{1,0:T(8,128)(2,1)}, bf16[1280,640]{1,0:T(8,128)(2,1)}, u32[]{:S(2)}, u32[]{:S(2)}) collective-permute-start(bf16[1280,640]{1,0:T(8,128)(2,1)} %get-tuple-element.335), channel_id=1, source_target_pairs={{0,8},{8,0},{16,24},{24,16},{1,9},{9,1},{17,25},{25,17},{2,10},{10... | collective-permute-start | bytes 4915208 | tf_op jit(solution)/shard_map/ppermute | solution.py:580
  667.9 54.5 %collective-permute-start.50 = (bf16[1280,640]{1,0:T(8,128)(2,1)}, bf16[1280,640]{1,0:T(8,128)(2,1)}, u32[]{:S(2)}, u32[]{:S(2)}) collective-permute-start(bf16[1280,640]{1,0:T(8,128)(2,1)} %get-tuple-element.336), channel_id=1, source_target_pairs={{0,16},{8,24},{16,0},{24,8},{1,17},{9,25},{17,1},{25,9},{2,18},{10... | collective-permute-start | bytes 4915208 | tf_op jit(solution)/shard_map/ppermute | solution.py:580
  672.5 49.9 %collective-permute-start.51 = (bf16[640,640]{1,0:T(8,128)(2,1)}, bf16[640,640]{1,0:T(8,128)(2,1)}, u32[]{:S(2)}, u32[]{:S(2)}) collective-permute-start(bf16[640,640]{1,0:T(8,128)(2,1)} %add_convert_fusion.16), channel_id=1, source_target_pairs={{0,16},{8,24},{16,0},{24,8},{1,17},{9,25},{17,1},{25,9},{2,18},{10... | collective-permute-start | bytes 2457608 | tf_op jit(solution)/shard_map/ppermute | solution.py:580
  673.2 49.2 %collective-permute-start.52 = (bf16[640,640]{1,0:T(8,128)(2,1)}, bf16[640,640]{1,0:T(8,128)(2,1)}, u32[]{:S(2)}, u32[]{:S(2)}) collective-permute-start(bf16[640,640]{1,0:T(8,128)(2,1)} %add_convert_fusion.15), channel_id=1, source_target_pairs={{0,8},{8,0},{16,24},{24,16},{1,9},{9,1},{17,25},{25,17},{2,10},{10... | collective-permute-start | bytes 2457608 | tf_op jit(solution)/shard_map/ppermute | solution.py:580
  727.2 113.9 %reduce-scatter.12.cloned.1.call-start = ((), (), s32[]{:S(2)}) async-start(), calls=%async_computation.9 | async-start | bytes 2048000 | tf_op jit(solution)/shard_map/reduce_scatter | solution.py:909
  730.0 61.2 %collective-permute-start.58 = (bf16[1536,640]{1,0:T(8,128)(2,1)}, bf16[1536,640]{1,0:T(8,128)(2,1)S(1)}, u32[]{:S(2)}, u32[]{:S(2)}) collective-permute-start(bf16[1536,640]{1,0:T(8,128)(2,1)} %get-tuple-element.374), channel_id=1, source_target_pairs={{0,8},{8,0},{16,24},{24,16},{1,9},{9,1},{17,25},{25,17},{2,10},{10... | collective-permute-start | bytes 5898248 | tf_op jit(solution)/shard_map/ppermute | solution.py:580
  730.7 61.7 %collective-permute-start.59 = (bf16[1536,640]{1,0:T(8,128)(2,1)}, bf16[1536,640]{1,0:T(8,128)(2,1)}, u32[]{:S(2)}, u32[]{:S(2)}) collective-permute-start(bf16[1536,640]{1,0:T(8,128)(2,1)} %get-tuple-element.375), channel_id=1, source_target_pairs={{0,16},{8,24},{16,0},{24,8},{1,17},{9,25},{17,1},{25,9},{2,18},{10... | collective-permute-start | bytes 5898248 | tf_op jit(solution)/shard_map/ppermute | solution.py:580
  731.1 60.1 %collective-permute-start.56 = (bf16[640,640]{1,0:T(8,128)(2,1)S(1)}, bf16[640,640]{1,0:T(8,128)(2,1)S(1)}, u32[]{:S(2)}, u32[]{:S(2)}) collective-permute-start(bf16[640,640]{1,0:T(8,128)(2,1)S(1)} %add_convert_fusion.14), channel_id=1, source_target_pairs={{0,16},{8,24},{16,0},{24,8},{1,17},{9,25},{17,1},{25,9},{2,18},{10... | collective-permute-start | bytes 2457608 | tf_op jit(solution)/shard_map/ppermute | solution.py:580
  732.7 58.5 %collective-permute-start.57 = (bf16[640,640]{1,0:T(8,128)(2,1)S(1)}, bf16[640,640]{1,0:T(8,128)(2,1)S(1)}, u32[]{:S(2)}, u32[]{:S(2)}) collective-permute-start(bf16[640,640]{1,0:T(8,128)(2,1)S(1)} %add_convert_fusion.13), channel_id=1, source_target_pairs={{0,8},{8,0},{16,24},{24,16},{1,9},{9,1},{17,25},{25,17},{2,10},{10... | collective-permute-start | bytes 2457608 | tf_op jit(solution)/shard_map/ppermute | solution.py:580
  803.1 122.5 %reduce-scatter.14.cloned.1.call-start = ((), (), s32[]{:S(2)}) async-start(), calls=%async_computation.10 | async-start | bytes 2457600 | tf_op jit(solution)/shard_map/reduce_scatter | solution.py:909
  869.9 51.5 %collective-permute-start.66 = (f32[256,2560]{1,0:T(8,128)}, f32[256,2560]{1,0:T(8,128)S(1)}, u32[]{:S(2)}, u32[]{:S(2)}) collective-permute-start(f32[256,2560]{1,0:T(8,128)} %subtract_add_fusion), channel_id=1, source_target_pairs={{0,1},{1,0},{2,3},{3,2},{4,5},{5,4},{6,7},{7,6},{8,9},{9,8},{10,11... | collective-permute-start | bytes 7864328 | tf_op jit(solution)/shard_map/ppermute | solution.py:31
  (140 other events, 2313.4 us)
Sparse Core Ops, SparseCore 0:
  13.0 46.2 all-gather.9
  61.5 64.4 all-gather.7
  130.0 268.2 all-gather.5
  445.3 93.5 reduce-scatter.5
  541.1 180.2 reduce-scatter.7
  727.3 36.8 reduce-scatter.9
  803.2 37.9 reduce-scatter.11
  855.8 40.5 reduce-scatter.13

commit v5 on v4

--- a/solution.py
+++ b/solution.py
@@ -858,10 +858,6 @@
 
     square = lax.axis_size("fsdp") == SQUARE
     places = lax.axis_index("fsdp").astype(jnp.int32) ^ jnp.array(ORDER, jnp.int32)
-    feed_parts, feed_kept = token_parts(feed_own, feed_theirs)
-    feed_parts, branch_grad = after(feed_parts, branch_grad)
-    feed_got = near_send(feed_parts, group)
-    feed_parts = feed_parts + feed_kept
     if square:
         outlet_parts = weight_grad_parts(branch_grad, recurrent, places)
     else:
@@ -875,8 +871,7 @@
         gelu_parts = weight_grad_parts(normed, gelu_low, places)
     else:
         gelu_parts = weight_grad(normed, gelu_low)
-    feed_got, outlet_got, gelu_parts, tprod, tsum = together(feed_got, outlet_got, gelu_parts, tprod, tsum)
-    feed_sums = near_middle(feed_parts, feed_got)
+    outlet_got, gelu_parts, tprod, tsum = together(outlet_got, gelu_parts, tprod, tsum)
     if square:
         outlet_sums, gelu_parts, tprod = together(near_middle(outlet_parts, outlet_got), gelu_parts, tprod)
         outlet_more, gelu_got = near_second(outlet_sums, "fsdp"), near_send(gelu_parts, "fsdp")
@@ -927,10 +922,14 @@
     normed_grad = ours + swap(theirs, "tp")
     norm_part, gain_one = rms_back(own(x), own(inverse_one), norm_gains[0], normed_grad)
     input_own = residual_grad + norm_part
-    late, gelu_part, expand_part, down_part, input_own, gain_one, feed_sums = together(
-        late, gelu_part, expand_part, down_part, input_own, gain_one, feed_sums
+    late, gelu_part, expand_part, down_part, input_own, gain_one, feed_own, feed_theirs = together(
+        late, gelu_part, expand_part, down_part, input_own, gain_one, feed_own, feed_theirs
     )
     late = wide(scatter_ctx(late))
+    feed_parts, feed_kept = token_parts(feed_own, feed_theirs)
+    feed_got = near_send(feed_parts, group)
+    feed_parts = feed_parts + feed_kept
+    feed_sums = near_middle(feed_parts, feed_got)
     input_grad = join(input_own).reshape(rows, length, width)
     feed_out = near_last(feed_parts, feed_got, near_second(feed_sums, group))
     block_output = join(low(residual + feed_out)).reshape(rows, length, width)

time: 950 us -> 999 us (1.052)
  waiting for transfers between devices: 375 us -> 419 us
    reduce_scatter x2, waiting for transfers between devices: 2.62 us -> 29.9 us  [scatter_feed(): return lax.psum_scatter(grad, along, scatter_dimension=1, tiled=True)]
    ppermute x54, waiting for transfers between devices: 298 us -> 319 us  [cross(): lax.ppermute(x, axis, [(i, i ^ r) for i in range(lax.axis_size(axis))])]
    unnamed x176 -> x188, local copies, waits for them, and re-layouts: 30.9 us -> 31.5 us
  transfers between devices with their start and end apart: 86 -> 86, of which waited for: 45 -> 48; matrix products, arithmetic and copies ran while one was open for 22% -> 21% of each run, Pallas kernels for 19% -> 18%
where the time goes in v5:
time: 999 us; the launch traced here: 989 us
  waiting for transfers between devices  419 us (42%)
  Pallas kernels  238 us (24%)
  local copies, waits for them, and re-layouts  103 us (10%)
  other arithmetic  97.5 us (10%)
  starting transfers between devices  87.4 us (9%)
  matrix products  27.2 us (3%)
  between operations  16.2 us (2%)
    ppermute x54, waiting for transfers between devices, cross(): lax.ppermute(x, axis, [(i, i ^ r) for i in range(lax.axis_size(axis))])  319 us
    ppermute x54, starting transfers between devices, cross(): lax.ppermute(x, axis, [(i, i ^ r) for i in range(lax.axis_size(axis))])  60.6 us
    pallas_call x1, Pallas kernels, feed_backward(): pl.pallas_call(body, grid=(tiles,), in_specs=[tokens_spec(width, tiles, m...  45.8 us
    pallas_call x2, Pallas kernels, weight_grad(): pl.pallas_call(body, grid=(width // deep,), in_specs=[pl.BlockSpec((count...  43.7 us
    pallas_call x1, Pallas kernels, feed_forward(): pl.pallas_call(body, grid=(tiles,), in_specs=[pl.BlockSpec(memory_space=p...  39.6 us
    pallas_call x3, Pallas kernels, weight_grad_parts(): pl.pallas_call(body, grid_spec=pltpu.PrefetchScalarGridSpec(num_scalar_pr...  31.6 us
    unnamed x188, local copies, waits for them, and re-layouts  31.5 us
    reduce_scatter x2, waiting for transfers between devices, scatter_feed(): return lax.psum_scatter(grad, along, scatter_dimension=1, tiled=True)  29.9 us
  transfers between devices with their start and end apart: 86, of which 48 were waited for; matrix products, arithmetic and copies ran while one was open for 21% of the time, Pallas kernels for 18%

profile of v5, /device:TPU:0, one launch (start us, length us, event | category | flops | bytes accessed | tf_op | source)
XLA Modules:
  0.0 988.9 jit_solution(10707358467792547597)
XLA Ops:
  40.4 18.9 %all-gather.10.cloned.1.call-done = bf16[768,1280]{1,0:T(8,128)(2,1)} async-done(((bf16[192,1280]{1,0:T(8,128)(2,1)}), bf16[768,1280]{1,0:T(8,128)(2,1)}) %all-gather.10.cloned.1.call-update) | async-done | bytes 1966096 | tf_op jit(solution)/shard_map/all_gather | solution.py:764
  74.7 34.1 %collective-permute-done = bf16[4,192,1280]{2,1,0:T(8,128)(2,1)S(1)} collective-permute-done((bf16[4,192,1280]{2,1,0:T(8,128)(2,1)}, bf16[4,192,1280]{2,1,0:T(8,128)(2,1)S(1)}, u32[]{:S(2)}, u32[]{:S(2)}) %collective-permute-start) | collective-permute-done | bytes 1966112 | tf_op jit(solution)/shard_map/ppermute | solution.py:580
  161.8 15.8 %recurrent_forward.1 = (bf16[2,256,1280]{2,1,0:T(8,128)(2,1)S(1)}, f32[2,256,1280]{2,1,0:T(8,128)}, f32[2,256,1280]{2,1,0:T(8,128)}, f32[2,256,1280]{2,1,0:T(8,1...) custom-call(bf16[2,256,1280]{2,1,0:T(8,128)(2,1)S(1)} %bitcast.210, f32[2,8,1280]{2,1,0:T(8,128)S(1)} %pad_convert_fusion.halo_ref, ...), custom_call_target="tpu_custom_call" | custom-call | flops 1 | bytes 1 | tf_op jit(solution)/shard_map/recurrent_forward/pallas_call | solution.py:153
  225.6 16.6 %collective-permute-done.15 = bf16[4,160,1280]{2,1,0:T(8,128)(2,1)S(1)} collective-permute-done((bf16[4,160,1280]{2,1,0:T(8,128)(2,1)}, bf16[4,160,1280]{2,1,0:T(8,128)(2,1)S(1)}, u32[]{:S(2)}, u32[]{:S(2)}) %collective-permute-start.15) | collective-permute-done | bytes 1638432 | tf_op jit(solution)/shard_map/ppermute | solution.py:580
  247.1 13.6 %collective-permute-done.17 = bf16[2,160,1280]{2,1,0:T(8,128)(2,1)S(1)} collective-permute-done((bf16[2,160,1280]{2,1,0:T(8,128)(2,1)S(1)}, bf16[2,160,1280]{2,1,0:T(8,128)(2,1)S(1)}, u32[]{:S(2)}, u32[]{:S(2)}) %collective-permute-start.17) | collective-permute-done | bytes 819232 | tf_op jit(solution)/shard_map/ppermute | solution.py:580
  278.5 29.1 %collective-permute-done.20.refs_0_ = bf16[256,2560]{1,0:T(8,128)(2,1)S(1)} collective-permute-done((bf16[256,2560]{1,0:T(8,128)(2,1)S(1)}, bf16[256,2560]{1,0:T(8,128)(2,1)S(1)}, u32[]{:S(2)}, u32[]{:S(2)}) %collective-permute-start.20) | collective-permute-done | bytes 1310752 | tf_op jit(solution)/shard_map/ppermute | solution.py:580
  310.6 13.2 %collective-permute-done.22.refs_1_ = bf16[128,2560]{1,0:T(8,128)(2,1)S(1)} collective-permute-done((bf16[128,2560]{1,0:T(8,128)(2,1)S(1)}, bf16[128,2560]{1,0:T(8,128)(2,1)S(1)}, u32[]{:S(2)}, u32[]{:S(2)}) %collective-permute-start.22) | collective-permute-done | bytes 655392 | tf_op jit(solution)/shard_map/ppermute | solution.py:580
  329.1 28.6 %collective-permute-done.29 = bf16[256,2560]{1,0:T(8,128)(2,1)S(1)} collective-permute-done((bf16[256,2560]{1,0:T(8,128)(2,1)S(1)}, bf16[256,2560]{1,0:T(8,128)(2,1)S(1)}, u32[]{:S(2)}, u32[]{:S(2)}) %collective-permute-start.29) | collective-permute-done | bytes 1310752 | tf_op jit(solution)/shard_map/ppermute | solution.py:580
  362.5 12.3 %collective-permute-done.31 = bf16[128,2560]{1,0:T(8,128)(2,1)S(1)} collective-permute-done((bf16[128,2560]{1,0:T(8,128)(2,1)S(1)}, bf16[128,2560]{1,0:T(8,128)(2,1)S(1)}, u32[]{:S(2)}, u32[]{:S(2)}) %collective-permute-start.31) | collective-permute-done | bytes 655392 | tf_op jit(solution)/shard_map/ppermute | solution.py:580
  384.8 13.5 %all-gather.6.cloned.1.call-done = bf16[4,640,3072]{2,1,0:T(8,128)(2,1)} async-done(((bf16[4,160,3072]{2,1,0:T(8,128)(2,1)}), bf16[4,640,3072]{2,1,0:T(8,128)(2,1)}) %all-gather.6.cloned.1.call-update) | async-done | bytes 15728656 | tf_op jit(solution)/shard_map/all_gather | solution.py:711
  398.3 39.6 %feed_forward.1 = (bf16[2048,2560]{1,0:T(8,128)(2,1)}, bf16[2048,1024]{1,0:T(8,128)(2,1)}, f32[2048,1024]{1,0:T(8,128)}, f32[2048,1024]{1,0:T(8,128)}) custom-call(bf16[256,2560]{1,0:T(8,128)(2,1)} %copy-done.24, bf16[128,2560]{1,0:T(8,128)(2,1)} %copy-done.63, bf16[128,2560]{1,0:T(8,128)(2,1)} %copy-done.64, bf16[256,2560]{1,0:T(8,128)(2,1)} %copy-done.25, ...), custom_call_target="tpu_custom_call" | custom-call | flops 1 | bytes 1 | tf_op jit(solution)/shard_map/feed_forward/pallas_call | solution.py:392
  437.9 15.6 %weight_grad.2 = bf16[2560,1024]{1,0:T(8,128)(2,1)} custom-call(bf16[2048,2560]{1,0:T(8,128)(2,1)} %constant_dynamic-update-slice_fusion.x_ref.fg_ref, bf16[2048,1024]{1,0:T(8,128)(2,1)} %get-tuple-element.282.g_ref.h_ref), custom_call_target="tpu_custom_call" | custom-call | flops 1 | bytes 1 | tf_op jit(solution)/shard_map/weight_grad/pallas_call | solution.py:470
  453.6 45.8 %feed_backward.1 = (bf16[2048,2048]{1,0:T(8,128)(2,1)}, bf16[1024,2560]{1,0:T(8,128)(2,1)}, bf16[1024,2560]{1,0:T(8,128)(2,1)}) custom-call(bf16[2048,2560]{1,0:T(8,128)(2,1)} %constant_dynamic-update-slice_fusion.x_ref.fg_ref, f32[2048,1024]{1,0:T(8,128)} %get-tuple-element.263.gate_ref, f32[2048,1024]{1,0:T(8,128)} %get-tuple-element.264.up_ref, ...), custom_call_target="tpu_custom_call" | custom-call | flops 1 | bytes 1 | tf_op jit(solution)/shard_map/feed_backward/pallas_call | solution.py:426
  515.5 28.1 %weight_grad.3 = bf16[2560,2048]{1,0:T(8,128)(2,1)} custom-call(bf16[2048,2560]{1,0:T(8,128)(2,1)} %get-tuple-element.272.x_ref, bf16[2048,2048]{1,0:T(8,128)(2,1)} %get-tuple-element.273.g_ref), custom_call_target="tpu_custom_call" | custom-call | flops 1 | bytes 1 | tf_op jit(solution)/shard_map/weight_grad/pallas_call | solution.py:470
  552.8 18.4 %feed_down.1 = (bf16[1024,2560]{1,0:T(8,128)(2,1)}, bf16[1024,2560]{1,0:T(8,128)(2,1)}) custom-call(bf16[2048,1024]{1,0:T(8,128)(2,1)} %get-tuple-element.282.g_ref.h_ref, bf16[2560,3072]{1,0:T(8,128)(2,1)} %bitcast.218), custom_call_target="tpu_custom_call" | custom-call | flops 1 | bytes 1 | tf_op jit(solution)/shard_map/feed_down/pallas_call | solution.py:450
  607.2 13.5 %recurrent_adjoint.1 = (bf16[2,256,1280]{2,1,0:T(8,128)(2,1)S(1)}, f32[2,256,1280]{2,1,0:T(8,128)S(1)}, f32[2,256,1280]{2,1,0:T(8,128)}) custom-call(f32[2,256,1280]{2,1,0:T(8,128)} %fusion.37.rg_ref, f32[2,256,1280]{2,1,0:T(8,128)} %get-tuple-element.561.gelu_ref, f32[2,256,1280]{2,1,0:T(8,128)} %get-tuple-element.299.a_ref, ...), custom_call_target="tpu_custom_call" | custom-call | flops 1 | bytes 1 | tf_op jit(solution)/shard_map/recurrent_adjoint/pallas_call | solution.py:195
  656.8 13.5 %recurrent_backward.1 = (f32[2,256,1280]{2,1,0:T(8,128)}, f32[2,8,1280]{2,1,0:T(8,128)S(1)}, f32[8,1280]{1,0:T(8,128)S(1)}, bf16[2,256,1280]{2,1,0:T(8,128)(2,1)S(1)}) custom-call(f32[2,256,1280]{2,1,0:T(8,128)} %copy-done.1, f32[2,256,1280]{2,1,0:T(8,128)} %get-tuple-element.331.tsum_ref, f32[2,8,1280]{2,1,0:T(8,128)S(1)} %broadcast_in_dim.161.leave_ref, ...), custom_call_target="tpu_custom_call" | custom-call | flops 1 | bytes 1 | tf_op jit(solution)/shard_map/recurrent_backward/pallas_call | solution.py:274
  702.4 27.4 %reduce-scatter.8.cloned.1.call-done = bf16[4,160,2048]{2,1,0:T(8,128)(2,1)} async-done(((bf16[4,640,2048]{2,1,0:T(8,128)(2,1)}), bf16[4,160,2048]{2,1,0:T(8,128)(2,1)}) %reduce-scatter.8.cloned.1.call-update) | async-done | bytes 2621456 | tf_op jit(solution)/shard_map/reduce_scatter | solution.py:719
  737.2 16.0 %unit_terms.1 = (f32[256,2560]{1,0:T(8,128)}, f32[256,2560]{1,0:T(8,128)}) custom-call(s32[2]{0:T(128)} %pad_add_fusion.1.order_ref, bf16[512,1280]{1,0:T(8,128)(2,1)} %bitcast.232, bf16[2560,1280]{1,0:T(8,128)(2,1)} %bitcast.224, bf16[512,1280]{1,0:T(8,128)(2,1)} %bitcast.213, bf16[2560,1280]{1,0:T(8,128)(2,1)} %bitcast.226), custom_call_target="tpu_custom_call" | custom-call | flops 1 | bytes 1 | tf_op jit(solution)/shard_map/unit_terms/pallas_call | solution.py:504
  753.2 42.9 %collective-permute-done.53 = bf16[640,640]{1,0:T(8,128)(2,1)S(1)} collective-permute-done((bf16[640,640]{1,0:T(8,128)(2,1)S(1)}, bf16[640,640]{1,0:T(8,128)(2,1)S(1)}, u32[]{:S(2)}, u32[]{:S(2)}) %collective-permute-start.53) | collective-permute-done | bytes 819232 | tf_op jit(solution)/shard_map/ppermute | solution.py:580
  809.7 20.3 %collective-permute-done.57 = bf16[768,640]{1,0:T(8,128)(2,1)S(1)} collective-permute-done((bf16[768,640]{1,0:T(8,128)(2,1)}, bf16[768,640]{1,0:T(8,128)(2,1)S(1)}, u32[]{:S(2)}, u32[]{:S(2)}) %collective-permute-start.57) | collective-permute-done | bytes 983072 | tf_op jit(solution)/shard_map/ppermute | solution.py:580
  903.2 16.2 %collective-permute-done.73 = bf16[160,2048]{1,0:T(8,128)(2,1)} collective-permute-done((bf16[160,2048]{1,0:T(8,128)(2,1)}, bf16[160,2048]{1,0:T(8,128)(2,1)}, u32[]{:S(2)}, u32[]{:S(2)}) %collective-permute-start.73) | collective-permute-done | bytes 655392 | tf_op jit(solution)/shard_map/ppermute | solution.py:580
  921.1 14.3 %collective-permute-done.61 = bf16[512,1280]{1,0:T(8,128)(2,1)S(1)} collective-permute-done((bf16[512,1280]{1,0:T(8,128)(2,1)}, bf16[512,1280]{1,0:T(8,128)(2,1)S(1)}, u32[]{:S(2)}, u32[]{:S(2)}) %collective-permute-start.61) | collective-permute-done | bytes 1310752 | tf_op jit(solution)/shard_map/ppermute | solution.py:580
  935.4 11.6 %collective-permute-done.62 = bf16[512,1280]{1,0:T(8,128)(2,1)S(1)} collective-permute-done((bf16[512,1280]{1,0:T(8,128)(2,1)S(1)}, bf16[512,1280]{1,0:T(8,128)(2,1)S(1)}, u32[]{:S(2)}, u32[]{:S(2)}) %collective-permute-start.62) | collective-permute-done | bytes 1310752 | tf_op jit(solution)/shard_map/ppermute | solution.py:580
  (534 shorter events, 453.8 us)
Async XLA Ops:
  7.2 52.1 %all-gather.10.cloned.1.call-start = ((), (), s32[]{:S(2)}) async-start(), calls=%async_computation.12 | async-start | bytes 2457600 | tf_op jit(solution)/shard_map/all_gather | solution.py:764
  12.9 113.1 %all-gather.8.cloned.1.call-start = ((), (), s32[]{:S(2)}) async-start(), calls=%async_computation.11 | async-start | bytes 4096000 | tf_op jit(solution)/shard_map/all_gather | solution.py:765
  24.6 45.7 %collective-permute-start.3 = (bf16[160,3072]{1,0:T(8,128)(2,1)}, bf16[160,3072]{1,0:T(8,128)(2,1)}, u32[]{:S(2)}, u32[]{:S(2)}) collective-permute-start(bf16[160,3072]{1,0:T(8,128)(2,1)} %pad_maximum_fusion.18), channel_id=1, source_target_pairs={{0,16},{8,24},{16,0},{24,8},{1,17},{9,25},{17,1},{25,9},{2,18},{10... | collective-permute-start | bytes 2949128 | tf_op jit(solution)/shard_map/ppermute | solution.py:580
  27.2 371.1 %all-gather.6.cloned.1.call-start = ((), (), s32[]{:S(2)}) async-start(), calls=%async_computation.5 | async-start | bytes 19660800 | tf_op jit(solution)/shard_map/all_gather | solution.py:711
  29.6 87.3 %collective-permute-start.8 = (s32[2,3]{1,0:T(2,128)S(1)}, s32[2,3]{1,0:T(2,128)S(1)}, u32[]{:S(2)}, u32[]{:S(2)}) collective-permute-start(s32[2,3]{1,0:T(2,128)S(1)} %slice.464), channel_id=1, source_target_pairs={{0,2},{2,4},{4,6},{1,3},{3,5},{5,7},{8,10},{10,12},{12,14},{9,11},... | collective-permute-start | bytes 80 | tf_op jit(solution)/shard_map/ppermute | solution.py:26
  59.3 49.5 %collective-permute-start = (bf16[4,192,1280]{2,1,0:T(8,128)(2,1)}, bf16[4,192,1280]{2,1,0:T(8,128)(2,1)S(1)}, u32[]{:S(2)}, u32[]{:S(2)}) collective-permute-start(bf16[4,192,1280]{2,1,0:T(8,128)(2,1)} %bitcast.250), channel_id=1, source_target_pairs={{0,8},{8,0},{16,24},{24,16},{1,9},{9,1},{17,25},{25,17},{2,10},{10... | collective-permute-start | bytes 5898248 | tf_op jit(solution)/shard_map/ppermute | solution.py:580
  60.8 50.5 %collective-permute-start.1 = (bf16[4,192,1280]{2,1,0:T(8,128)(2,1)}, bf16[4,192,1280]{2,1,0:T(8,128)(2,1)}, u32[]{:S(2)}, u32[]{:S(2)}) collective-permute-start(bf16[4,192,1280]{2,1,0:T(8,128)(2,1)} %bitcast.251), channel_id=1, source_target_pairs={{0,16},{8,24},{16,0},{24,8},{1,17},{9,25},{17,1},{25,9},{2,18},{10... | collective-permute-start | bytes 5898248 | tf_op jit(solution)/shard_map/ppermute | solution.py:580
  129.8 417.4 %reduce-scatter.6.cloned.1.call-start = ((), (), s32[]{:S(2)}) async-start(), calls=%async_computation.6 | async-start | bytes 6553600 | tf_op jit(solution)/shard_map/reduce_scatter | solution.py:719
  453.5 276.2 %reduce-scatter.8.cloned.1.call-start = ((), (), s32[]{:S(2)}) async-start(), calls=%async_computation.7 | async-start | bytes 13107200 | tf_op jit(solution)/shard_map/reduce_scatter | solution.py:719
  547.2 250.1 %reduce-scatter.10.cloned.1.call-start = ((), (), s32[]{:S(2)}) async-start(), calls=%async_computation.8 | async-start | bytes 2048000 | tf_op jit(solution)/shard_map/reduce_scatter | solution.py:904
  641.6 55.9 %collective-permute-start.46 = (bf16[1280,640]{1,0:T(8,128)(2,1)}, bf16[1280,640]{1,0:T(8,128)(2,1)}, u32[]{:S(2)}, u32[]{:S(2)}) collective-permute-start(bf16[1280,640]{1,0:T(8,128)(2,1)} %get-tuple-element.322), channel_id=1, source_target_pairs={{0,8},{8,0},{16,24},{24,16},{1,9},{9,1},{17,25},{25,17},{2,10},{10... | collective-permute-start | bytes 4915208 | tf_op jit(solution)/shard_map/ppermute | solution.py:580
  643.2 54.4 %collective-permute-start.47 = (bf16[1280,640]{1,0:T(8,128)(2,1)}, bf16[1280,640]{1,0:T(8,128)(2,1)}, u32[]{:S(2)}, u32[]{:S(2)}) collective-permute-start(bf16[1280,640]{1,0:T(8,128)(2,1)} %get-tuple-element.323), channel_id=1, source_target_pairs={{0,16},{8,24},{16,0},{24,8},{1,17},{9,25},{17,1},{25,9},{2,18},{10... | collective-permute-start | bytes 4915208 | tf_op jit(solution)/shard_map/ppermute | solution.py:580
  650.2 47.3 %collective-permute-start.48 = (bf16[640,640]{1,0:T(8,128)(2,1)}, bf16[640,640]{1,0:T(8,128)(2,1)}, u32[]{:S(2)}, u32[]{:S(2)}) collective-permute-start(bf16[640,640]{1,0:T(8,128)(2,1)} %add_convert_fusion.16), channel_id=1, source_target_pairs={{0,16},{8,24},{16,0},{24,8},{1,17},{9,25},{17,1},{25,9},{2,18},{10... | collective-permute-start | bytes 2457608 | tf_op jit(solution)/shard_map/ppermute | solution.py:580
  651.7 45.9 %collective-permute-start.49 = (bf16[640,640]{1,0:T(8,128)(2,1)}, bf16[640,640]{1,0:T(8,128)(2,1)}, u32[]{:S(2)}, u32[]{:S(2)}) collective-permute-start(bf16[640,640]{1,0:T(8,128)(2,1)} %add_convert_fusion.15), channel_id=1, source_target_pairs={{0,8},{8,0},{16,24},{24,16},{1,9},{9,1},{17,25},{25,17},{2,10},{10... | collective-permute-start | bytes 2457608 | tf_op jit(solution)/shard_map/ppermute | solution.py:580
  729.8 117.1 %reduce-scatter.12.cloned.1.call-start = ((), (), s32[]{:S(2)}) async-start(), calls=%async_computation.9 | async-start | bytes 2048000 | tf_op jit(solution)/shard_map/reduce_scatter | solution.py:904
  732.5 63.6 %collective-permute-start.55 = (bf16[1536,640]{1,0:T(8,128)(2,1)}, bf16[1536,640]{1,0:T(8,128)(2,1)S(1)}, u32[]{:S(2)}, u32[]{:S(2)}) collective-permute-start(bf16[1536,640]{1,0:T(8,128)(2,1)} %get-tuple-element.361), channel_id=1, source_target_pairs={{0,8},{8,0},{16,24},{24,16},{1,9},{9,1},{17,25},{25,17},{2,10},{10... | collective-permute-start | bytes 5898248 | tf_op jit(solution)/shard_map/ppermute | solution.py:580
  734.0 63.3 %collective-permute-start.56 = (bf16[1536,640]{1,0:T(8,128)(2,1)}, bf16[1536,640]{1,0:T(8,128)(2,1)}, u32[]{:S(2)}, u32[]{:S(2)}) collective-permute-start(bf16[1536,640]{1,0:T(8,128)(2,1)} %get-tuple-element.362), channel_id=1, source_target_pairs={{0,16},{8,24},{16,0},{24,8},{1,17},{9,25},{17,1},{25,9},{2,18},{10... | collective-permute-start | bytes 5898248 | tf_op jit(solution)/shard_map/ppermute | solution.py:580
  735.5 60.6 %collective-permute-start.53 = (bf16[640,640]{1,0:T(8,128)(2,1)S(1)}, bf16[640,640]{1,0:T(8,128)(2,1)S(1)}, u32[]{:S(2)}, u32[]{:S(2)}) collective-permute-start(bf16[640,640]{1,0:T(8,128)(2,1)S(1)} %add_convert_fusion.14), channel_id=1, source_target_pairs={{0,16},{8,24},{16,0},{24,8},{1,17},{9,25},{17,1},{25,9},{2,18},{10... | collective-permute-start | bytes 2457608 | tf_op jit(solution)/shard_map/ppermute | solution.py:580
  736.1 60.1 %collective-permute-start.54 = (bf16[640,640]{1,0:T(8,128)(2,1)S(1)}, bf16[640,640]{1,0:T(8,128)(2,1)S(1)}, u32[]{:S(2)}, u32[]{:S(2)}) collective-permute-start(bf16[640,640]{1,0:T(8,128)(2,1)S(1)} %add_convert_fusion.13), channel_id=1, source_target_pairs={{0,8},{8,0},{16,24},{24,16},{1,9},{9,1},{17,25},{25,17},{2,10},{10... | collective-permute-start | bytes 2457608 | tf_op jit(solution)/shard_map/ppermute | solution.py:580
  737.2 109.6 %collective-permute-start.60 = (bf16[1024,2560]{1,0:T(8,128)(2,1)}, bf16[1024,2560]{1,0:T(8,128)(2,1)}, u32[]{:S(2)}, u32[]{:S(2)}) collective-permute-start(bf16[1024,2560]{1,0:T(8,128)(2,1)} %get-tuple-element.397), channel_id=1, source_target_pairs={{0,1},{1,0},{2,3},{3,2},{4,5},{5,4},{6,7},{7,6},{8,9},{9,8},{10,11... | collective-permute-start | bytes 15728648 | tf_op jit(solution)/shard_map/ppermute | solution.py:31
  808.4 167.9 %reduce-scatter.14.cloned.1.call-start = ((), (), s32[]{:S(2)}) async-start(), calls=%async_computation.10 | async-start | bytes 2457600 | tf_op jit(solution)/shard_map/reduce_scatter | solution.py:904
  854.5 45.9 %collective-permute-start.72 = (bf16[160,2048]{1,0:T(8,128)(2,1)}, bf16[160,2048]{1,0:T(8,128)(2,1)}, u32[]{:S(2)}, u32[]{:S(2)}) collective-permute-start(bf16[160,2048]{1,0:T(8,128)(2,1)} %get-tuple-element.514), channel_id=1, source_target_pairs={{0,8},{8,0},{16,24},{24,16},{1,9},{9,1},{17,25},{25,17},{2,10},{10... | collective-permute-start | bytes 1966088 | tf_op jit(solution)/shard_map/ppermute | solution.py:580
  893.3 76.7 %collective-permute-start.66 = (f32[256,2560]{1,0:T(8,128)}, f32[256,2560]{1,0:T(8,128)S(1)}, u32[]{:S(2)}, u32[]{:S(2)}) collective-permute-start(f32[256,2560]{1,0:T(8,128)} %subtract_add_fusion), channel_id=1, source_target_pairs={{0,1},{1,0},{2,3},{3,2},{4,5},{5,4},{6,7},{7,6},{8,9},{9,8},{10,11... | collective-permute-start | bytes 7864328 | tf_op jit(solution)/shard_map/ppermute | solution.py:31
  900.6 46.4 %collective-permute-start.62 = (bf16[512,1280]{1,0:T(8,128)(2,1)S(1)}, bf16[512,1280]{1,0:T(8,128)(2,1)S(1)}, u32[]{:S(2)}, u32[]{:S(2)}) collective-permute-start(bf16[512,1280]{1,0:T(8,128)(2,1)S(1)} %copy-done.45), channel_id=1, source_target_pairs={{0,16},{8,24},{16,0},{24,8},{1,17},{9,25},{17,1},{25,9},{2,18},{10... | collective-permute-start | bytes 3932168 | tf_op jit(solution)/shard_map/ppermute | solution.py:580
  (146 other events, 2489.7 us)
Sparse Core Ops, SparseCore 0:
  13.0 46.2 all-gather.9
  61.4 64.4 all-gather.7
  130.0 268.2 all-gather.5
  453.6 93.5 reduce-scatter.5
  549.4 180.2 reduce-scatter.7
  732.5 37.2 reduce-scatter.9
  808.5 36.4 reduce-scatter.11
  856.0 44.1 reduce-scatter.13

commit v6 on v4

--- a/solution.py
+++ b/solution.py
@@ -913,7 +913,7 @@
     if square:
         gelu_more, branch_got, theirs, ours, outlet_part = together(gelu_more, branch_got, theirs, ours, outlet_part)
         gelu_part = low(near_last(gelu_parts, gelu_got, gelu_more))
-        late_sums, gelu_part = after(near_middle(branch_parts, branch_got), gelu_part)
+        late_sums, gelu_part, down_part = together(near_middle(branch_parts, branch_got), gelu_part, down_part)
         late_more = near_second(late_sums, "fsdp")
     else:
         gelu_part, outlet_part = after(gelu_part, outlet_part)
@@ -927,6 +927,7 @@
     normed_grad = ours + swap(theirs, "tp")
     norm_part, gain_one = rms_back(own(x), own(inverse_one), norm_gains[0], normed_grad)
     input_own = residual_grad + norm_part
+    down_part = to_owners(down_part)
     late, gelu_part, expand_part, down_part, input_own, gain_one, feed_sums = together(
         late, gelu_part, expand_part, down_part, input_own, gain_one, feed_sums
     )
@@ -935,7 +936,6 @@
     feed_out = near_last(feed_parts, feed_got, near_second(feed_sums, group))
     block_output = join(low(residual + feed_out)).reshape(rows, length, width)
 
-    down_part = to_owners(down_part)
     expand_part = to_owners(expand_part)
 
     def columns(part, n):

time: 950 us -> 951 us (level)
    unnamed x176 -> x164, local copies, waits for them, and re-layouts: 30.9 us -> 29.1 us
  transfers between devices with their start and end apart: 86 -> 86, of which waited for: 45 -> 42; matrix products, arithmetic and copies ran while one was open for 22% -> 23% of each run, Pallas kernels for 19% -> 19%
where the time goes in v6:
time: 951 us; the launch traced here: 940 us
  waiting for transfers between devices  372 us (39%)
  Pallas kernels  229 us (24%)
  other arithmetic  105 us (11%)
  local copies, waits for them, and re-layouts  100 us (11%)
  starting transfers between devices  90.2 us (9%)
  matrix products  27.3 us (3%)
  between operations  16.1 us (2%)
    ppermute x54, waiting for transfers between devices, cross(): lax.ppermute(x, axis, [(i, i ^ r) for i in range(lax.axis_size(axis))])  297 us
    ppermute x54, starting transfers between devices, cross(): lax.ppermute(x, axis, [(i, i ^ r) for i in range(lax.axis_size(axis))])  62.5 us
    pallas_call x1, Pallas kernels, feed_backward(): pl.pallas_call(body, grid=(tiles,), in_specs=[tokens_spec(width, tiles, m...  45.8 us
    pallas_call x2, Pallas kernels, weight_grad(): pl.pallas_call(body, grid=(width // deep,), in_specs=[pl.BlockSpec((count...  43.8 us
    pallas_call x3, Pallas kernels, weight_grad_parts(): pl.pallas_call(body, grid_spec=pltpu.PrefetchScalarGridSpec(num_scalar_pr...  31.4 us
    pallas_call x1, Pallas kernels, feed_forward(): pl.pallas_call(body, grid=(tiles,), in_specs=[pl.BlockSpec(memory_space=p...  31.2 us
    convert_element_type x11, other arithmetic, low(): return v.astype(BF16)  29.5 us
    unnamed x164, local copies, waits for them, and re-layouts  29.1 us
  transfers between devices with their start and end apart: 86, of which 42 were waited for; matrix products, arithmetic and copies ran while one was open for 23% of the time, Pallas kernels for 19%

profile of v6, /device:TPU:0, one launch (start us, length us, event | category | flops | bytes accessed | tf_op | source)
XLA Modules:
  0.0 940.2 jit_solution(11210709620480319795)
XLA Ops:
  40.4 18.9 %all-gather.10.cloned.1.call-done = bf16[768,1280]{1,0:T(8,128)(2,1)} async-done(((bf16[192,1280]{1,0:T(8,128)(2,1)}), bf16[768,1280]{1,0:T(8,128)(2,1)}) %all-gather.10.cloned.1.call-update) | async-done | bytes 1966096 | tf_op jit(solution)/shard_map/all_gather | solution.py:764
  74.7 34.1 %collective-permute-done = bf16[4,192,1280]{2,1,0:T(8,128)(2,1)S(1)} collective-permute-done((bf16[4,192,1280]{2,1,0:T(8,128)(2,1)}, bf16[4,192,1280]{2,1,0:T(8,128)(2,1)S(1)}, u32[]{:S(2)}, u32[]{:S(2)}) %collective-permute-start) | collective-permute-done | bytes 1966112 | tf_op jit(solution)/shard_map/ppermute | solution.py:580
  161.9 15.9 %recurrent_forward.1 = (bf16[2,256,1280]{2,1,0:T(8,128)(2,1)S(1)}, f32[2,256,1280]{2,1,0:T(8,128)}, f32[2,256,1280]{2,1,0:T(8,128)}, f32[2,256,1280]{2,1,0:T(8,1...) custom-call(bf16[2,256,1280]{2,1,0:T(8,128)(2,1)S(1)} %bitcast.210, f32[2,8,1280]{2,1,0:T(8,128)S(1)} %pad_convert_fusion.halo_ref, ...), custom_call_target="tpu_custom_call" | custom-call | flops 1 | bytes 1 | tf_op jit(solution)/shard_map/recurrent_forward/pallas_call | solution.py:153
  225.7 16.6 %collective-permute-done.15 = bf16[4,160,1280]{2,1,0:T(8,128)(2,1)S(1)} collective-permute-done((bf16[4,160,1280]{2,1,0:T(8,128)(2,1)}, bf16[4,160,1280]{2,1,0:T(8,128)(2,1)S(1)}, u32[]{:S(2)}, u32[]{:S(2)}) %collective-permute-start.15) | collective-permute-done | bytes 1638432 | tf_op jit(solution)/shard_map/ppermute | solution.py:580
  247.2 13.5 %collective-permute-done.17 = bf16[2,160,1280]{2,1,0:T(8,128)(2,1)S(1)} collective-permute-done((bf16[2,160,1280]{2,1,0:T(8,128)(2,1)S(1)}, bf16[2,160,1280]{2,1,0:T(8,128)(2,1)S(1)}, u32[]{:S(2)}, u32[]{:S(2)}) %collective-permute-start.17) | collective-permute-done | bytes 819232 | tf_op jit(solution)/shard_map/ppermute | solution.py:580
  278.6 29.0 %collective-permute-done.20.refs_0_ = bf16[256,2560]{1,0:T(8,128)(2,1)S(1)} collective-permute-done((bf16[256,2560]{1,0:T(8,128)(2,1)S(1)}, bf16[256,2560]{1,0:T(8,128)(2,1)S(1)}, u32[]{:S(2)}, u32[]{:S(2)}) %collective-permute-start.20) | collective-permute-done | bytes 1310752 | tf_op jit(solution)/shard_map/ppermute | solution.py:580
  310.7 13.2 %collective-permute-done.22.refs_1_ = bf16[128,2560]{1,0:T(8,128)(2,1)S(1)} collective-permute-done((bf16[128,2560]{1,0:T(8,128)(2,1)S(1)}, bf16[128,2560]{1,0:T(8,128)(2,1)S(1)}, u32[]{:S(2)}, u32[]{:S(2)}) %collective-permute-start.22) | collective-permute-done | bytes 655392 | tf_op jit(solution)/shard_map/ppermute | solution.py:580
  329.3 28.6 %collective-permute-done.29 = bf16[256,2560]{1,0:T(8,128)(2,1)S(1)} collective-permute-done((bf16[256,2560]{1,0:T(8,128)(2,1)S(1)}, bf16[256,2560]{1,0:T(8,128)(2,1)S(1)}, u32[]{:S(2)}, u32[]{:S(2)}) %collective-permute-start.29) | collective-permute-done | bytes 1310752 | tf_op jit(solution)/shard_map/ppermute | solution.py:580
  362.6 12.3 %collective-permute-done.31 = bf16[128,2560]{1,0:T(8,128)(2,1)S(1)} collective-permute-done((bf16[128,2560]{1,0:T(8,128)(2,1)S(1)}, bf16[128,2560]{1,0:T(8,128)(2,1)S(1)}, u32[]{:S(2)}, u32[]{:S(2)}) %collective-permute-start.31) | collective-permute-done | bytes 655392 | tf_op jit(solution)/shard_map/ppermute | solution.py:580
  384.9 13.4 %all-gather.6.cloned.1.call-done = bf16[4,640,3072]{2,1,0:T(8,128)(2,1)} async-done(((bf16[4,160,3072]{2,1,0:T(8,128)(2,1)}), bf16[4,640,3072]{2,1,0:T(8,128)(2,1)}) %all-gather.6.cloned.1.call-update) | async-done | bytes 15728656 | tf_op jit(solution)/shard_map/all_gather | solution.py:711
  398.3 31.2 %feed_forward.1 = (bf16[2048,2560]{1,0:T(8,128)(2,1)}, bf16[2048,1024]{1,0:T(8,128)(2,1)}, f32[2048,1024]{1,0:T(8,128)}, f32[2048,1024]{1,0:T(8,128)}) custom-call(bf16[256,2560]{1,0:T(8,128)(2,1)} %copy-done.24, bf16[128,2560]{1,0:T(8,128)(2,1)} %copy-done.53, bf16[128,2560]{1,0:T(8,128)(2,1)} %copy-done.54, bf16[256,2560]{1,0:T(8,128)(2,1)} %copy-done.25, ...), custom_call_target="tpu_custom_call" | custom-call | flops 1 | bytes 1 | tf_op jit(solution)/shard_map/feed_forward/pallas_call | solution.py:392
  429.5 15.7 %weight_grad.2 = bf16[2560,1024]{1,0:T(8,128)(2,1)} custom-call(bf16[2048,2560]{1,0:T(8,128)(2,1)} %constant_dynamic-update-slice_fusion.x_ref.fg_ref, bf16[2048,1024]{1,0:T(8,128)(2,1)} %get-tuple-element.288.g_ref.h_ref), custom_call_target="tpu_custom_call" | custom-call | flops 1 | bytes 1 | tf_op jit(solution)/shard_map/weight_grad/pallas_call | solution.py:470
  445.2 45.8 %feed_backward.1 = (bf16[2048,2048]{1,0:T(8,128)(2,1)}, bf16[1024,2560]{1,0:T(8,128)(2,1)}, bf16[1024,2560]{1,0:T(8,128)(2,1)}) custom-call(bf16[2048,2560]{1,0:T(8,128)(2,1)} %constant_dynamic-update-slice_fusion.x_ref.fg_ref, f32[2048,1024]{1,0:T(8,128)} %get-tuple-element.269.gate_ref, f32[2048,1024]{1,0:T(8,128)} %get-tuple-element.270.up_ref, ...), custom_call_target="tpu_custom_call" | custom-call | flops 1 | bytes 1 | tf_op jit(solution)/shard_map/feed_backward/pallas_call | solution.py:426
  507.1 28.1 %weight_grad.3 = bf16[2560,2048]{1,0:T(8,128)(2,1)} custom-call(bf16[2048,2560]{1,0:T(8,128)(2,1)} %get-tuple-element.278.x_ref, bf16[2048,2048]{1,0:T(8,128)(2,1)} %get-tuple-element.279.g_ref), custom_call_target="tpu_custom_call" | custom-call | flops 1 | bytes 1 | tf_op jit(solution)/shard_map/weight_grad/pallas_call | solution.py:470
  544.9 18.0 %feed_down.1 = (bf16[1024,2560]{1,0:T(8,128)(2,1)}, bf16[1024,2560]{1,0:T(8,128)(2,1)}) custom-call(bf16[2048,1024]{1,0:T(8,128)(2,1)} %get-tuple-element.288.g_ref.h_ref, bf16[2560,3072]{1,0:T(8,128)(2,1)} %bitcast.218), custom_call_target="tpu_custom_call" | custom-call | flops 1 | bytes 1 | tf_op jit(solution)/shard_map/feed_down/pallas_call | solution.py:450
  606.6 13.7 %recurrent_adjoint.1 = (bf16[2,256,1280]{2,1,0:T(8,128)(2,1)S(1)}, f32[2,256,1280]{2,1,0:T(8,128)S(1)}, f32[2,256,1280]{2,1,0:T(8,128)}) custom-call(f32[2,256,1280]{2,1,0:T(8,128)} %fusion.37.rg_ref, f32[2,256,1280]{2,1,0:T(8,128)} %get-tuple-element.573.gelu_ref, f32[2,256,1280]{2,1,0:T(8,128)} %get-tuple-element.311.a_ref, ...), custom_call_target="tpu_custom_call" | custom-call | flops 1 | bytes 1 | tf_op jit(solution)/shard_map/recurrent_adjoint/pallas_call | solution.py:195
  621.3 10.3 %weight_grad_parts.4 = (bf16[1280,640]{1,0:T(8,128)(2,1)}, bf16[1280,640]{1,0:T(8,128)(2,1)}, bf16[640,640]{1,0:T(8,128)(2,1)}, bf16[640,640]{1,0:T(8,128)(2,1)}...) custom-call(s32[4]{0:T(128)} %broadcast_xor_fusion.places_ref, bf16[512,2560]{1,0:T(8,128)(2,1)} %multiply_convert_fusion.x_ref, ...), custom_call_target="tpu_custom_call" | custom-call | flops 1 | bytes 1 | tf_op jit(solution)/shard_map/weight_grad_parts/pallas_call | solution.py:548
  631.6 27.3 %collective-permute-done.45 = bf16[512,1280]{1,0:T(8,128)(2,1)} collective-permute-done((bf16[512,1280]{1,0:T(8,128)(2,1)}, bf16[512,1280]{1,0:T(8,128)(2,1)}, u32[]{:S(2)}, u32[]{:S(2)}) %collective-permute-start.45) | collective-permute-done | bytes 1310752 | tf_op jit(solution)/shard_map/ppermute | solution.py:580
  678.5 13.4 %recurrent_backward.1 = (f32[2,256,1280]{2,1,0:T(8,128)}, f32[2,8,1280]{2,1,0:T(8,128)S(1)}, f32[8,1280]{1,0:T(8,128)S(1)}, bf16[2,256,1280]{2,1,0:T(8,128)(2,1)S(1)}) custom-call(f32[2,256,1280]{2,1,0:T(8,128)} %copy-done.1, f32[2,256,1280]{2,1,0:T(8,128)} %get-tuple-element.345.tsum_ref, f32[2,8,1280]{2,1,0:T(8,128)S(1)} %broadcast_in_dim.161.leave_ref, ...), custom_call_target="tpu_custom_call" | custom-call | flops 1 | bytes 1 | tf_op jit(solution)/shard_map/recurrent_backward/pallas_call | solution.py:274
  708.5 10.8 %weight_grad_parts.5 = (bf16[1536,640]{1,0:T(8,128)(2,1)}, bf16[1536,640]{1,0:T(8,128)(2,1)}, bf16[768,640]{1,0:T(8,128)(2,1)}, bf16[768,640]{1,0:T(8,128)(2,1)}...) custom-call(s32[4]{0:T(128)} %broadcast_xor_fusion.places_ref, bf16[512,2560]{1,0:T(8,128)(2,1)} %multiply_convert_fusion.x_ref, ...), custom_call_target="tpu_custom_call" | custom-call | flops 1 | bytes 1 | tf_op jit(solution)/shard_map/weight_grad_parts/pallas_call | solution.py:548
  736.5 15.7 %unit_terms.1 = (f32[256,2560]{1,0:T(8,128)}, f32[256,2560]{1,0:T(8,128)}) custom-call(s32[2]{0:T(128)} %pad_add_fusion.1.order_ref, bf16[512,1280]{1,0:T(8,128)(2,1)} %bitcast.232, bf16[2560,1280]{1,0:T(8,128)(2,1)} %bitcast.224, bf16[512,1280]{1,0:T(8,128)(2,1)} %bitcast.213, bf16[2560,1280]{1,0:T(8,128)(2,1)} %bitcast.226), custom_call_target="tpu_custom_call" | custom-call | flops 1 | bytes 1 | tf_op jit(solution)/shard_map/unit_terms/pallas_call | solution.py:504
  752.2 40.8 %collective-permute-done.56 = bf16[640,640]{1,0:T(8,128)(2,1)} collective-permute-done((bf16[640,640]{1,0:T(8,128)(2,1)}, bf16[640,640]{1,0:T(8,128)(2,1)}, u32[]{:S(2)}, u32[]{:S(2)}) %collective-permute-start.56) | collective-permute-done | bytes 819232 | tf_op jit(solution)/shard_map/ppermute | solution.py:580
  818.2 23.6 %collective-permute-done.64 = bf16[160,1024]{1,0:T(8,128)(2,1)S(1)} collective-permute-done((bf16[160,1024]{1,0:T(8,128)(2,1)S(1)}, bf16[160,1024]{1,0:T(8,128)(2,1)S(1)}, u32[]{:S(2)}, u32[]{:S(2)}) %collective-permute-start.64) | collective-permute-done | bytes 327712 | tf_op jit(solution)/shard_map/ppermute | solution.py:580
  898.9 11.3 %collective-permute-done.66 = bf16[256,1280]{1,0:T(8,128)(2,1)} collective-permute-done((bf16[256,1280]{1,0:T(8,128)(2,1)}, bf16[256,1280]{1,0:T(8,128)(2,1)}, u32[]{:S(2)}, u32[]{:S(2)}) %collective-permute-start.66) | collective-permute-done | bytes 655392 | tf_op jit(solution)/shard_map/ppermute | solution.py:580
  (509 shorter events, 423.0 us)
Async XLA Ops:
  7.2 52.1 %all-gather.10.cloned.1.call-start = ((), (), s32[]{:S(2)}) async-start(), calls=%async_computation.12 | async-start | bytes 2457600 | tf_op jit(solution)/shard_map/all_gather | solution.py:764
  12.9 113.1 %all-gather.8.cloned.1.call-start = ((), (), s32[]{:S(2)}) async-start(), calls=%async_computation.11 | async-start | bytes 4096000 | tf_op jit(solution)/shard_map/all_gather | solution.py:765
  27.2 371.1 %all-gather.6.cloned.1.call-start = ((), (), s32[]{:S(2)}) async-start(), calls=%async_computation.5 | async-start | bytes 19660800 | tf_op jit(solution)/shard_map/all_gather | solution.py:711
  29.6 87.3 %collective-permute-start.8 = (s32[2,3]{1,0:T(2,128)S(1)}, s32[2,3]{1,0:T(2,128)S(1)}, u32[]{:S(2)}, u32[]{:S(2)}) collective-permute-start(s32[2,3]{1,0:T(2,128)S(1)} %slice.464), channel_id=1, source_target_pairs={{0,2},{2,4},{4,6},{1,3},{3,5},{5,7},{8,10},{10,12},{12,14},{9,11},... | collective-permute-start | bytes 80 | tf_op jit(solution)/shard_map/ppermute | solution.py:26
  59.3 49.5 %collective-permute-start = (bf16[4,192,1280]{2,1,0:T(8,128)(2,1)}, bf16[4,192,1280]{2,1,0:T(8,128)(2,1)S(1)}, u32[]{:S(2)}, u32[]{:S(2)}) collective-permute-start(bf16[4,192,1280]{2,1,0:T(8,128)(2,1)} %bitcast.248), channel_id=1, source_target_pairs={{0,8},{8,0},{16,24},{24,16},{1,9},{9,1},{17,25},{25,17},{2,10},{10... | collective-permute-start | bytes 5898248 | tf_op jit(solution)/shard_map/ppermute | solution.py:580
  60.8 50.5 %collective-permute-start.1 = (bf16[4,192,1280]{2,1,0:T(8,128)(2,1)}, bf16[4,192,1280]{2,1,0:T(8,128)(2,1)}, u32[]{:S(2)}, u32[]{:S(2)}) collective-permute-start(bf16[4,192,1280]{2,1,0:T(8,128)(2,1)} %bitcast.249), channel_id=1, source_target_pairs={{0,16},{8,24},{16,0},{24,8},{1,17},{9,25},{17,1},{25,9},{2,18},{10... | collective-permute-start | bytes 5898248 | tf_op jit(solution)/shard_map/ppermute | solution.py:580
  129.9 409.0 %reduce-scatter.6.cloned.1.call-start = ((), (), s32[]{:S(2)}) async-start(), calls=%async_computation.6 | async-start | bytes 6553600 | tf_op jit(solution)/shard_map/reduce_scatter | solution.py:719
  445.2 282.0 %reduce-scatter.8.cloned.1.call-start = ((), (), s32[]{:S(2)}) async-start(), calls=%async_computation.7 | async-start | bytes 13107200 | tf_op jit(solution)/shard_map/reduce_scatter | solution.py:719
  538.9 254.2 %reduce-scatter.10.cloned.1.call-start = ((), (), s32[]{:S(2)}) async-start(), calls=%async_computation.8 | async-start | bytes 2048000 | tf_op jit(solution)/shard_map/reduce_scatter | solution.py:909
  592.4 66.5 %collective-permute-start.47 = (bf16[1280,640]{1,0:T(8,128)(2,1)}, bf16[1280,640]{1,0:T(8,128)(2,1)}, u32[]{:S(2)}, u32[]{:S(2)}) collective-permute-start(bf16[1280,640]{1,0:T(8,128)(2,1)} %get-tuple-element.306), channel_id=1, source_target_pairs={{0,8},{8,0},{16,24},{24,16},{1,9},{9,1},{17,25},{25,17},{2,10},{10... | collective-permute-start | bytes 4915208 | tf_op jit(solution)/shard_map/ppermute | solution.py:580
  592.9 66.1 %collective-permute-start.48 = (bf16[1280,640]{1,0:T(8,128)(2,1)}, bf16[1280,640]{1,0:T(8,128)(2,1)}, u32[]{:S(2)}, u32[]{:S(2)}) collective-permute-start(bf16[1280,640]{1,0:T(8,128)(2,1)} %get-tuple-element.307), channel_id=1, source_target_pairs={{0,16},{8,24},{16,0},{24,8},{1,17},{9,25},{17,1},{25,9},{2,18},{10... | collective-permute-start | bytes 4915208 | tf_op jit(solution)/shard_map/ppermute | solution.py:580
  593.4 65.5 %collective-permute-start.45 = (bf16[512,1280]{1,0:T(8,128)(2,1)}, bf16[512,1280]{1,0:T(8,128)(2,1)}, u32[]{:S(2)}, u32[]{:S(2)}) collective-permute-start(bf16[512,1280]{1,0:T(8,128)(2,1)} %get-tuple-element.295), channel_id=1, source_target_pairs={{0,8},{8,0},{16,24},{24,16},{1,9},{9,1},{17,25},{25,17},{2,10},{10... | collective-permute-start | bytes 3932168 | tf_op jit(solution)/shard_map/ppermute | solution.py:580
  594.9 64.1 %collective-permute-start.46 = (bf16[512,1280]{1,0:T(8,128)(2,1)}, bf16[512,1280]{1,0:T(8,128)(2,1)}, u32[]{:S(2)}, u32[]{:S(2)}) collective-permute-start(bf16[512,1280]{1,0:T(8,128)(2,1)} %get-tuple-element.296), channel_id=1, source_target_pairs={{0,16},{8,24},{16,0},{24,8},{1,17},{9,25},{17,1},{25,9},{2,18},{10... | collective-permute-start | bytes 3932168 | tf_op jit(solution)/shard_map/ppermute | solution.py:580
  666.2 56.3 %collective-permute-start.49 = (bf16[1280,640]{1,0:T(8,128)(2,1)}, bf16[1280,640]{1,0:T(8,128)(2,1)}, u32[]{:S(2)}, u32[]{:S(2)}) collective-permute-start(bf16[1280,640]{1,0:T(8,128)(2,1)} %get-tuple-element.336), channel_id=1, source_target_pairs={{0,8},{8,0},{16,24},{24,16},{1,9},{9,1},{17,25},{25,17},{2,10},{10... | collective-permute-start | bytes 4915208 | tf_op jit(solution)/shard_map/ppermute | solution.py:580
  667.9 54.5 %collective-permute-start.50 = (bf16[1280,640]{1,0:T(8,128)(2,1)}, bf16[1280,640]{1,0:T(8,128)(2,1)}, u32[]{:S(2)}, u32[]{:S(2)}) collective-permute-start(bf16[1280,640]{1,0:T(8,128)(2,1)} %get-tuple-element.337), channel_id=1, source_target_pairs={{0,16},{8,24},{16,0},{24,8},{1,17},{9,25},{17,1},{25,9},{2,18},{10... | collective-permute-start | bytes 4915208 | tf_op jit(solution)/shard_map/ppermute | solution.py:580
  672.5 49.9 %collective-permute-start.51 = (bf16[640,640]{1,0:T(8,128)(2,1)}, bf16[640,640]{1,0:T(8,128)(2,1)}, u32[]{:S(2)}, u32[]{:S(2)}) collective-permute-start(bf16[640,640]{1,0:T(8,128)(2,1)} %add_convert_fusion.16), channel_id=1, source_target_pairs={{0,16},{8,24},{16,0},{24,8},{1,17},{9,25},{17,1},{25,9},{2,18},{10... | collective-permute-start | bytes 2457608 | tf_op jit(solution)/shard_map/ppermute | solution.py:580
  673.2 49.2 %collective-permute-start.52 = (bf16[640,640]{1,0:T(8,128)(2,1)}, bf16[640,640]{1,0:T(8,128)(2,1)}, u32[]{:S(2)}, u32[]{:S(2)}) collective-permute-start(bf16[640,640]{1,0:T(8,128)(2,1)} %add_convert_fusion.15), channel_id=1, source_target_pairs={{0,8},{8,0},{16,24},{24,16},{1,9},{9,1},{17,25},{25,17},{2,10},{10... | collective-permute-start | bytes 2457608 | tf_op jit(solution)/shard_map/ppermute | solution.py:580
  727.2 131.4 %reduce-scatter.12.cloned.1.call-start = ((), (), s32[]{:S(2)}) async-start(), calls=%async_computation.9 | async-start | bytes 2048000 | tf_op jit(solution)/shard_map/reduce_scatter | solution.py:909
  731.8 61.2 %collective-permute-start.58 = (bf16[1536,640]{1,0:T(8,128)(2,1)}, bf16[1536,640]{1,0:T(8,128)(2,1)S(1)}, u32[]{:S(2)}, u32[]{:S(2)}) collective-permute-start(bf16[1536,640]{1,0:T(8,128)(2,1)} %get-tuple-element.375), channel_id=1, source_target_pairs={{0,8},{8,0},{16,24},{24,16},{1,9},{9,1},{17,25},{25,17},{2,10},{10... | collective-permute-start | bytes 5898248 | tf_op jit(solution)/shard_map/ppermute | solution.py:580
  732.4 60.6 %collective-permute-start.59 = (bf16[1536,640]{1,0:T(8,128)(2,1)}, bf16[1536,640]{1,0:T(8,128)(2,1)}, u32[]{:S(2)}, u32[]{:S(2)}) collective-permute-start(bf16[1536,640]{1,0:T(8,128)(2,1)} %get-tuple-element.376), channel_id=1, source_target_pairs={{0,16},{8,24},{16,0},{24,8},{1,17},{9,25},{17,1},{25,9},{2,18},{10... | collective-permute-start | bytes 5898248 | tf_op jit(solution)/shard_map/ppermute | solution.py:580
  732.9 60.2 %collective-permute-start.56 = (bf16[640,640]{1,0:T(8,128)(2,1)}, bf16[640,640]{1,0:T(8,128)(2,1)}, u32[]{:S(2)}, u32[]{:S(2)}) collective-permute-start(bf16[640,640]{1,0:T(8,128)(2,1)} %add_convert_fusion.14), channel_id=1, source_target_pairs={{0,16},{8,24},{16,0},{24,8},{1,17},{9,25},{17,1},{25,9},{2,18},{10... | collective-permute-start | bytes 2457608 | tf_op jit(solution)/shard_map/ppermute | solution.py:580
  734.5 58.6 %collective-permute-start.57 = (bf16[640,640]{1,0:T(8,128)(2,1)}, bf16[640,640]{1,0:T(8,128)(2,1)}, u32[]{:S(2)}, u32[]{:S(2)}) collective-permute-start(bf16[640,640]{1,0:T(8,128)(2,1)} %add_convert_fusion.13), channel_id=1, source_target_pairs={{0,8},{8,0},{16,24},{24,16},{1,9},{9,1},{17,25},{25,17},{2,10},{10... | collective-permute-start | bytes 2457608 | tf_op jit(solution)/shard_map/ppermute | solution.py:580
  793.1 55.2 %collective-permute-start.65 = (f32[256,2560]{1,0:T(8,128)}, f32[256,2560]{1,0:T(8,128)}, u32[]{:S(2)}, u32[]{:S(2)}) collective-permute-start(f32[256,2560]{1,0:T(8,128)} %get-tuple-element.410), channel_id=1, source_target_pairs={{0,1},{1,0},{2,3},{3,2},{4,5},{5,4},{6,7},{7,6},{8,9},{9,8},{10,11... | collective-permute-start | bytes 7864328 | tf_op jit(solution)/shard_map/ppermute | solution.py:31
  812.0 115.7 %reduce-scatter.14.cloned.1.call-start = ((), (), s32[]{:S(2)}) async-start(), calls=%async_computation.10 | async-start | bytes 2457600 | tf_op jit(solution)/shard_map/reduce_scatter | solution.py:909
  (134 other events, 2292.7 us)
Sparse Core Ops, SparseCore 0:
  13.0 46.2 all-gather.9
  61.5 64.4 all-gather.7
  130.0 268.2 all-gather.5
  445.3 93.5 reduce-scatter.5
  541.1 180.2 reduce-scatter.7
  727.3 36.9 reduce-scatter.9
  812.1 37.0 reduce-scatter.11
  869.8 43.1 reduce-scatter.13
